TPU v7x, 512 devices: a whole 4x4x16 slice. The times are simulated.
512 devices in a mesh: wide: 32 (over z, core), narrow: 16 (over x, y).
Axes of the slice: x: 4, y: 4, z: 16, core: 2. Of those that a mesh axis runs over, the one named last changes fastest.
Arguments:
- activations: bfloat16 [512, 16384], P(None, 'wide'), may hold values from -6 to 6
- enc_weight: bfloat16 [16384, 16384], P('wide', 'narrow'), may hold values from -0.046875 to 0.046875
- enc_bias: float32 [16384], P('narrow'), may hold values from -4 to 4
- dec_weight: bfloat16 [16384, 16384], P('narrow', 'wide'), may hold values from -0.375 to 0.375
- dec_bias: float32 [16384], P('wide'), may hold values from -4 to 4
- active_ids: int32 [512, 64], replicated, may hold values from 0 to 16383, all different within a row
Outputs:
- dec_grad: bfloat16 [16384, 16384], P('narrow', 'wide')
- latent_grad: float32 [512, 16384], P('wide', 'narrow')
Inputs may be any that keep to these rules, and one draw needn't show every extreme that they name: `active_ids`: each row names 64 different latents; every latent is named by some row.
All inputs are finite; a program needn't handle non-finite values.
Results may differ from a plain program's by a relative error of at most 0.0058.
Values may be sent and summed in bfloat16 or wider, within the bound.
No kernel may reach another device: no remote copies, remote signals or barrier semaphores. Data moves between devices by JAX's collectives and lax.ppermute only.
A program may use at most 128 MiB of HBM per device.

v0:
```python
import jax
import jax.numpy as jnp
from jax import lax
from jax.sharding import Mesh
from jax.sharding import PartitionSpec as P

NARROW = ("narrow_0", "narrow_1")
WIDE = ("wide_0", "wide_1")


def filled_with(value, identity):
    return jnp.broadcast_to(jnp.asarray(identity, value.dtype), value.shape)


def carried_in(value, axes, combine, identity, reverse):
    before = start = filled_with(value, identity)
    total = value
    for axis in reversed(axes):
        length, position = (lax.axis_size(axis), lax.axis_index(axis))
        pieces = lax.all_gather(total, axis)
        inside, total = (start, start)
        for k in reversed(range(length)) if reverse else range(length):
            passed = k > position if reverse else k < position
            total = combine(total, pieces[k])
            inside = jnp.where(passed, total, inside)
        before = combine(inside, before)
    return before


def reduced_to_own(pieces, axes, turns):
    inside = pieces.shape[1:]
    pieces = pieces.reshape(*(lax.axis_size(a) for a in axes), *inside)
    pieces = jnp.moveaxis(pieces, turns, range(len(axes))).reshape(-1, *inside)
    for k in turns:
        pieces = lax.psum_scatter(pieces, axes[k], scatter_dimension=0, tiled=True)
    return pieces[0]


def in_blocks(value, dim, length):
    dims = value.shape
    pieces = value.reshape(*dims[:dim], length, dims[dim] // length, *dims[dim + 1 :])
    return jnp.moveaxis(pieces, dim, 0)


def summed_rows(value, axes, turns, dim):
    length = lax.axis_size(axes)
    return reduced_to_own(in_blocks(value, dim, length), axes, turns)


def add_fields(earlier, later):
    return jax.tree.map(jnp.add, earlier, later)


def local(activations, enc_weight, enc_bias, dec_weight, dec_bias, active_ids):
    token_count = activations.shape[0]
    latent_width = enc_weight.shape[1]
    groups = lax.axis_size(NARROW)
    group_index = lax.axis_index(NARROW)
    first_latent = group_index * latent_width
    inside = (active_ids >= first_latent) & (active_ids < first_latent + latent_width)
    local_ids = jnp.where(inside, active_ids - first_latent, latent_width)
    row_index = jnp.arange(token_count, dtype=jnp.int32)[:, None]
    active_mask = (
        jnp.zeros((token_count, latent_width), jnp.float32)
        .at[row_index, local_ids]
        .set(1.0, mode="drop")
    )
    share_rows = token_count // lax.axis_size(WIDE)
    offset = lax.axis_index(WIDE) * share_rows
    own_mask = lax.dynamic_slice_in_dim(active_mask, offset, share_rows, 0)
    partial_pre = jnp.dot(activations, enc_weight, preferred_element_type=jnp.float32)
    preact = lax.psum(partial_pre, WIDE) + enc_bias
    latents = (active_mask * preact).astype(jnp.bfloat16)
    recon_part = jnp.dot(latents, dec_weight, preferred_element_type=jnp.float32)
    target = activations.astype(jnp.float32)
    nothing = jnp.zeros_like(recon_part)
    before = carried_in(recon_part, NARROW, add_fields, nothing, False)
    errors_here = dec_bias + before + recon_part - target
    later_sum = carried_in(errors_here, NARROW, add_fields, nothing, True)
    suffix = later_sum + errors_here
    errors = (suffix / groups).astype(jnp.bfloat16)
    dec_grad = lax.dot_general(
        latents, errors, (((0,), (0,)), ((), ())), preferred_element_type=jnp.float32
    ).astype(jnp.bfloat16)
    latent_rows = summed_rows(
        lax.dot_general(
            errors, dec_weight, (((1,), (1,)), ((), ())), preferred_element_type=jnp.float32
        ),
        WIDE,
        (1, 0),
        0,
    )
    latent_out = own_mask * latent_rows
    return (dec_grad, latent_out)


def solution(mesh):
    split = Mesh(mesh.devices.reshape(16, 2, 4, 4), ("wide_0", "wide_1", "narrow_0", "narrow_1"))
    return jax.shard_map(
        local,
        mesh=split,
        in_specs=(P(None, WIDE), P(WIDE, NARROW), P(NARROW), P(NARROW, WIDE), P(WIDE), P()),
        out_specs=(P(NARROW, WIDE), P(WIDE, NARROW)),
        check_vma=False,
    )
```

profile of v0, /device:TPU:1, one launch (start us, length us, event | category | flops | bytes accessed | tf_op | source)
XLA Modules:
  0.0 573.7 jit_solution(8263159260602203690)
XLA Ops:
  7.2 3.5 fusion.17
  10.8 0.0 all-gather.11.cloned.1.call-start
  10.9 0.5 copy-done.11
  11.4 0.1 multiply_reduce_fusion
  11.5 0.1 and_reduce_fusion
  11.7 0.1 copy.10
  11.8 0.1 reshape.66
  11.9 121.5 %scatter_custom_fusion = f32[524288]{0:T(1024)} fusion(s32[32768]{0:T(1024)S(1)} %reshape.66, f32[32768]{0:T(1024)S(1)} %broadcast.52, f32[]{:T(128)} %constant.17.clone.1), kind=kCustom, calls=%fused_computation.31 | custom fusion | bytes 2097156
  133.4 1.7 reshape.63
  135.1 95.2 %all-reduce.2.cloned.1.call-done = f32[512,1024]{1,0:T(8,128)} async-done(((f32[512,1024]{1,0:T(8,128)}), f32[512,1024]{1,0:T(8,128)}) %all-reduce.2.cloned.1.call-update) | async-done | bytes 2097168 | tf_op jit(solution)/shard_map/psum | solution.py:72
  230.4 2.1 multiply_convert_fusion
  232.5 1.0 copy-done.5
  233.4 1.7 fusion.18
  235.2 0.0 all-gather.7.cloned.1.call-start
  235.2 55.8 %all-gather.11.cloned.1.call-done = f32[2048,512]{1,0:T(8,128)} async-done(((f32[512,512]{1,0:T(8,128)}), f32[2048,512]{1,0:T(8,128)}) %all-gather.11.cloned.1.call-update) | async-done | bytes 4194320 | tf_op jit(solution)/shard_map/all_gather | solution.py:20
  291.0 3.7 fusion.13
  294.7 0.0 all-gather.13.cloned.1.call-start
  294.7 56.4 %all-gather.7.cloned.1.call-done = f32[4,512,512]{2,1,0:T(8,128)} async-done(((f32[1,512,512]{2,1,0:T(8,128)}), f32[4,512,512]{2,1,0:T(8,128)}) %all-gather.7.cloned.1.call-update) | async-done | bytes 4194320 | tf_op jit(solution)/shard_map/all_gather | solution.py:20
  351.1 5.6 fusion.12
  356.8 0.0 all-gather.9.cloned.1.call-start
  356.8 56.5 %all-gather.13.cloned.1.call-done = f32[2048,512]{1,0:T(8,128)} async-done(((f32[512,512]{1,0:T(8,128)}), f32[2048,512]{1,0:T(8,128)}) %all-gather.13.cloned.1.call-update) | async-done | bytes 4194320 | tf_op jit(solution)/shard_map/all_gather | solution.py:20
  413.3 3.7 fusion.6
  417.0 0.0 reduce-scatter.3.cloned.1.call-start
  417.1 56.4 %all-gather.9.cloned.1.call-done = f32[4,512,512]{2,1,0:T(8,128)} async-done(((f32[1,512,512]{2,1,0:T(8,128)}), f32[4,512,512]{2,1,0:T(8,128)}) %all-gather.9.cloned.1.call-update) | async-done | bytes 4194320 | tf_op jit(solution)/shard_map/all_gather | solution.py:20
  473.5 4.6 fusion.5
  478.1 0.7 fusion.19
  478.8 1.5 copy.11
  480.3 0.0 reduce-scatter.5.cloned.1.call-start
  480.4 21.9 %reduce-scatter.3.cloned.1.call-done = f32[16,16,1024]{2,1,0:T(8,128)} async-done(((f32[32,16,1024]{2,1,0:T(8,128)}), f32[16,16,1024]{2,1,0:T(8,128)}) %reduce-scatter.3.cloned.1.call-update) | async-done | bytes 1048592 | tf_op jit(solution)/shard_map/reduce_scatter | solution.py:35
  502.3 1.7 convolution_convert_fusion
  504.1 61.3 %reduce-scatter.5.cloned.1.call-done = f32[1,16,1024]{2,1,0:T(8,128)} async-done(((f32[16,16,1024]{2,1,0:T(8,128)}), f32[1,16,1024]{2,1,0:T(8,128)}) %reduce-scatter.5.cloned.1.call-update) | async-done | bytes 65552 | tf_op jit(solution)/shard_map/reduce_scatter | solution.py:35
  565.3 1.5 bitcast_multiply_fusion
  (34 shorter events, 0.3 us)
Async XLA Ops:
  7.2 226.3 %copy-start = (bf16[1024,512]{1,0:T(8,128)(2,1)S(1)}, bf16[1024,512]{1,0:T(8,128)(2,1)}, u32[]{:S(2)}) copy-start(bf16[1024,512]{1,0:T(8,128)(2,1)} %param.9) | copy-start | bytes 3145732
  7.2 3.7 copy-start.7
  7.2 223.2 %all-reduce.2.cloned.1.call-start = ((), (), s32[]{:S(2)}) async-start(), calls=%async_computation.2 | async-start | bytes 4194304 | tf_op jit(solution)/shard_map/psum | solution.py:72
  10.8 0.7 copy-start.11
  10.8 0.7 copy-start.10
  10.8 280.2 %all-gather.11.cloned.1.call-start = ((), (), s32[]{:S(2)}) async-start(), calls=%async_computation.7 | async-start | bytes 5242880 | tf_op jit(solution)/shard_map/all_gather | solution.py:20
  133.4 97.0 %copy-start.8 = (f32[1024]{0:T(1024)S(1)}, f32[1024]{0:T(1024)}, u32[]{:S(2)}) copy-start(f32[1024]{0:T(1024)} %param.8) | copy-start | bytes 12292
  135.1 97.3 %copy-start.2 = (f32[512,1024]{1,0:T(8,128)}, f32[512,1024]{1,0:T(8,128)S(1)}, u32[]{:S(2)}) copy-start(f32[512,1024]{1,0:T(8,128)S(1)} %reshape.63) | copy-start | bytes 6291460
  232.5 1.0 copy-start.5
  235.1 116.0 %copy-start.3 = (f32[512,512]{1,0:T(8,128)S(1)}, f32[512,512]{1,0:T(8,128)}, u32[]{:S(2)}) copy-start(f32[512,512]{1,0:T(8,128)} %fusion.18) | copy-start | bytes 3145732
  235.2 116.0 %copy-start.4 = (bf16[512,512]{1,0:T(8,128)(2,1)S(1)}, bf16[512,512]{1,0:T(8,128)(2,1)}, u32[]{:S(2)}) copy-start(bf16[512,512]{1,0:T(8,128)(2,1)} %param.6) | copy-start | bytes 1572868
  235.2 116.0 %copy-start.9 = (f32[512]{0:T(512)S(1)}, f32[512]{0:T(512)}, u32[]{:S(2)}) copy-start(f32[512]{0:T(512)} %param.10) | copy-start | bytes 6148
  235.2 116.0 %all-gather.7.cloned.1.call-start = ((), (), s32[]{:S(2)}) async-start(), calls=%async_computation.3 | async-start | bytes 5242880 | tf_op jit(solution)/shard_map/all_gather | solution.py:20
  294.7 118.7 %all-gather.13.cloned.1.call-start = ((), (), s32[]{:S(2)}) async-start(), calls=%async_computation.8 | async-start | bytes 5242880 | tf_op jit(solution)/shard_map/all_gather | solution.py:20
  356.8 116.7 %copy-start.1 = (f32[512,512]{1,0:T(8,128)S(1)}, f32[512,512]{1,0:T(8,128)}, u32[]{:S(2)}) copy-start(f32[512,512]{1,0:T(8,128)} %fusion.12) | copy-start | bytes 3145732
  356.8 116.7 %all-gather.9.cloned.1.call-start = ((), (), s32[]{:S(2)}) async-start(), calls=%async_computation.4 | async-start | bytes 5242880 | tf_op jit(solution)/shard_map/all_gather | solution.py:20
  417.0 85.3 %reduce-scatter.3.cloned.1.call-start = ((), (), s32[]{:S(2)}) async-start(), calls=%async_computation.5 | async-start | bytes 3145728 | tf_op jit(solution)/shard_map/reduce_scatter | solution.py:35
  480.3 22.0 %copy-start.6 = (bf16[512,1024]{1,0:T(8,128)(2,1)S(1)}, bf16[512,1024]{1,0:T(8,128)(2,1)}, u32[]{:S(2)}) copy-start(bf16[512,1024]{1,0:T(8,128)(2,1)} %copy-done.5) | copy-start | bytes 3145732
  480.3 85.0 %reduce-scatter.5.cloned.1.call-start = ((), (), s32[]{:S(2)}) async-start(), calls=%async_computation.6 | async-start | bytes 1114112 | tf_op jit(solution)/shard_map/reduce_scatter | solution.py:35
Sparse Core Ops, SparseCore 0:
  10.9 219.4 all-reduce.1
  235.3 55.6 all-gather.10
  294.8 56.2 all-gather.6
  356.9 56.3 all-gather.12
  417.1 56.2 all-gather.8
  480.4 21.8 reduce-scatter.2
  505.1 60.1 reduce-scatter.4
where the time goes:
time: 583 us; the launch traced here: 574 us
  waiting for transfers between devices  404 us (69%)
  local copies, waits for them, and re-layouts  126 us (22%)
  other arithmetic  21.4 us (4%)
  between operations  14.3 us (2%)
  matrix products  7.66 us (1%)
    all_gather x4, waiting for transfers between devices, carried_in(): pieces = lax.all_gather(total, axis)  225 us
    unnamed x28, local copies, waits for them, and re-layouts  123 us
    psum x1, waiting for transfers between devices, local(): preact = lax.psum(partial_pre, WIDE) + enc_bias  95.2 us
    reduce_scatter x2, waiting for transfers between devices, reduced_to_own(): pieces = lax.psum_scatter(pieces, axes[k], scatter_dimension=0, tiled=True)  83.2 us
  transfers between devices with their start and end apart: 7, of which 7 were waited for; matrix products, arithmetic and copies ran while one was open for 22% of the time, Pallas kernels for 0%

commit v1 on v0

v1 whole, which is shorter than its diff:
```python
import jax
import jax.numpy as jnp
from jax import lax
from jax.experimental import pallas as pl
from jax.experimental.pallas import tpu as pltpu
from jax.sharding import Mesh
from jax.sharding import PartitionSpec as P

NARROW = ("narrow_0", "narrow_1")
WIDE = ("wide_0", "wide_1")
LANES = 128
HALF = 64
F32 = jnp.float32
BF16 = jnp.bfloat16
LIMIT = 48 * 1024 * 1024


def lookup(rows, lanes):
    return jnp.take_along_axis(rows, lanes, axis=1, mode="promise_in_bounds")


def spread_slots(ids):
    token = lax.broadcasted_iota(jnp.int32, (ids.shape[0], LANES), 0)
    lane = lax.broadcasted_iota(jnp.int32, (ids.shape[0], LANES), 1)
    both = jnp.concatenate([ids, ids], axis=1)
    return jnp.where((token >> 3) & 1 == lane >> 6, both, -1)


def pick_slots(rows, slots):
    low, high = slots & (LANES - 1), slots >> 7
    picked = jnp.zeros(slots.shape, F32)
    for c in range(rows.shape[1] // LANES):
        picked = jnp.where(high == c, lookup(rows[:, c * LANES : (c + 1) * LANES], low), picked)
    picked = picked.reshape(-1, 2, 8, LANES)
    return (picked[:, 0] + picked[:, 1]).reshape(-1, LANES)


def unpack_rows(packed):
    rows = packed.reshape(-1, 1, 8, LANES)
    return jnp.concatenate([rows, rows], axis=1).reshape(-1, LANES)


def slot_lanes(maps, c):
    return (maps[c // 4] >> (8 * (c % 4))) & 255


def place(values, maps, c, shift=None):
    lanes = slot_lanes(maps, c)
    placed = lookup(values, (lanes - 1) & (LANES - 1))
    if shift is not None:
        placed = placed + shift
    return jnp.where(lanes > 0, placed, 0.0)


def encode_kernel(act, weight, slots, out):
    step = 128
    for i in range(act.shape[0] // step):
        rows = pl.ds(i * step, step)
        part = jnp.dot(act[rows, :], weight[...], preferred_element_type=F32)
        out[pl.ds(i * step // 2, step // 2), :] = pick_slots(part, slots[rows, :]).astype(out.dtype)


def maps_kernel(ids_by_slot, out):
    count, tokens = ids_by_slot.shape
    line = lax.broadcasted_iota(jnp.int32, (LANES, LANES), 0)
    token = lax.broadcasted_iota(jnp.int32, (1, LANES), 1)
    half = HALF * ((token >> 3) & 1)
    for i in range(tokens // LANES):
        cols = pl.ds(i * LANES, LANES)

        def body(block_of_eight, maps):
            first = pl.multiple_of(8 * block_of_eight, 8)
            eight = ids_by_slot[pl.ds(first, 8), cols]
            block = eight >> 7
            code = (half + first + 1 + lax.broadcasted_iota(jnp.int32, eight.shape, 0)) << (8 * (block & 3))
            low = eight & (LANES - 1)
            codes = [
                jnp.where((block >= 0) & (block < 4), code, 0),
                jnp.where((block >= 4) & (block < 8), code, 0),
            ]
            for k in range(8):
                hit = line == low[k : k + 1]
                maps = [m | jnp.where(hit, f[k : k + 1], 0) for m, f in zip(maps, codes)]
            return tuple(maps)

        zero = jnp.zeros((LANES, LANES), jnp.int32)
        maps = lax.fori_loop(0, count // 8, body, (zero, zero))
        for m in range(2):
            out[m, cols, :] = maps[m].T


def decode_kernel(packed, maps, bias, weight, latents, rec):
    step = 128
    for i in range(latents.shape[0] // step):
        rows = pl.ds(i * step, step)
        values = unpack_rows(packed[pl.ds(i * step // 2, step // 2), :].astype(F32))
        mine = [maps[0, rows, :], maps[1, rows, :]]
        for c in range(latents.shape[1] // LANES):
            cols = pl.ds(c * LANES, LANES)
            latents[rows, cols] = place(values, mine, c, bias[:, cols]).astype(BF16)
        rec[rows, :] = jnp.dot(latents[rows, :], weight[...], preferred_element_type=F32).astype(rec.dtype)


def mix_kernel(recs, act, bias, out):
    groups = recs.shape[0]
    for r in range(0, recs.shape[1], 8):
        for c in range(0, recs.shape[2], LANES):
            at = (pl.ds(r, 8), pl.ds(c, LANES))
            err = bias[:, pl.ds(c, LANES)] - act[at].astype(F32)
            errs = []
            for g in range(groups):
                err = err + recs[(g, *at)].astype(F32)
                errs.append(err)
            suffix = jnp.zeros_like(err)
            for g in reversed(range(groups)):
                suffix = suffix + errs[g]
                out[(g, *at)] = (suffix * (1.0 / groups)).astype(out.dtype)


def grad_kernel(back, weight, slots, out):
    step = 128
    for i in range(back.shape[0] // step):
        rows = pl.ds(i * step, step)
        part = lax.dot_general(back[rows, :], weight[...], (((1,), (1,)), ((), ())), preferred_element_type=F32)
        out[pl.ds(i * step // 2, step // 2), :] = pick_slots(part, slots[rows, :]).astype(out.dtype)


def own_kernel(pieces, maps, out):
    values = unpack_rows(jnp.sum(pieces[...].astype(F32), axis=0))
    mine = [maps[0], maps[1]]
    for c in range(out.shape[1] // LANES):
        out[:, pl.ds(c * LANES, LANES)] = place(values, mine, c)


def call(kernel, shapes, flops, *args):
    moved = sum(a.size * a.dtype.itemsize for a in (*args, *jax.tree.leaves(shapes)))
    return pl.pallas_call(
        kernel,
        out_shape=shapes,
        compiler_params=pltpu.CompilerParams(vmem_limit_bytes=LIMIT),
        cost_estimate=pl.CostEstimate(flops=flops, bytes_accessed=moved, transcendentals=0),
    )(*args)


def array(shape, dtype):
    return jax.ShapeDtypeStruct(shape, dtype)


def swap(pieces, axes):
    return lax.all_to_all(pieces, axes, 0, 0)


def local(activations, enc_weight, enc_bias, dec_weight, dec_bias, active_ids):
    tokens, channels = activations.shape
    width = enc_weight.shape[1]
    groups, wide = lax.axis_size(NARROW), lax.axis_size(WIDE)
    group = lax.axis_index(NARROW)
    work = 2 * tokens * channels * width
    ids = active_ids - group * width
    slots = spread_slots(ids)
    packed = (tokens // 2, LANES)
    share = (wide, tokens // 2 // wide, LANES)

    partial = call(encode_kernel, array(packed, BF16), work, activations, enc_weight, slots)
    pieces = swap(partial.reshape(share), WIDE)
    maps = call(maps_kernel, array((2, tokens, LANES), jnp.int32), work // 8, ids.T)
    owned = jnp.sum(pieces.astype(F32), axis=0).astype(BF16)
    preact = swap(jnp.broadcast_to(owned[None], share), WIDE).reshape(packed)
    latents, rec = call(
        decode_kernel,
        (array((tokens, width), BF16), array((tokens, channels), BF16)),
        work,
        preact,
        maps,
        enc_bias[None],
        dec_weight,
    )
    rows = tokens // groups
    recs = swap(rec.reshape(groups, rows, channels), NARROW)
    act_rows = lax.dynamic_slice_in_dim(activations, group * rows, rows, 0)
    mixed = call(mix_kernel, array(recs.shape, BF16), 8 * recs.size, recs, act_rows, dec_bias[None])
    back = swap(mixed, NARROW).reshape(tokens, channels)
    grads = call(grad_kernel, array(packed, BF16), work, back, dec_weight, slots)
    parts = swap(grads.reshape(share), WIDE)
    dec_grad = lax.dot_general(
        latents, back, (((0,), (0,)), ((), ())), preferred_element_type=F32
    ).astype(BF16)
    own_rows = tokens // wide
    own_maps = lax.dynamic_slice_in_dim(maps, lax.axis_index(WIDE) * own_rows, own_rows, 1)
    latent_grad = call(own_kernel, array((own_rows, width), F32), 1 << 20, parts, own_maps)
    return dec_grad, latent_grad


def solution(mesh):
    split = Mesh(mesh.devices.reshape(16, 2, 4, 4), ("wide_0", "wide_1", "narrow_0", "narrow_1"))
    return jax.shard_map(
        local,
        mesh=split,
        in_specs=(P(None, WIDE), P(WIDE, NARROW), P(NARROW), P(NARROW, WIDE), P(WIDE), P()),
        out_specs=(P(NARROW, WIDE), P(WIDE, NARROW)),
        check_vma=False,
    )
```

time: 583 us -> 112 us (0.19); the launches traced: 574 us -> 111 us
  waiting for transfers between devices: 404 us -> 38.1 us
  local copies, waits for them, and re-layouts: 126 us -> 4.06 us
  blocking collectives: 0 us -> 29.8 us
  starting transfers between devices: 0.29 us -> 23.7 us
  other arithmetic: 21.4 us -> 0.29 us
  between operations: 14.3 us -> 0.82 us
  Pallas kernels: 0 us -> 12.6 us
  matrix products: 7.66 us -> 1.72 us
    all_gather x4 -> x0, waiting for transfers between devices: 225 us -> none  [carried_in(): pieces = lax.all_gather(total, axis)]
    unnamed x28 -> x15, local copies, waits for them, and re-layouts: 123 us -> 3.29 us
    psum x1 -> x0, waiting for transfers between devices: 95.2 us -> none  [local(): preact = lax.psum(partial_pre, WIDE) + enc_bias]
    reduce_scatter x2 -> x0, waiting for transfers between devices: 83.2 us -> none  [reduced_to_own(): pieces = lax.psum_scatter(pieces, axes[k], scatter_dimension=0, tiled=True)]
    all_to_all x0 -> x4, waiting for transfers between devices: none -> 38.1 us  [swap(): return lax.all_to_all(pieces, axes, 0, 0)]
    all_to_all x0 -> x1, blocking collectives: none -> 29.8 us  [swap(): return lax.all_to_all(pieces, axes, 0, 0)]
    all_to_all x0 -> x4, starting transfers between devices: none -> 23.7 us  [swap(): return lax.all_to_all(pieces, axes, 0, 0)]
    pallas_call x0 -> x6, Pallas kernels: none -> 12.6 us  [call(): pl.pallas_call(kernel, out_shape=shapes, compiler_params=pltpu.CompilerPa...]
  transfers between devices with their start and end apart: 7 -> 4, of which waited for: 7 -> 4; matrix products, arithmetic and copies ran while one was open for 22% -> 2% of each run, Pallas kernels for 0% -> 4%
where the time goes in v1:
time: 112 us; the launch traced here: 111 us
  waiting for transfers between devices  38.1 us (34%)
  blocking collectives  29.8 us (27%)
  starting transfers between devices  23.7 us (21%)
  Pallas kernels  12.6 us (11%)
  local copies, waits for them, and re-layouts  4.06 us (4%)
  matrix products  1.72 us (2%)
    all_to_all x4, waiting for transfers between devices, swap(): return lax.all_to_all(pieces, axes, 0, 0)  38.1 us
    all_to_all x1, blocking collectives, swap(): return lax.all_to_all(pieces, axes, 0, 0)  29.8 us
    all_to_all x4, starting transfers between devices, swap(): return lax.all_to_all(pieces, axes, 0, 0)  23.7 us
    pallas_call x6, Pallas kernels, call(): pl.pallas_call(kernel, out_shape=shapes, compiler_params=pltpu.CompilerPa...  12.6 us
    unnamed x15, local copies, waits for them, and re-layouts  3.29 us
  transfers between devices with their start and end apart: 4, of which 4 were waited for; matrix products, arithmetic and copies ran while one was open for 2% of the time, Pallas kernels for 4%

profile of v1, /device:TPU:1, one launch (start us, length us, event | category | flops | bytes accessed | tf_op | source)
XLA Modules:
  0.0 111.0 jit_solution(6274848579970095000)
XLA Ops:
  0.6 0.0 copy-start.1
  0.7 1.1 copy.8
  1.8 0.2 add_select_fusion.slots
  2.0 0.0 copy-done.1
  2.0 0.0 copy-start.2
  2.0 1.2 %copy-done.2 = bf16[512,1024]{1,0:T(8,128)(2,1)S(1)} copy-done((bf16[512,1024]{1,0:T(8,128)(2,1)S(1)}, bf16[512,1024]{1,0:T(8,128)(2,1)}, u32[]{:S(2)}) %copy-start.2) | copy-done | bytes 1048600
  3.2 1.3 %shard_map.77 = bf16[256,128]{1,0:T(8,128)(2,1)S(1)} custom-call(bf16[512,512]{1,0:T(8,128)(2,1)S(1)} %copy-done.1, bf16[512,1024]{1,0:T(8,128)(2,1)S(1)} %copy-done.2, s32[512,128]{1,0:T(8,128)S(1)} %add_select_fusion.slots), custom_call_target="tpu_custom_call" | custom-call | flops 536870912 | bytes 1900544 | tf_op jit(solution)/shard_map/pallas_call | solution.py:137
  4.6 0.0 copy-start.3
  4.6 0.0 copy-start.4
  4.6 29.8 %all_to_all.25 = bf16[32,8,128]{2,1,0:T(8,128)(2,1)S(1)} all-to-all(bf16[32,8,128]{2,1,0:T(8,128)(2,1)S(1)} %bitcast.14), channel_id=1, replica_groups=mesh['wide_0'=16,'wide_1'=2,'narrow_0'=4,'narrow_1'=4] {'wide_0','wide_1'}, dimensions={0} | all-to-all | bytes 131072 | tf_op jit(solution)/shard_map/all_to_all | solution.py:150
  34.4 0.6 broadcast_in_dim.17
  35.0 5.1 %all-to-all-start.1 = ((bf16[32,8,128]{2,1,0:T(8,128)(2,1)}), bf16[32,8,128]{2,1,0:T(8,128)(2,1)S(1)}, u32[]{:S(2)}, u32[]{:S(2)}) async-start(bf16[32,8,128]{2,1,0:T(8,128)(2,1)} %broadcast_in_dim.17), calls=%async_computation.1 | async-start | bytes 131072 | tf_op jit(solution)/shard_map/all_to_all | solution.py:150
  40.2 0.1 copy.9.ids_by_slot
  40.3 4.3 %shard_map.78.maps = s32[2,512,128]{2,1,0:T(8,128)S(1)} custom-call(s32[64,512]{1,0:T(8,128)S(1)} %copy.9.ids_by_slot), custom_call_target="tpu_custom_call" | custom-call | flops 67108864 | bytes 655360 | tf_op jit(solution)/shard_map/pallas_call | solution.py:137
  44.6 8.6 %all-to-all-done.1 = bf16[32,8,128]{2,1,0:T(8,128)(2,1)S(1)} async-done(((bf16[32,8,128]{2,1,0:T(8,128)(2,1)}), bf16[32,8,128]{2,1,0:T(8,128)(2,1)S(1)}, u32[]{:S(2)}, u32[]{:S(2)}) %all-to-all-start.1) | async-done | bytes 65568 | tf_op jit(solution)/shard_map/all_to_all | solution.py:150
  53.2 0.0 copy-done.3
  53.2 0.0 copy-done.4
  53.2 2.8 %shard_map.79 = (bf16[512,1024]{1,0:T(8,128)(2,1)S(1)}, bf16[512,512]{1,0:T(8,128)(2,1)}) custom-call(bf16[256,128]{1,0:T(8,128)(2,1)S(1)} %bitcast.13, s32[2,512,128]{2,1,0:T(8,128)S(1)} %shard_map.78.maps, f32[1,1024]{1,0:T(1,128)S(1)} %bitcast.16, bf16[1024,512]{1,0:T(8,128)(2,1)S(1)} %copy-done.3), custom_call_target="tpu_custom_call" | custom-call | flops 536870912 | bytes 3215360 | tf_op jit(solution)/shard_map/pallas_call | solution.py:137
  56.1 0.0 copy-start.5
  56.1 1.0 copy-done.5
  57.0 6.9 %all-to-all-start.2 = ((bf16[16,32,512]{2,1,0:T(8,128)(2,1)}), bf16[16,32,512]{2,1,0:T(8,128)(2,1)S(1)}, u32[]{:S(2)}, u32[]{:S(2)}) async-start(bf16[16,32,512]{2,1,0:T(8,128)(2,1)} %bitcast.4), calls=%async_computation.2 | async-start | bytes 1048576 | tf_op jit(solution)/shard_map/all_to_all | solution.py:150
  63.9 9.2 %all-to-all-done.2.recs = bf16[16,32,512]{2,1,0:T(8,128)(2,1)S(1)} async-done(((bf16[16,32,512]{2,1,0:T(8,128)(2,1)}), bf16[16,32,512]{2,1,0:T(8,128)(2,1)S(1)}, u32[]{:S(2)}, u32[]{:S(2)}) %all-to-all-start.2) | async-done | bytes 524320 | tf_op jit(solution)/shard_map/all_to_all | solution.py:150
  73.1 0.0 copy-done
  73.1 1.0 shard_map.80
  74.1 3.6 %all-to-all-start.3 = ((bf16[16,32,512]{2,1,0:T(8,128)(2,1)}), bf16[16,32,512]{2,1,0:T(8,128)(2,1)S(1)}, u32[]{:S(2)}, u32[]{:S(2)}) async-start(bf16[16,32,512]{2,1,0:T(8,128)(2,1)} %shard_map.80), calls=%async_computation.3 | async-start | bytes 1048576 | tf_op jit(solution)/shard_map/all_to_all | solution.py:150
  77.7 8.9 %all-to-all-done.3 = bf16[16,32,512]{2,1,0:T(8,128)(2,1)S(1)} async-done(((bf16[16,32,512]{2,1,0:T(8,128)(2,1)}), bf16[16,32,512]{2,1,0:T(8,128)(2,1)S(1)}, u32[]{:S(2)}, u32[]{:S(2)}) %all-to-all-start.3) | async-done | bytes 524320 | tf_op jit(solution)/shard_map/all_to_all | solution.py:150
  86.7 2.3 %shard_map.81 = bf16[256,128]{1,0:T(8,128)(2,1)} custom-call(bf16[512,512]{1,0:T(8,128)(2,1)S(1)} %bitcast.11, bf16[1024,512]{1,0:T(8,128)(2,1)S(1)} %copy-done.3, s32[512,128]{1,0:T(8,128)S(1)} %add_select_fusion.slots), custom_call_target="tpu_custom_call" | custom-call | flops 536870912 | bytes 1900544 | tf_op jit(solution)/shard_map/pallas_call | solution.py:137
  89.0 8.1 %all-to-all-start.4 = ((bf16[32,8,128]{2,1,0:T(8,128)(2,1)}), bf16[32,8,128]{2,1,0:T(8,128)(2,1)S(1)}, u32[]{:S(2)}, u32[]{:S(2)}) async-start(bf16[32,8,128]{2,1,0:T(8,128)(2,1)} %bitcast.7), calls=%async_computation.4 | async-start | bytes 131072 | tf_op jit(solution)/shard_map/all_to_all | solution.py:150
  97.1 0.0 copy-done.6
  97.1 1.7 %convolution_convert_fusion = bf16[1024,512]{1,0:T(8,128)(2,1)} fusion(bf16[512,1024]{1,0:T(8,128)(2,1)S(1)} %copy-done.6, bf16[512,512]{1,0:T(8,128)(2,1)S(1)} %bitcast.12), kind=kOutput, calls=%fused_computation | convolution fusion | flops 537395200 | bytes 2621440 | tf_op jit(solution)/shard_map/dot_general | solution.py:185
  98.8 11.3 %all-to-all-done.4.pieces = bf16[32,8,128]{2,1,0:T(8,128)(2,1)S(1)} async-done(((bf16[32,8,128]{2,1,0:T(8,128)(2,1)}), bf16[32,8,128]{2,1,0:T(8,128)(2,1)S(1)}, u32[]{:S(2)}, u32[]{:S(2)}) %all-to-all-start.4) | async-done | bytes 65568 | tf_op jit(solution)/shard_map/all_to_all | solution.py:150
  110.2 0.8 shard_map.82
  (9 shorter events, 0.1 us)
Async XLA Ops:
  0.6 1.4 %copy-start.1 = (bf16[512,512]{1,0:T(8,128)(2,1)S(1)}, bf16[512,512]{1,0:T(8,128)(2,1)}, u32[]{:S(2)}) copy-start(bf16[512,512]{1,0:T(8,128)(2,1)} %act.1) | copy-start | bytes 1572868
  2.0 1.2 %copy-start.2 = (bf16[512,1024]{1,0:T(8,128)(2,1)S(1)}, bf16[512,1024]{1,0:T(8,128)(2,1)}, u32[]{:S(2)}) copy-start(bf16[512,1024]{1,0:T(8,128)(2,1)} %weight.3) | copy-start | bytes 3145732
  4.6 48.6 %copy-start.3 = (bf16[1024,512]{1,0:T(8,128)(2,1)S(1)}, bf16[1024,512]{1,0:T(8,128)(2,1)}, u32[]{:S(2)}) copy-start(bf16[1024,512]{1,0:T(8,128)(2,1)} %weight.5) | copy-start | bytes 3145732
  4.6 48.6 %copy-start.4 = (f32[1024]{0:T(1024)S(1)}, f32[1024]{0:T(1024)}, u32[]{:S(2)}) copy-start(f32[1024]{0:T(1024)} %param.8) | copy-start | bytes 12292
  35.0 18.2 %all-to-all-start.1 = ((bf16[32,8,128]{2,1,0:T(8,128)(2,1)}), bf16[32,8,128]{2,1,0:T(8,128)(2,1)S(1)}, u32[]{:S(2)}, u32[]{:S(2)}) async-start(bf16[32,8,128]{2,1,0:T(8,128)(2,1)} %broadcast_in_dim.17), calls=%async_computation.1 | async-start | bytes 131072 | tf_op jit(solution)/shard_map/all_to_all | solution.py:150
  56.1 1.0 copy-start.5
  57.0 16.1 %copy-start = (f32[512]{0:T(512)S(1)}, f32[512]{0:T(512)}, u32[]{:S(2)}) copy-start(f32[512]{0:T(512)} %param.10) | copy-start | bytes 6148
  57.0 16.1 %all-to-all-start.2 = ((bf16[16,32,512]{2,1,0:T(8,128)(2,1)}), bf16[16,32,512]{2,1,0:T(8,128)(2,1)S(1)}, u32[]{:S(2)}, u32[]{:S(2)}) async-start(bf16[16,32,512]{2,1,0:T(8,128)(2,1)} %bitcast.4), calls=%async_computation.2 | async-start | bytes 1048576 | tf_op jit(solution)/shard_map/all_to_all | solution.py:150
  74.1 12.5 %all-to-all-start.3 = ((bf16[16,32,512]{2,1,0:T(8,128)(2,1)}), bf16[16,32,512]{2,1,0:T(8,128)(2,1)S(1)}, u32[]{:S(2)}, u32[]{:S(2)}) async-start(bf16[16,32,512]{2,1,0:T(8,128)(2,1)} %shard_map.80), calls=%async_computation.3 | async-start | bytes 1048576 | tf_op jit(solution)/shard_map/all_to_all | solution.py:150
  86.7 10.5 %copy-start.6 = (bf16[512,1024]{1,0:T(8,128)(2,1)S(1)}, bf16[512,1024]{1,0:T(8,128)(2,1)}, u32[]{:S(2)}) copy-start(bf16[512,1024]{1,0:T(8,128)(2,1)} %copy-done.5) | copy-start | bytes 3145732
  89.0 21.2 %all-to-all-start.4 = ((bf16[32,8,128]{2,1,0:T(8,128)(2,1)}), bf16[32,8,128]{2,1,0:T(8,128)(2,1)S(1)}, u32[]{:S(2)}, u32[]{:S(2)}) async-start(bf16[32,8,128]{2,1,0:T(8,128)(2,1)} %bitcast.7), calls=%async_computation.4 | async-start | bytes 131072 | tf_op jit(solution)/shard_map/all_to_all | solution.py:150

commit v2 on v1

v2 whole, which is shorter than its diff:
```python
import functools

import jax
import jax.numpy as jnp
from jax import lax
from jax.experimental import pallas as pl
from jax.experimental.pallas import tpu as pltpu
from jax.sharding import Mesh
from jax.sharding import PartitionSpec as P

NARROW = ("narrow_0", "narrow_1")
WIDE = ("wide_0", "wide_1")
LANES = 128
F32 = jnp.float32
BF16 = jnp.bfloat16
LIMIT = 16 * 1024 * 1024


def lookup(rows, lanes):
    return jnp.take_along_axis(rows, lanes, axis=1, mode="promise_in_bounds")


def pick_slots(rows, slots, per):
    low, high = slots & (LANES - 1), slots >> 7
    picked = jnp.zeros(slots.shape, F32)
    for c in range(rows.shape[1] // LANES):
        picked = jnp.where(high == c, lookup(rows[:, c * LANES : (c + 1) * LANES], low), picked)
    picked = picked.reshape(-1, per, 8, LANES)
    total = picked[:, 0]
    for j in range(1, per):
        total = total + picked[:, j]
    return total.reshape(-1, LANES)


def unpack_rows(packed, per):
    rows = packed.reshape(-1, 1, 8, LANES)
    return jnp.concatenate([rows] * per, axis=1).reshape(-1, LANES)


def place(values, maps, c, shift=None):
    lanes = (maps[c // 4] >> (8 * (c % 4))) & 255
    placed = lookup(values, (lanes - 1) & (LANES - 1))
    if shift is not None:
        placed = placed + shift
    return jnp.where(lanes > 0, placed, 0.0)


def fill_kernel(per, width, group, ids, named, slots, most):
    count = LANES // per
    token = lax.broadcasted_iota(jnp.int32, (1, LANES), 1)
    line = lax.broadcasted_iota(jnp.int32, (LANES, LANES), 0)
    place_of = lax.broadcasted_iota(jnp.int32, (count, LANES), 0)
    groups = lax.broadcasted_iota(jnp.int32, (16, LANES), 0)
    shift = width.bit_length() - 1
    needed = jnp.zeros((16, LANES), jnp.int32)
    for i in range(ids.shape[1] // LANES):
        cols = pl.ds(i * LANES, LANES)
        theirs = ids[:, cols]
        within = theirs - group[0] * width
        mine = (within >= 0) & (within < width)
        if count == ids.shape[0]:
            held = jnp.where(mine, within, -1)
        else:
            which = theirs >> shift
            held = jnp.full((count, LANES), -1, jnp.int32)
            taken = jnp.zeros((1, LANES), jnp.int32)
            tally = jnp.zeros((16, LANES), jnp.int32)
            for k in range(ids.shape[0]):
                here = mine[k : k + 1]
                at = jnp.where(here, taken, count)
                held = jnp.where(place_of == at, within[k : k + 1], held)
                taken = taken + jnp.where(here, 1, 0)
                tally = tally + jnp.where(groups == which[k : k + 1], 1, 0)
            needed = jnp.maximum(needed, tally)
        named[:, cols] = held
        spread = jnp.concatenate([held] * per, axis=0)
        spread = jnp.where(line // count == (token >> 3) & (per - 1), spread, -1)
        slots[cols, :] = spread.T
    most[...] = needed


def maps_kernel(per, named, out):
    count, tokens = named.shape
    line = lax.broadcasted_iota(jnp.int32, (LANES, LANES), 0)
    token = lax.broadcasted_iota(jnp.int32, (1, LANES), 1)
    base = count * ((token >> 3) & (per - 1)) + 1
    for i in range(tokens // LANES):
        cols = pl.ds(i * LANES, LANES)

        def body(n, maps):
            first = pl.multiple_of(8 * n, 8)
            eight = named[pl.ds(first, 8), cols]
            block = eight >> 7
            code = (base + first + lax.broadcasted_iota(jnp.int32, eight.shape, 0)) << (8 * (block & 3))
            low = eight & (LANES - 1)
            codes = [
                jnp.where((block >= 0) & (block < 4), code, 0),
                jnp.where((block >= 4) & (block < 8), code, 0),
            ]
            for k in range(8):
                hit = line == low[k : k + 1]
                maps = [m | jnp.where(hit, f[k : k + 1], 0) for m, f in zip(maps, codes)]
            return tuple(maps)

        zero = jnp.zeros((LANES, LANES), jnp.int32)
        maps = lax.fori_loop(0, count // 8, body, (zero, zero))
        for m in range(2):
            out[m, cols, :] = maps[m].T


def encode_kernel(per, act, weight, slots, out):
    step = 128
    for i in range(act.shape[0] // step):
        rows = pl.ds(i * step, step)
        part = jnp.dot(act[rows, :], weight[...], preferred_element_type=F32)
        out[pl.ds(i * step // per, step // per), :] = pick_slots(part, slots[rows, :], per)


def decode_kernel(per, packed, maps, bias, weight, latents, rec):
    step = 128
    for i in range(latents.shape[0] // step):
        rows = pl.ds(i * step, step)
        values = unpack_rows(packed[pl.ds(i * step // per, step // per), :], per)
        mine = [maps[0, rows, :], maps[1, rows, :]]
        for c in range(latents.shape[1] // LANES):
            cols = pl.ds(c * LANES, LANES)
            latents[rows, cols] = place(values, mine, c, bias[:, cols]).astype(BF16)
        rec[rows, :] = jnp.dot(latents[rows, :], weight[...], preferred_element_type=F32).astype(rec.dtype)


def mix_kernel(recs, act, bias, out):
    groups = recs.shape[0]
    for r in range(0, recs.shape[1], 8):
        for c in range(0, recs.shape[2], LANES):
            at = (pl.ds(r, 8), pl.ds(c, LANES))
            err = bias[:, pl.ds(c, LANES)] - act[at].astype(F32)
            errs = []
            for g in range(groups):
                err = err + recs[(g, *at)].astype(F32)
                errs.append(err)
            suffix = jnp.zeros_like(err)
            for g in reversed(range(groups)):
                suffix = suffix + errs[g]
                out[(g, *at)] = (suffix * (1.0 / groups)).astype(out.dtype)


def grad_kernel(per, back, weight, slots, out):
    step = 128
    for i in range(back.shape[0] // step):
        rows = pl.ds(i * step, step)
        part = lax.dot_general(back[rows, :], weight[...], (((1,), (1,)), ((), ())), preferred_element_type=F32)
        packed = pick_slots(part, slots[rows, :], per)
        for owner in range(step // 16):
            block = 2 * owner // per
            out[i * step // 16 + owner] = packed[8 * block : 8 * block + 8]


def own_kernel(pieces, maps, out):
    values = unpack_rows(jnp.sum(pieces[...], axis=0), 2)
    mine = [maps[0], maps[1]]
    for c in range(out.shape[1] // LANES):
        out[:, pl.ds(c * LANES, LANES)] = place(values, mine, c)


def call(kernel, shapes, flops, *args, **params):
    moved = sum(a.size * a.dtype.itemsize for a in (*args, *jax.tree.leaves(shapes)))
    return pl.pallas_call(
        kernel,
        out_shape=shapes,
        compiler_params=pltpu.CompilerParams(vmem_limit_bytes=LIMIT),
        cost_estimate=pl.CostEstimate(flops=flops, bytes_accessed=moved, transcendentals=0),
        **params,
    )(*args)


def array(shape, dtype):
    return jax.ShapeDtypeStruct(shape, dtype)


def swap(pieces, axes):
    return lax.all_to_all(pieces, axes, 0, 0)


def summed_over_wide(partial):
    ring, core = WIDE
    rows = partial.shape[0] // 2
    both = lax.all_gather(partial, core)
    half = lax.dynamic_slice_in_dim(both, lax.axis_index(core) * rows, rows, 1)
    half = (half[0] + half[1]).astype(BF16)
    pieces = swap(jnp.broadcast_to(half[None], (lax.axis_size(ring), *half.shape)), ring)
    return lax.all_gather(jnp.sum(pieces.astype(F32), axis=0), core, tiled=True)


def fill(per, group, ids, width):
    tokens = ids.shape[1]
    in_vmem = pl.BlockSpec(memory_space=pltpu.VMEM)
    return call(
        functools.partial(fill_kernel, per, width),
        (
            array((LANES // per, tokens), jnp.int32),
            array((tokens, LANES), jnp.int32),
            array((16, LANES), jnp.int32),
        ),
        1 << 20,
        group,
        ids,
        in_specs=[pl.BlockSpec(memory_space=pltpu.SMEM), in_vmem],
    )


def step_with(per, activations, enc_weight, enc_bias, dec_weight, dec_bias, named, slots):
    tokens, channels = activations.shape
    width = enc_weight.shape[1]
    groups, wide = lax.axis_size(NARROW), lax.axis_size(WIDE)
    group = lax.axis_index(NARROW)
    work = 2 * tokens * channels * width

    partial = call(
        functools.partial(encode_kernel, per),
        array((tokens // per, LANES), F32),
        work,
        activations,
        enc_weight,
        slots,
    )
    maps = call(functools.partial(maps_kernel, per), array((2, tokens, LANES), jnp.int32), work // 8, named)
    preact = summed_over_wide(partial)
    latents, rec = call(
        functools.partial(decode_kernel, per),
        (array((tokens, width), BF16), array((tokens, channels), BF16)),
        work,
        preact,
        maps,
        enc_bias[None],
        dec_weight,
    )
    rows = tokens // groups
    recs = swap(rec.reshape(groups, rows, channels), NARROW)
    act_rows = lax.dynamic_slice_in_dim(activations, group * rows, rows, 0)
    mixed = call(mix_kernel, array(recs.shape, BF16), 8 * recs.size, recs, act_rows, dec_bias[None])
    back = swap(mixed, NARROW).reshape(tokens, channels)
    grads = call(
        functools.partial(grad_kernel, per), array((wide, 8, LANES), F32), work, back, dec_weight, slots
    )
    parts = swap(grads, WIDE)
    dec_grad = lax.dot_general(
        latents, back, (((0,), (0,)), ((), ())), preferred_element_type=F32
    ).astype(BF16)
    own_rows = tokens // wide
    own_maps = lax.dynamic_slice_in_dim(maps, lax.axis_index(WIDE) * own_rows, own_rows, 1)
    latent_grad = call(own_kernel, array((own_rows, width), F32), 1 << 20, parts, own_maps)
    return dec_grad, latent_grad


def local(activations, enc_weight, enc_bias, dec_weight, dec_bias, active_ids):
    width = enc_weight.shape[1]
    group = lax.axis_index(NARROW)[None]
    ids = active_ids.T
    named, slots, most = fill(8, group, ids, width)
    arrays = (activations, enc_weight, enc_bias, dec_weight, dec_bias)

    def few():
        return step_with(8, *arrays, named, slots)

    def many():
        named, slots, _ = fill(2, group, ids, width)
        return step_with(2, *arrays, named, slots)

    return lax.cond(jnp.max(most) <= LANES // 8, few, many)


def solution(mesh):
    split = Mesh(mesh.devices.reshape(16, 2, 4, 4), ("wide_0", "wide_1", "narrow_0", "narrow_1"))
    return jax.shard_map(
        local,
        mesh=split,
        in_specs=(P(None, WIDE), P(WIDE, NARROW), P(NARROW), P(NARROW, WIDE), P(WIDE), P()),
        out_specs=(P(NARROW, WIDE), P(WIDE, NARROW)),
        check_vma=False,
    )
```

time: 112 us -> 103 us (0.920)
  blocking collectives: 29.8 us -> 26.1 us
  waiting for transfers between devices: 38.1 us -> 34.5 us
  local copies, waits for them, and re-layouts: 4.06 us -> 1.47 us
    all_to_all x1, blocking collectives: 29.8 us -> 12.9 us  [swap(): return lax.all_to_all(pieces, axes, 0, 0)]
    all_gather x0 -> x2, blocking collectives: none -> 13.2 us  [the longest x1 8.52 us: summed_over_wide(): both = lax.all_gather(partial, core)]
    all_to_all x4 -> x3, waiting for transfers between devices: 38.1 us -> 34.5 us  [swap(): return lax.all_to_all(pieces, axes, 0, 0)]
    unnamed x15 -> x6, local copies, waits for them, and re-layouts: 3.29 us -> 0.01 us
    pallas_call x6 -> x7, Pallas kernels: 12.6 us -> 12.8 us  [call(): pl.pallas_call(kernel, out_shape=shapes, compiler_params=pltpu.CompilerPa...]
    all_to_all x4 -> x3, starting transfers between devices: 23.7 us -> 23.7 us  [swap(): return lax.all_to_all(pieces, axes, 0, 0)]
  transfers between devices with their start and end apart: 4 -> 3, of which waited for: 4 -> 3; matrix products, arithmetic and copies ran while one was open for 2% -> 2% of each run, Pallas kernels for 4% -> 1%
where the time goes in v2:
time: 103 us; the launch traced here: 102 us
  waiting for transfers between devices  34.5 us (33%)
  blocking collectives  26.1 us (25%)
  starting transfers between devices  23.7 us (23%)
  Pallas kernels  12.8 us (12%)
  matrix products  1.72 us (2%)
  local copies, waits for them, and re-layouts  1.47 us (1%)
  between operations  1.34 us (1%)
    all_to_all x3, waiting for transfers between devices, swap(): return lax.all_to_all(pieces, axes, 0, 0)  34.5 us
    all_to_all x3, starting transfers between devices, swap(): return lax.all_to_all(pieces, axes, 0, 0)  23.7 us
    all_to_all x1, blocking collectives, swap(): return lax.all_to_all(pieces, axes, 0, 0)  12.9 us
    pallas_call x7, Pallas kernels, call(): pl.pallas_call(kernel, out_shape=shapes, compiler_params=pltpu.CompilerPa...  12.8 us
    all_gather x1, blocking collectives, summed_over_wide(): both = lax.all_gather(partial, core)  8.52 us
    all_gather x1, blocking collectives, summed_over_wide(): return lax.all_gather(jnp.sum(pieces.astype(F32), axis=0), core, tiled=True)  4.73 us
  transfers between devices with their start and end apart: 3, of which 3 were waited for; matrix products, arithmetic and copies ran while one was open for 2% of the time, Pallas kernels for 1%

profile of v2, /device:TPU:1, one launch (start us, length us, event | category | flops | bytes accessed | tf_op | source)
XLA Modules:
  0.0 102.4 jit_solution(13759095359707206601)
XLA Ops:
  0.6 0.0 copy-start
  0.6 2.5 %shard_map.77 = (s32[16,512]{1,0:T(8,128)S(1)}, s32[512,128]{1,0:T(8,128)}, s32[16,128]{1,0:T(8,128)S(1)}) custom-call(s32[1]{0:T(128)} %bitcast.12.group, s32[64,512]{1,0:T(8,128)} %bitcast.25), custom_call_target="tpu_custom_call" | custom-call | flops 1048576 | bytes 434180 | tf_op jit(solution)/shard_map/pallas_call | solution.py:167
  3.1 0.0 copy-start.5
  3.1 0.6 reduce_max.9
  3.8 0.0 copy-start.1
  4.4 0.0 copy-done
  4.4 0.0 copy-done.5
  4.4 0.0 copy-done.1
  4.5 97.9 %conditional.2 = (bf16[1024,512]{1,0:T(8,128)(2,1)}, f32[16,1024]{1,0:T(8,128)}) conditional(s32[]{:T(128)} %convert_element_type.22, (s32[1]{0:T(128)}, s32[64,512]{1,0:T(8,128)S(1)}, bf16[512,512]{1,0:T(8,128)(2,1)}, bf16[512,1024]{1,0:T(8,128)(2,1)}, f32[1024]{0:T(1024)S(1)}, /*index=5*/bf16[1024,512]{1,0:T(8,128)(2,1)}, ...), branch_computations={%region_1.0_spmd, %region_3.0_spmd} | conditional | flops 2219327488 | bytes 23099864
  4.5 2.8 %branch_1_fun.6 = f32[64,128]{1,0:T(8,128)S(1)} custom-call(bf16[512,512]{1,0:T(8,128)(2,1)} %get-tuple-element.42.act, bf16[512,1024]{1,0:T(8,128)(2,1)} %get-tuple-element.43.weight, s32[512,128]{1,0:T(8,128)} %get-tuple-element.44.slots), custom_call_target="tpu_custom_call" | custom-call | flops 536870912 | bytes 1867776 | tf_op jit(solution)/shard_map/cond/branch_1_fun/pallas_call | solution.py:167
  7.3 0.0 copy-start.3
  7.3 8.5 %all-gather.1 = f32[128,128]{1,0:T(8,128)S(1)} all-gather(f32[64,128]{1,0:T(8,128)S(1)} %branch_1_fun.6), channel_id=3, replica_groups=mesh['wide_0'=16,'wide_1'=2,'narrow_0'=4,'narrow_1'=4] {'wide_1'}, dimensions={0}, use_global_device_ids=true | all-gather | bytes 98304 | tf_op jit(solution)/shard_map/cond/branch_1_fun/all_gather | solution.py:187
  15.8 0.7 broadcast_in_dim.27
  16.5 9.5 %all-to-all-start.4 = ((bf16[16,32,128]{2,1,0:T(8,128)(2,1)}), bf16[16,32,128]{2,1,0:T(8,128)(2,1)S(1)}, u32[]{:S(2)}, u32[]{:S(2)}) async-start(bf16[16,32,128]{2,1,0:T(8,128)(2,1)} %broadcast_in_dim.27), calls=%async_computation.4 | async-start | bytes 262144 | tf_op jit(solution)/shard_map/cond/branch_1_fun/all_to_all | solution.py:181
  26.0 1.4 %branch_1_fun.7.maps = s32[2,512,128]{2,1,0:T(8,128)S(1)} custom-call(s32[16,512]{1,0:T(8,128)S(1)} %get-tuple-element.45.named), custom_call_target="tpu_custom_call" | custom-call | flops 67108864 | bytes 557056 | tf_op jit(solution)/shard_map/cond/branch_1_fun/pallas_call | solution.py:167
  27.4 10.8 %all-to-all-done.4 = bf16[16,32,128]{2,1,0:T(8,128)(2,1)S(1)} async-done(((bf16[16,32,128]{2,1,0:T(8,128)(2,1)}), bf16[16,32,128]{2,1,0:T(8,128)(2,1)S(1)}, u32[]{:S(2)}, u32[]{:S(2)}) %all-to-all-start.4) | async-done | bytes 131104 | tf_op jit(solution)/shard_map/cond/branch_1_fun/all_to_all | solution.py:181
  38.2 4.7 %all_gather.17.packed = f32[64,128]{1,0:T(8,128)S(1)} all-gather(f32[32,128]{1,0:T(8,128)S(1)} %convert_reduce_fusion.1), channel_id=1, replica_groups=mesh['wide_0'=16,'wide_1'=2,'narrow_0'=4,'narrow_1'=4] {'wide_1'}, dimensions={0}, use_global_device_ids=true | all-gather | bytes 49152 | tf_op jit(solution)/shard_map/cond/branch_1_fun/all_gather | solution.py:191
  42.9 0.0 copy-done.3
  42.9 2.8 %branch_1_fun.8 = (bf16[512,1024]{1,0:T(8,128)(2,1)S(1)}, bf16[512,512]{1,0:T(8,128)(2,1)}) custom-call(f32[64,128]{1,0:T(8,128)S(1)} %all_gather.17.packed, s32[2,512,128]{2,1,0:T(8,128)S(1)} %branch_1_fun.7.maps, f32[1,1024]{1,0:T(1,128)S(1)} %bitcast.31, bf16[1024,512]{1,0:T(8,128)(2,1)S(1)} %copy-done.3), custom_call_target="tpu_custom_call" | custom-call | flops 536870912 | bytes 3182592 | tf_op jit(solution)/shard_map/cond/branch_1_fun/pallas_call | solution.py:167
  45.8 6.8 %all-to-all-start.5 = ((bf16[16,32,512]{2,1,0:T(8,128)(2,1)}), bf16[16,32,512]{2,1,0:T(8,128)(2,1)S(1)}, u32[]{:S(2)}, u32[]{:S(2)}) async-start(bf16[16,32,512]{2,1,0:T(8,128)(2,1)} %bitcast.9), calls=%async_computation.5 | async-start | bytes 1048576 | tf_op jit(solution)/shard_map/cond/branch_1_fun/all_to_all | solution.py:181
  52.5 0.8 constant_dynamic-slice_fusion.3.act
  53.3 9.6 %all-to-all-done.5.recs = bf16[16,32,512]{2,1,0:T(8,128)(2,1)S(1)} async-done(((bf16[16,32,512]{2,1,0:T(8,128)(2,1)}), bf16[16,32,512]{2,1,0:T(8,128)(2,1)S(1)}, u32[]{:S(2)}, u32[]{:S(2)}) %all-to-all-start.5) | async-done | bytes 524320 | tf_op jit(solution)/shard_map/cond/branch_1_fun/all_to_all | solution.py:181
  62.9 0.2 branch_1_fun.9
  63.1 0.0 copy-start.4
  63.1 12.9 %all_to_all.33 = bf16[16,32,512]{2,1,0:T(8,128)(2,1)S(1)} all-to-all(bf16[16,32,512]{2,1,0:T(8,128)(2,1)S(1)} %branch_1_fun.9), channel_id=1, replica_groups=mesh['wide_0'=16,'wide_1'=2,'narrow_0'=4,'narrow_1'=4] {'narrow_0','narr..., dimensions={0} | all-to-all | bytes 1048576 | tf_op jit(solution)/shard_map/cond/branch_1_fun/all_to_all | solution.py:181
  76.0 0.0 copy-done.4
  76.0 2.3 %branch_1_fun.10 = f32[32,8,128]{2,1,0:T(8,128)} custom-call(bf16[512,512]{1,0:T(8,128)(2,1)S(1)} %bitcast.22, bf16[1024,512]{1,0:T(8,128)(2,1)S(1)} %copy-done.3, s32[512,128]{1,0:T(8,128)S(1)} %copy-done.4), custom_call_target="tpu_custom_call" | custom-call | flops 536870912 | bytes 1966080 | tf_op jit(solution)/shard_map/cond/branch_1_fun/pallas_call | solution.py:167
  78.3 7.4 %all-to-all-start.7 = ((f32[32,8,128]{2,1,0:T(8,128)}), f32[32,8,128]{2,1,0:T(8,128)S(1)}, u32[]{:S(2)}, u32[]{:S(2)}) async-start(f32[32,8,128]{2,1,0:T(8,128)} %branch_1_fun.10), calls=%async_computation.7 | async-start | bytes 262144 | tf_op jit(solution)/shard_map/cond/branch_1_fun/all_to_all | solution.py:181
  85.8 1.7 %fusion.5 = bf16[1024,512]{1,0:T(8,128)(2,1)} fusion(bf16[512,1024]{1,0:T(8,128)(2,1)S(1)} %get-tuple-element.48, bf16[512,512]{1,0:T(8,128)(2,1)S(1)} %bitcast.23), kind=kOutput, calls=%fused_computation.13 | convolution fusion | flops 536870912 | bytes 2621440 | tf_op jit(solution)/shard_map/cond/branch_1_fun/dot_general | solution.py:246
  87.5 14.1 %all-to-all-done.7.pieces = f32[32,8,128]{2,1,0:T(8,128)S(1)} async-done(((f32[32,8,128]{2,1,0:T(8,128)}), f32[32,8,128]{2,1,0:T(8,128)S(1)}, u32[]{:S(2)}, u32[]{:S(2)}) %all-to-all-start.7) | async-done | bytes 131104 | tf_op jit(solution)/shard_map/cond/branch_1_fun/all_to_all | solution.py:181
  101.6 0.8 branch_1_fun.11
  (3 shorter events, 0.0 us)
Async XLA Ops:
  0.6 3.8 %copy-start = (s32[512,64]{0,1:T(8,128)S(1)}, s32[512,64]{0,1:T(8,128)}, u32[]{:S(2)}) copy-start(s32[512,64]{0,1:T(8,128)} %param.13) | copy-start | bytes 393220
  3.1 1.3 %copy-start.5 = (f32[1024]{0:T(1024)S(1)}, f32[1024]{0:T(1024)}, u32[]{:S(2)}) copy-start(f32[1024]{0:T(1024)} %param.10) | copy-start | bytes 12292
  3.8 0.7 copy-start.1
  7.3 35.7 %copy-start.3 = (bf16[1024,512]{1,0:T(8,128)(2,1)S(1)}, bf16[1024,512]{1,0:T(8,128)(2,1)}, u32[]{:S(2)}) copy-start(bf16[1024,512]{1,0:T(8,128)(2,1)} %get-tuple-element.47.weight) | copy-start | bytes 3145732 | tf_op jit(solution)/shard_map/conditional
  16.5 21.7 %all-to-all-start.4 = ((bf16[16,32,128]{2,1,0:T(8,128)(2,1)}), bf16[16,32,128]{2,1,0:T(8,128)(2,1)S(1)}, u32[]{:S(2)}, u32[]{:S(2)}) async-start(bf16[16,32,128]{2,1,0:T(8,128)(2,1)} %broadcast_in_dim.27), calls=%async_computation.4 | async-start | bytes 262144 | tf_op jit(solution)/shard_map/cond/branch_1_fun/all_to_all | solution.py:181
  45.8 17.1 %all-to-all-start.5 = ((bf16[16,32,512]{2,1,0:T(8,128)(2,1)}), bf16[16,32,512]{2,1,0:T(8,128)(2,1)S(1)}, u32[]{:S(2)}, u32[]{:S(2)}) async-start(bf16[16,32,512]{2,1,0:T(8,128)(2,1)} %bitcast.9), calls=%async_computation.5 | async-start | bytes 1048576 | tf_op jit(solution)/shard_map/cond/branch_1_fun/all_to_all | solution.py:181
  63.1 12.9 %copy-start.4 = (s32[512,128]{1,0:T(8,128)S(1)}, s32[512,128]{1,0:T(8,128)}, u32[]{:S(2)}) copy-start(s32[512,128]{1,0:T(8,128)} %get-tuple-element.44.slots) | copy-start | bytes 786436 | tf_op jit(solution)/shard_map/conditional
  78.3 23.3 %all-to-all-start.7 = ((f32[32,8,128]{2,1,0:T(8,128)}), f32[32,8,128]{2,1,0:T(8,128)S(1)}, u32[]{:S(2)}, u32[]{:S(2)}) async-start(f32[32,8,128]{2,1,0:T(8,128)} %branch_1_fun.10), calls=%async_computation.7 | async-start | bytes 262144 | tf_op jit(solution)/shard_map/cond/branch_1_fun/all_to_all | solution.py:181

commit v3 on v2

v3 whole, which is shorter than its diff:
```python
import functools

import jax
import jax.numpy as jnp
from jax import lax
from jax.experimental import pallas as pl
from jax.experimental.pallas import tpu as pltpu
from jax.sharding import Mesh
from jax.sharding import PartitionSpec as P

NARROW = ("narrow_0", "narrow_1")
WIDE = ("wide_0", "wide_1")
LANES = 128
F32 = jnp.float32
BF16 = jnp.bfloat16
LIMIT = 16 * 1024 * 1024

CHUNK = 16
FEW = 16


def lookup(rows, lanes):
    return jnp.take_along_axis(rows, lanes, axis=1, mode="promise_in_bounds")


def pick_slots(rows, slots, few):
    low, high = slots & (LANES - 1), slots >> 7
    picked = jnp.zeros(slots.shape, F32)
    for c in range(rows.shape[1] // LANES):
        picked = jnp.where(high == c, lookup(rows[:, c * LANES : (c + 1) * LANES], low), picked)
    picked = picked.reshape(-1, 2, 8, LANES)
    picked = picked[:, 0] + picked[:, 1]
    return jnp.sum(picked, axis=1, keepdims=True) if few else picked


def unpack_rows(packed, few):
    if few:
        return jnp.broadcast_to(packed, (CHUNK, LANES))
    return jnp.concatenate([packed, packed], axis=0)


def place(values, maps, c, shift=None):
    lanes = (maps[c // 4] >> (8 * (c % 4))) & 255
    placed = lookup(values, (lanes - 1) & (LANES - 1))
    if shift is not None:
        placed = placed + shift
    return jnp.where(lanes > 0, placed, 0.0)


def fill_slots(few, group, width, ids, named, slots, base, most):
    lane = lax.broadcasted_iota(jnp.int32, (1, LANES), 1)
    line = lax.broadcasted_iota(jnp.int32, (LANES, LANES), 0)
    entry = lax.broadcasted_iota(jnp.int32, (FEW, LANES), 0)
    every = lax.broadcasted_iota(jnp.int32, (16, LANES), 0)
    shift = width.bit_length() - 1
    needed = jnp.zeros((16, LANES), jnp.int32)

    def up_to(counts):
        at = lax.broadcasted_iota(jnp.int32, counts.shape, 1) & (CHUNK - 1)
        for s in (1, 2, 4, 8):
            counts = counts + jnp.where(at >= s, pltpu.roll(counts, s, axis=1), 0)
        return counts

    for i in range(ids.shape[1] // LANES):
        cols = pl.ds(i * LANES, LANES)
        theirs = ids[:, cols]
        within = theirs - group * width
        mine = (within >= 0) & (within < width)
        if few:
            owner = theirs >> shift
            held = jnp.full((FEW, LANES), -1, jnp.int32)
            taken = jnp.zeros((1, LANES), jnp.int32)
            tally = jnp.zeros((16, LANES), jnp.int32)
            for k in range(ids.shape[0]):
                here = mine[k : k + 1]
                held = jnp.where(entry == jnp.where(here, taken, FEW), within[k : k + 1], held)
                taken = taken + jnp.where(here, 1, 0)
                tally = tally + jnp.where(every == owner[k : k + 1], 1, 0)
            needed = jnp.maximum(needed, jnp.maximum(tally * (LANES // FEW), up_to(tally)))
            counts = jnp.broadcast_to(taken, (8, LANES))
            first = up_to(counts) - counts
            spread = jnp.full((LANES, LANES), -1, jnp.int32)
            for k in range(FEW):
                at = jnp.where(held[k : k + 1] >= 0, first[:1] + k, -1)
                spread = jnp.where(line == at, held[k : k + 1], spread)
        else:
            held = jnp.where(mine, within, -1)
            first = jnp.broadcast_to(64 * ((lane >> 3) & 1), (8, LANES))
            spread = jnp.concatenate([held, held], axis=0)
            spread = jnp.where(line >> 6 == (lane >> 3) & 1, spread, -1)
        named[:, cols] = held
        base[:, cols] = first
        slots[cols, :] = spread.T
    most[0] = jnp.max(needed)


def maps_kernel(named, base, out):
    count, tokens = named.shape
    line = lax.broadcasted_iota(jnp.int32, (LANES, LANES), 0)
    for i in range(tokens // LANES):
        cols = pl.ds(i * LANES, LANES)
        start = base[:, cols] + lax.broadcasted_iota(jnp.int32, (8, LANES), 0) + 1

        def body(n, maps):
            first = pl.multiple_of(8 * n, 8)
            eight = named[pl.ds(first, 8), cols]
            block = eight >> 7
            code = (start + first) << (8 * (block & 3))
            low = eight & (LANES - 1)
            codes = [
                jnp.where((block >= 0) & (block < 4), code, 0),
                jnp.where((block >= 4) & (block < 8), code, 0),
            ]
            for k in range(8):
                hit = line == low[k : k + 1]
                maps = [m | jnp.where(hit, f[k : k + 1], 0) for m, f in zip(maps, codes)]
            return tuple(maps)

        zero = jnp.zeros((LANES, LANES), jnp.int32)
        maps = lax.fori_loop(0, count // 8, body, (zero, zero))
        for m in range(2):
            out[m, cols, :] = maps[m].T


def encode_kernel(few, group, ids, act, weight, packed, named, slots, base, most, act_here, weight_here, arrived):
    copies = [
        pltpu.make_async_copy(act, act_here, arrived.at[0]),
        pltpu.make_async_copy(weight, weight_here, arrived.at[1]),
    ]
    for copy in copies:
        copy.start()
    fill_slots(few, group[0], weight.shape[1], ids, named, slots, base, most)
    for copy in copies:
        copy.wait()
    step = 8 * CHUNK
    for i in range(act.shape[0] // step):
        rows = pl.ds(i * step, step)
        part = jnp.dot(act_here[rows, :], weight_here[...], preferred_element_type=F32)
        picked = pick_slots(part, slots[rows, :], few)
        depth = 8 * picked.shape[1]
        packed[pl.ds(i * depth, depth), :] = picked.reshape(depth, LANES)


def decode_kernel(few, packed, maps, bias, weight, latents, rec):
    step = 8 * CHUNK
    depth = 1 if few else 8
    for i in range(latents.shape[0] // step):
        rows = pl.ds(i * step, step)
        chunks = [unpack_rows(packed[pl.ds((8 * i + q) * depth, depth), :], few) for q in range(8)]
        values = jnp.concatenate(chunks, axis=0)
        mine = [maps[0, rows, :], maps[1, rows, :]]
        for c in range(latents.shape[1] // LANES):
            cols = pl.ds(c * LANES, LANES)
            latents[rows, cols] = place(values, mine, c, bias[:, cols]).astype(BF16)
        rec[rows, :] = jnp.dot(latents[rows, :], weight[...], preferred_element_type=F32).astype(rec.dtype)


def mix_kernel(recs, act, bias, out):
    groups = recs.shape[0]
    for r in range(0, recs.shape[1], 16):
        for c in range(0, recs.shape[2], LANES):
            at = (pl.ds(r, 16), pl.ds(c, LANES))
            err = bias[:, pl.ds(c, LANES)] - act[at].astype(F32)
            errs = []
            for g in range(groups):
                err = err + recs[(g, *at)].astype(F32)
                errs.append(err)
            suffix = jnp.zeros_like(err)
            for g in reversed(range(groups)):
                suffix = suffix + errs[g]
                out[(g, *at)] = (suffix * (1.0 / groups)).astype(out.dtype)


def grad_kernel(few, back, weight, slots, out):
    step = 8 * CHUNK
    for i in range(back.shape[0] // step):
        rows = pl.ds(i * step, step)
        part = lax.dot_general(back[rows, :], weight[...], (((1,), (1,)), ((), ())), preferred_element_type=F32)
        out[pl.ds(8 * i, 8)] = pick_slots(part, slots[rows, :], few)


def own_kernel(few, pieces, maps, out):
    values = unpack_rows(jnp.sum(pieces[...], axis=0), few)
    mine = [maps[0], maps[1]]
    for c in range(out.shape[1] // LANES):
        out[:, pl.ds(c * LANES, LANES)] = place(values, mine, c)


def call(kernel, shapes, flops, *args, **params):
    moved = sum(a.size * a.dtype.itemsize for a in (*args, *jax.tree.leaves(shapes)))
    return pl.pallas_call(
        kernel,
        out_shape=shapes,
        compiler_params=pltpu.CompilerParams(vmem_limit_bytes=LIMIT),
        cost_estimate=pl.CostEstimate(flops=flops, bytes_accessed=moved, transcendentals=0),
        **params,
    )(*args)


def array(shape, dtype):
    return jax.ShapeDtypeStruct(shape, dtype)


def swap(pieces, axes):
    return lax.all_to_all(pieces, axes, 0, 0)


def summed_over_wide(partial):
    ring, core = WIDE
    rows = partial.shape[0] // 2
    both = lax.all_gather(partial, core)
    half = lax.dynamic_slice_in_dim(both, lax.axis_index(core) * rows, rows, 1)
    half = (half[0] + half[1]).astype(BF16)
    pieces = swap(jnp.broadcast_to(half[None], (lax.axis_size(ring), *half.shape)), ring)
    return lax.all_gather(jnp.sum(pieces.astype(F32), axis=0), core, tiled=True)


def encode(few, group, ids, activations, enc_weight):
    tokens, channels = activations.shape
    width = enc_weight.shape[1]
    depth = tokens // CHUNK * (1 if few else 8)
    vmem, smem = (pl.BlockSpec(memory_space=m) for m in (pltpu.VMEM, pltpu.SMEM))
    partial, named, slots, base, most = call(
        functools.partial(encode_kernel, few),
        (
            array((depth, LANES), F32),
            array((FEW if few else ids.shape[0], tokens), jnp.int32),
            array((tokens, LANES), jnp.int32),
            array((8, tokens), jnp.int32),
            array((1,), jnp.int32),
        ),
        2 * tokens * channels * width,
        group,
        ids,
        activations,
        enc_weight,
        in_specs=[smem, vmem, pl.BlockSpec(memory_space=pl.ANY), pl.BlockSpec(memory_space=pl.ANY)],
        out_specs=(vmem, vmem, vmem, vmem, smem),
        scratch_shapes=[
            pltpu.VMEM(activations.shape, BF16),
            pltpu.VMEM(enc_weight.shape, BF16),
            pltpu.SemaphoreType.DMA((2,)),
        ],
    )
    maps = call(maps_kernel, array((2, tokens, LANES), jnp.int32), 1 << 26, named, base)
    return summed_over_wide(partial), slots, maps, most[0]


def decode(few, preact, slots, maps, activations, enc_bias, dec_weight, dec_bias):
    tokens, channels = activations.shape
    width = dec_weight.shape[0]
    groups, wide = lax.axis_size(NARROW), lax.axis_size(WIDE)
    group = lax.axis_index(NARROW)
    work = 2 * tokens * channels * width
    latents, rec = call(
        functools.partial(decode_kernel, few),
        (array((tokens, width), BF16), array((tokens, channels), BF16)),
        work,
        preact,
        maps,
        enc_bias[None],
        dec_weight,
    )
    rows = tokens // groups
    recs = swap(rec.reshape(groups, rows, channels), NARROW)
    act_rows = lax.dynamic_slice_in_dim(activations, group * rows, rows, 0)
    mixed = call(mix_kernel, array(recs.shape, BF16), 8 * recs.size, recs, act_rows, dec_bias[None])
    back = swap(mixed, NARROW).reshape(tokens, channels)
    grads = call(
        functools.partial(grad_kernel, few),
        array((wide, 1 if few else 8, LANES), F32),
        work,
        back,
        dec_weight,
        slots,
    )
    parts = swap(grads, WIDE)
    dec_grad = lax.dot_general(
        latents, back, (((0,), (0,)), ((), ())), preferred_element_type=F32
    ).astype(BF16)
    own_rows = tokens // wide
    own_maps = lax.dynamic_slice_in_dim(maps, lax.axis_index(WIDE) * own_rows, own_rows, 1)
    latent_grad = call(
        functools.partial(own_kernel, few), array((own_rows, width), F32), 1 << 20, parts, own_maps
    )
    return dec_grad, latent_grad


def local(activations, enc_weight, enc_bias, dec_weight, dec_bias, active_ids):
    group = lax.axis_index(NARROW)[None]
    ids = active_ids.T
    rest = (activations, enc_bias, dec_weight, dec_bias)
    preact, slots, maps, needed = encode(True, group, ids, activations, enc_weight)

    def few():
        return decode(True, preact, slots, maps, *rest)

    def many():
        preact, slots, maps, _ = encode(False, group, ids, activations, enc_weight)
        return decode(False, preact, slots, maps, *rest)

    return lax.cond(needed <= LANES, few, many)


def solution(mesh):
    split = Mesh(mesh.devices.reshape(16, 2, 4, 4), ("wide_0", "wide_1", "narrow_0", "narrow_1"))
    return jax.shard_map(
        local,
        mesh=split,
        in_specs=(P(None, WIDE), P(WIDE, NARROW), P(NARROW), P(NARROW, WIDE), P(WIDE), P()),
        out_specs=(P(NARROW, WIDE), P(WIDE, NARROW)),
        check_vma=False,
    )
```

time: 103 us -> 97.8 us (0.950)
  blocking collectives: 26.1 us -> 12 us
  waiting for transfers between devices: 34.5 us -> 39.3 us
  starting transfers between devices: 23.7 us -> 26.9 us
  Pallas kernels: 12.8 us -> 14.5 us
    all_to_all x1 -> x0, blocking collectives: 12.9 us -> none  [swap(): return lax.all_to_all(pieces, axes, 0, 0)]
    all_to_all x3 -> x4, waiting for transfers between devices: 34.5 us -> 39.3 us  [swap(): return lax.all_to_all(pieces, axes, 0, 0)]
    all_to_all x3 -> x4, starting transfers between devices: 23.7 us -> 26.9 us  [swap(): return lax.all_to_all(pieces, axes, 0, 0)]
    pallas_call x7 -> x6, Pallas kernels: 12.8 us -> 14.5 us  [call(): pl.pallas_call(kernel, out_shape=shapes, compiler_params=pltpu.CompilerPa...]
    all_gather x1, blocking collectives: 4.73 us -> 3.53 us  [summed_over_wide(): return lax.all_gather(jnp.sum(pieces.astype(F32), axis=0), core, tiled=True)]
  transfers between devices with their start and end apart: 3 -> 4, of which waited for: 3 -> 4; matrix products, arithmetic and copies ran while one was open for 2% -> 2% of each run, Pallas kernels for 1% -> 1%
where the time goes in v3:
time: 97.8 us; the launch traced here: 97.2 us
  waiting for transfers between devices  39.3 us (40%)
  starting transfers between devices  26.9 us (28%)
  Pallas kernels  14.5 us (15%)
  blocking collectives  12 us (12%)
  matrix products  1.72 us (2%)
  between operations  1.36 us (1%)
  local copies, waits for them, and re-layouts  1.35 us (1%)
    all_to_all x4, waiting for transfers between devices, swap(): return lax.all_to_all(pieces, axes, 0, 0)  39.3 us
    all_to_all x4, starting transfers between devices, swap(): return lax.all_to_all(pieces, axes, 0, 0)  26.9 us
    pallas_call x6, Pallas kernels, call(): pl.pallas_call(kernel, out_shape=shapes, compiler_params=pltpu.CompilerPa...  14.5 us
    all_gather x1, blocking collectives, summed_over_wide(): both = lax.all_gather(partial, core)  8.5 us
    all_gather x1, blocking collectives, summed_over_wide(): return lax.all_gather(jnp.sum(pieces.astype(F32), axis=0), core, tiled=True)  3.53 us
  transfers between devices with their start and end apart: 4, of which 4 were waited for; matrix products, arithmetic and copies ran while one was open for 2% of the time, Pallas kernels for 1%

profile of v3, /device:TPU:1, one launch (start us, length us, event | category | flops | bytes accessed | tf_op | source)
XLA Modules:
  0.0 97.2 jit_solution(8556065880747925233)
XLA Ops:
  0.6 0.0 copy-start.2
  0.6 5.0 %shard_map.77 = (f32[32,128]{1,0:T(8,128)S(1)}, s32[16,512]{1,0:T(8,128)S(1)}, s32[512,128]{1,0:T(8,128)S(1)}, s32[8,512]{1,0:T(8,128)S(1)}, s32[1]{0:T(128)}) custom-call(s32[1]{0:T(128)} %bitcast.10.group, s32[64,512]{1,0:T(8,128)} %bitcast.29, bf16[512,512]{1,0:T(8,128)(2,1)} %act.1, bf16[512,1024]{1,0:T(8,128)(2,1)} %weight.1), custom_call_target="tpu_custom_call" | custom-call | flops 536870912 | bytes 2031624 | tf_op jit(solution)/shard_map/pallas_call | solution.py:191
  5.7 0.0 copy-start.1
  5.7 8.5 %all-gather.1 = f32[64,128]{1,0:T(8,128)S(1)} all-gather(f32[32,128]{1,0:T(8,128)S(1)} %get-tuple-element.63), channel_id=3, replica_groups=mesh['wide_0'=16,'wide_1'=2,'narrow_0'=4,'narrow_1'=4] {'wide_1'}, dimensions={0}, use_global_device_ids=true | all-gather | bytes 49152 | tf_op jit(solution)/shard_map/all_gather | solution.py:211
  14.2 0.6 broadcast_in_dim.33
  14.9 9.5 %all-to-all-start.7 = ((bf16[16,16,128]{2,1,0:T(8,128)(2,1)}), bf16[16,16,128]{2,1,0:T(8,128)(2,1)S(1)}, u32[]{:S(2)}, u32[]{:S(2)}) async-start(bf16[16,16,128]{2,1,0:T(8,128)(2,1)} %broadcast_in_dim.33), calls=%async_computation.7 | async-start | bytes 131072 | tf_op jit(solution)/shard_map/all_to_all | solution.py:205
  25.0 0.0 copy-start.5
  25.1 1.3 %shard_map.78 = s32[2,512,128]{2,1,0:T(8,128)S(1)} custom-call(s32[16,512]{1,0:T(8,128)S(1)} %get-tuple-element.64.named, s32[8,512]{1,0:T(8,128)S(1)} %get-tuple-element.65.base), custom_call_target="tpu_custom_call" | custom-call | flops 67108864 | bytes 573440 | tf_op jit(solution)/shard_map/pallas_call | solution.py:191
  26.4 9.7 %all-to-all-done.7 = bf16[16,16,128]{2,1,0:T(8,128)(2,1)S(1)} async-done(((bf16[16,16,128]{2,1,0:T(8,128)(2,1)}), bf16[16,16,128]{2,1,0:T(8,128)(2,1)S(1)}, u32[]{:S(2)}, u32[]{:S(2)}) %all-to-all-start.7) | async-done | bytes 65568 | tf_op jit(solution)/shard_map/all_to_all | solution.py:205
  36.1 0.0 copy-start.6
  36.1 3.5 %all_gather.20 = f32[32,128]{1,0:T(8,128)S(1)} all-gather(f32[16,128]{1,0:T(8,128)S(1)} %convert_reduce_fusion.1), channel_id=1, replica_groups=mesh['wide_0'=16,'wide_1'=2,'narrow_0'=4,'narrow_1'=4] {'wide_1'}, dimensions={0}, use_global_device_ids=true | all-gather | bytes 24576 | tf_op jit(solution)/shard_map/all_gather | solution.py:215
  39.6 0.0 copy-start
  39.7 0.0 copy-done.2
  39.7 0.0 copy-done.1
  39.7 0.0 copy-done.5
  39.7 0.0 copy-done.6
  39.7 0.7 copy-done
  40.3 56.9 %conditional.2 = (bf16[1024,512]{1,0:T(8,128)(2,1)}, f32[16,1024]{1,0:T(8,128)}) conditional(s32[]{:T(128)} %bitcast.12, (s32[1]{0:T(128)}, s32[64,512]{1,0:T(8,128)S(1)}, bf16[512,512]{1,0:T(8,128)(2,1)S(1)}, bf16[512,1024]{1,0:T(8,128)(2,1)S(1)}, f32[1024]{0:T(1024)S(1)}, /*index=5*/bf16[1024,512]{1,0:T(8,128)(2,1)}, f32[512]{0:T(512)S(1)}) %tuple.30, ...), branch_computations={%region_1.0_spmd, %region_3.0_spmd} | conditional | flops 2218278912 | bytes 22862300
  40.3 4.1 %branch_1_fun.4 = (bf16[512,1024]{1,0:T(8,128)(2,1)S(1)}, bf16[512,512]{1,0:T(8,128)(2,1)}) custom-call(f32[32,128]{1,0:T(8,128)S(1)} %get-tuple-element.44.packed, s32[2,512,128]{2,1,0:T(8,128)S(1)} %get-tuple-element.45.maps, f32[1,1024]{1,0:T(1,128)S(1)} %bitcast.32, bf16[1024,512]{1,0:T(8,128)(2,1)} %get-tuple-element.47.weight), custom_call_target="tpu_custom_call" | custom-call | flops 536870912 | bytes 3166208 | tf_op jit(solution)/shard_map/cond/branch_1_fun/pallas_call | solution.py:191
  44.4 6.8 %all-to-all-start.4 = ((bf16[16,32,512]{2,1,0:T(8,128)(2,1)}), bf16[16,32,512]{2,1,0:T(8,128)(2,1)S(1)}, u32[]{:S(2)}, u32[]{:S(2)}) async-start(bf16[16,32,512]{2,1,0:T(8,128)(2,1)} %bitcast.7), calls=%async_computation.4 | async-start | bytes 1048576 | tf_op jit(solution)/shard_map/cond/branch_1_fun/all_to_all | solution.py:205
  51.2 10.4 %all-to-all-done.4.recs = bf16[16,32,512]{2,1,0:T(8,128)(2,1)S(1)} async-done(((bf16[16,32,512]{2,1,0:T(8,128)(2,1)}), bf16[16,32,512]{2,1,0:T(8,128)(2,1)S(1)}, u32[]{:S(2)}, u32[]{:S(2)}) %all-to-all-start.4) | async-done | bytes 524320 | tf_op jit(solution)/shard_map/cond/branch_1_fun/all_to_all | solution.py:205
  61.5 1.0 %branch_1_fun.5 = bf16[16,32,512]{2,1,0:T(8,128)(2,1)} custom-call(bf16[16,32,512]{2,1,0:T(8,128)(2,1)S(1)} %all-to-all-done.4.recs, bf16[32,512]{1,0:T(8,128)(2,1)S(1)} %constant_dynamic-slice_fusion.3.act, f32[1,512]{1,0:T(1,128)S(1)} %bitcast.28), custom_call_target="tpu_custom_call" | custom-call | flops 2097152 | bytes 1083392 | tf_op jit(solution)/shard_map/cond/branch_1_fun/pallas_call | solution.py:191
  62.5 0.0 copy-start.4
  62.5 3.9 %all-to-all-start.5 = ((bf16[16,32,512]{2,1,0:T(8,128)(2,1)}), bf16[16,32,512]{2,1,0:T(8,128)(2,1)S(1)}, u32[]{:S(2)}, u32[]{:S(2)}) async-start(bf16[16,32,512]{2,1,0:T(8,128)(2,1)} %branch_1_fun.5), calls=%async_computation.5 | async-start | bytes 1048576 | tf_op jit(solution)/shard_map/cond/branch_1_fun/all_to_all | solution.py:205
  66.5 9.2 %all-to-all-done.5 = bf16[16,32,512]{2,1,0:T(8,128)(2,1)S(1)} async-done(((bf16[16,32,512]{2,1,0:T(8,128)(2,1)}), bf16[16,32,512]{2,1,0:T(8,128)(2,1)S(1)}, u32[]{:S(2)}, u32[]{:S(2)}) %all-to-all-start.5) | async-done | bytes 524320 | tf_op jit(solution)/shard_map/cond/branch_1_fun/all_to_all | solution.py:205
  75.6 0.0 copy-done.4
  75.6 2.3 %branch_1_fun.6 = f32[32,1,128]{2,1,0:T(1,128)} custom-call(bf16[512,512]{1,0:T(8,128)(2,1)S(1)} %bitcast.21, bf16[1024,512]{1,0:T(8,128)(2,1)S(1)} %copy-done.4, s32[512,128]{1,0:T(8,128)S(1)} %get-tuple-element.52.slots), custom_call_target="tpu_custom_call" | custom-call | flops 536870912 | bytes 1851392 | tf_op jit(solution)/shard_map/cond/branch_1_fun/pallas_call | solution.py:191
  77.9 6.7 %all-to-all-start.6 = ((f32[32,1,128]{2,1,0:T(1,128)}), f32[32,1,128]{2,1,0:T(1,128)S(1)}, u32[]{:S(2)}, u32[]{:S(2)}) async-start(f32[32,1,128]{2,1,0:T(1,128)} %branch_1_fun.6), calls=%async_computation.6 | async-start | bytes 32768 | tf_op jit(solution)/shard_map/cond/branch_1_fun/all_to_all | solution.py:205
  84.7 1.7 %fusion.5 = bf16[1024,512]{1,0:T(8,128)(2,1)} fusion(bf16[512,1024]{1,0:T(8,128)(2,1)S(1)} %get-tuple-element.48, bf16[512,512]{1,0:T(8,128)(2,1)S(1)} %bitcast.22), kind=kOutput, calls=%fused_computation.13 | convolution fusion | flops 536870912 | bytes 2621440 | tf_op jit(solution)/shard_map/cond/branch_1_fun/dot_general | solution.py:278
  86.4 10.1 %all-to-all-done.6.pieces = f32[32,1,128]{2,1,0:T(1,128)S(1)} async-done(((f32[32,1,128]{2,1,0:T(1,128)}), f32[32,1,128]{2,1,0:T(1,128)S(1)}, u32[]{:S(2)}, u32[]{:S(2)}) %all-to-all-start.6) | async-done | bytes 16416 | tf_op jit(solution)/shard_map/cond/branch_1_fun/all_to_all | solution.py:205
  96.5 0.8 branch_1_fun.7
  (4 shorter events, 0.0 us)
Async XLA Ops:
  0.6 39.0 %copy-start.2 = (bf16[512,1024]{1,0:T(8,128)(2,1)S(1)}, bf16[512,1024]{1,0:T(8,128)(2,1)}, u32[]{:S(2)}) copy-start(bf16[512,1024]{1,0:T(8,128)(2,1)} %weight.1) | copy-start | bytes 3145732
  5.7 34.0 %copy-start.1 = (bf16[512,512]{1,0:T(8,128)(2,1)S(1)}, bf16[512,512]{1,0:T(8,128)(2,1)}, u32[]{:S(2)}) copy-start(bf16[512,512]{1,0:T(8,128)(2,1)} %act.1) | copy-start | bytes 1572868
  14.9 21.2 %all-to-all-start.7 = ((bf16[16,16,128]{2,1,0:T(8,128)(2,1)}), bf16[16,16,128]{2,1,0:T(8,128)(2,1)S(1)}, u32[]{:S(2)}, u32[]{:S(2)}) async-start(bf16[16,16,128]{2,1,0:T(8,128)(2,1)} %broadcast_in_dim.33), calls=%async_computation.7 | async-start | bytes 131072 | tf_op jit(solution)/shard_map/all_to_all | solution.py:205
  25.0 14.6 %copy-start.5 = (s32[512,64]{0,1:T(8,128)S(1)}, s32[512,64]{0,1:T(8,128)}, u32[]{:S(2)}) copy-start(s32[512,64]{0,1:T(8,128)} %param.13) | copy-start | bytes 393220
  36.1 3.6 %copy-start.6 = (f32[1024]{0:T(1024)S(1)}, f32[1024]{0:T(1024)}, u32[]{:S(2)}) copy-start(f32[1024]{0:T(1024)} %param.10) | copy-start | bytes 12292
  39.6 0.7 copy-start
  44.4 17.1 %all-to-all-start.4 = ((bf16[16,32,512]{2,1,0:T(8,128)(2,1)}), bf16[16,32,512]{2,1,0:T(8,128)(2,1)S(1)}, u32[]{:S(2)}, u32[]{:S(2)}) async-start(bf16[16,32,512]{2,1,0:T(8,128)(2,1)} %bitcast.7), calls=%async_computation.4 | async-start | bytes 1048576 | tf_op jit(solution)/shard_map/cond/branch_1_fun/all_to_all | solution.py:205
  62.5 13.1 %copy-start.4 = (bf16[1024,512]{1,0:T(8,128)(2,1)S(1)}, bf16[1024,512]{1,0:T(8,128)(2,1)}, u32[]{:S(2)}) copy-start(bf16[1024,512]{1,0:T(8,128)(2,1)} %get-tuple-element.47.weight) | copy-start | bytes 3145732 | tf_op jit(solution)/shard_map/conditional
  62.5 13.1 %all-to-all-start.5 = ((bf16[16,32,512]{2,1,0:T(8,128)(2,1)}), bf16[16,32,512]{2,1,0:T(8,128)(2,1)S(1)}, u32[]{:S(2)}, u32[]{:S(2)}) async-start(bf16[16,32,512]{2,1,0:T(8,128)(2,1)} %branch_1_fun.5), calls=%async_computation.5 | async-start | bytes 1048576 | tf_op jit(solution)/shard_map/cond/branch_1_fun/all_to_all | solution.py:205
  77.9 18.5 %all-to-all-start.6 = ((f32[32,1,128]{2,1,0:T(1,128)}), f32[32,1,128]{2,1,0:T(1,128)S(1)}, u32[]{:S(2)}, u32[]{:S(2)}) async-start(f32[32,1,128]{2,1,0:T(1,128)} %branch_1_fun.6), calls=%async_computation.6 | async-start | bytes 32768 | tf_op jit(solution)/shard_map/cond/branch_1_fun/all_to_all | solution.py:205

commit v4 on v3

--- a/solution.py
+++ b/solution.py
@@ -176,7 +176,8 @@
     for i in range(back.shape[0] // step):
         rows = pl.ds(i * step, step)
         part = lax.dot_general(back[rows, :], weight[...], (((1,), (1,)), ((), ())), preferred_element_type=F32)
-        out[pl.ds(8 * i, 8)] = pick_slots(part, slots[rows, :], few)
+        first = (8 * i + out.shape[0] // 2) % out.shape[0]
+        out[pl.ds(first, 8)] = pick_slots(part, slots[rows, :], few)
 
 
 def own_kernel(few, pieces, maps, out):
@@ -205,13 +206,19 @@
     return lax.all_to_all(pieces, axes, 0, 0)
 
 
+def swap_from_half(pieces, axes):
+    size = lax.axis_size(axes)
+    order = [[(i + size // 2) % size for i in range(size)]]
+    return lax.all_to_all(pieces, axes, 0, 0, axis_index_groups=order)
+
+
 def summed_over_wide(partial):
     ring, core = WIDE
     rows = partial.shape[0] // 2
     both = lax.all_gather(partial, core)
     half = lax.dynamic_slice_in_dim(both, lax.axis_index(core) * rows, rows, 1)
     half = (half[0] + half[1]).astype(BF16)
-    pieces = swap(jnp.broadcast_to(half[None], (lax.axis_size(ring), *half.shape)), ring)
+    pieces = swap_from_half(jnp.broadcast_to(half[None], (lax.axis_size(ring), *half.shape)), ring)
     return lax.all_gather(jnp.sum(pieces.astype(F32), axis=0), core, tiled=True)
 
 
@@ -274,7 +281,7 @@
         dec_weight,
         slots,
     )
-    parts = swap(grads, WIDE)
+    parts = swap_from_half(grads, WIDE)
     dec_grad = lax.dot_general(
         latents, back, (((0,), (0,)), ((), ())), preferred_element_type=F32
     ).astype(BF16)

time: 97.8 us -> 91.6 us (0.937)
  waiting for transfers between devices: 39.3 us -> 21.9 us
  starting transfers between devices: 26.9 us -> 39.2 us
  blocking collectives: 12 us -> 10.8 us
    all_to_all x0 -> x2, starting transfers between devices: none -> 28.6 us  [swap_from_half(): return lax.all_to_all(pieces, axes, 0, 0, axis_index_groups=order)]
    all_to_all x4 -> x2, waiting for transfers between devices: 39.3 us -> 19.5 us  [swap(): return lax.all_to_all(pieces, axes, 0, 0)]
    all_to_all x4 -> x2, starting transfers between devices: 26.9 us -> 10.7 us  [swap(): return lax.all_to_all(pieces, axes, 0, 0)]
    all_to_all x0 -> x2, waiting for transfers between devices: none -> 2.4 us  [swap_from_half(): return lax.all_to_all(pieces, axes, 0, 0, axis_index_groups=order)]
    all_gather x1, blocking collectives: 3.53 us -> 2.34 us  [summed_over_wide(): return lax.all_gather(jnp.sum(pieces.astype(F32), axis=0), core, tiled=True)]
where the time goes in v4:
time: 91.6 us; the launch traced here: 91 us
  starting transfers between devices  39.2 us (43%)
  waiting for transfers between devices  21.9 us (24%)
  Pallas kernels  14.5 us (16%)
  blocking collectives  10.8 us (12%)
  matrix products  1.72 us (2%)
  between operations  1.36 us (1%)
  local copies, waits for them, and re-layouts  1.35 us (1%)
    all_to_all x2, starting transfers between devices, swap_from_half(): return lax.all_to_all(pieces, axes, 0, 0, axis_index_groups=order)  28.6 us
    all_to_all x2, waiting for transfers between devices, swap(): return lax.all_to_all(pieces, axes, 0, 0)  19.5 us
    pallas_call x6, Pallas kernels, call(): pl.pallas_call(kernel, out_shape=shapes, compiler_params=pltpu.CompilerPa...  14.5 us
    all_to_all x2, starting transfers between devices, swap(): return lax.all_to_all(pieces, axes, 0, 0)  10.7 us
    all_gather x1, blocking collectives, summed_over_wide(): both = lax.all_gather(partial, core)  8.5 us
    all_to_all x2, waiting for transfers between devices, swap_from_half(): return lax.all_to_all(pieces, axes, 0, 0, axis_index_groups=order)  2.4 us
    all_gather x1, blocking collectives, summed_over_wide(): return lax.all_gather(jnp.sum(pieces.astype(F32), axis=0), core, tiled=True)  2.34 us
  transfers between devices with their start and end apart: 4, of which 4 were waited for; matrix products, arithmetic and copies ran while one was open for 2% of the time, Pallas kernels for 1%

profile of v4, /device:TPU:1, one launch (start us, length us, event | category | flops | bytes accessed | tf_op | source)
XLA Modules:
  0.0 91.0 jit_solution(5386287496306201550)
XLA Ops:
  0.6 0.0 copy-start.2
  0.6 5.0 %shard_map.77 = (f32[32,128]{1,0:T(8,128)S(1)}, s32[16,512]{1,0:T(8,128)S(1)}, s32[512,128]{1,0:T(8,128)S(1)}, s32[8,512]{1,0:T(8,128)S(1)}, s32[1]{0:T(128)}) custom-call(s32[1]{0:T(128)} %bitcast.10.group, s32[64,512]{1,0:T(8,128)} %bitcast.29, bf16[512,512]{1,0:T(8,128)(2,1)} %act.1, bf16[512,1024]{1,0:T(8,128)(2,1)} %weight.1), custom_call_target="tpu_custom_call" | custom-call | flops 536870912 | bytes 2031624 | tf_op jit(solution)/shard_map/pallas_call | solution.py:192
  5.7 0.0 copy-start.1
  5.7 8.5 %all-gather.1 = f32[64,128]{1,0:T(8,128)S(1)} all-gather(f32[32,128]{1,0:T(8,128)S(1)} %get-tuple-element.63), channel_id=3, replica_groups=mesh['wide_0'=16,'wide_1'=2,'narrow_0'=4,'narrow_1'=4] {'wide_1'}, dimensions={0}, use_global_device_ids=true | all-gather | bytes 49152 | tf_op jit(solution)/shard_map/all_gather | solution.py:218
  14.2 0.6 broadcast_in_dim.33
  14.9 12.9 %all-to-all-start.7 = ((bf16[16,16,128]{2,1,0:T(8,128)(2,1)}), bf16[16,16,128]{2,1,0:T(8,128)(2,1)S(1)}, u32[]{:S(2)}, u32[]{:S(2)}) async-start(bf16[16,16,128]{2,1,0:T(8,128)(2,1)} %broadcast_in_dim.33), calls=%async_computation.7 | async-start | bytes 131072 | tf_op jit(solution)/shard_map/all_to_all | solution.py:212
  28.4 0.0 copy-start.5
  28.4 1.3 %shard_map.78 = s32[2,512,128]{2,1,0:T(8,128)S(1)} custom-call(s32[16,512]{1,0:T(8,128)S(1)} %get-tuple-element.64.named, s32[8,512]{1,0:T(8,128)S(1)} %get-tuple-element.65.base), custom_call_target="tpu_custom_call" | custom-call | flops 67108864 | bytes 573440 | tf_op jit(solution)/shard_map/pallas_call | solution.py:192
  29.8 2.1 %all-to-all-done.7 = bf16[16,16,128]{2,1,0:T(8,128)(2,1)S(1)} async-done(((bf16[16,16,128]{2,1,0:T(8,128)(2,1)}), bf16[16,16,128]{2,1,0:T(8,128)(2,1)S(1)}, u32[]{:S(2)}, u32[]{:S(2)}) %all-to-all-start.7) | async-done | bytes 65568 | tf_op jit(solution)/shard_map/all_to_all | solution.py:212
  31.9 0.0 copy-start.6
  31.9 2.3 %all_gather.20 = f32[32,128]{1,0:T(8,128)S(1)} all-gather(f32[16,128]{1,0:T(8,128)S(1)} %convert_reduce_fusion.1), channel_id=1, replica_groups=mesh['wide_0'=16,'wide_1'=2,'narrow_0'=4,'narrow_1'=4] {'wide_1'}, dimensions={0}, use_global_device_ids=true | all-gather | bytes 24576 | tf_op jit(solution)/shard_map/all_gather | solution.py:222
  34.2 0.0 copy-start
  34.2 0.0 copy-done.2
  34.2 0.0 copy-done.1
  34.2 0.0 copy-done.5
  34.2 0.0 copy-done.6
  34.3 0.7 copy-done
  34.9 56.1 %conditional.2 = (bf16[1024,512]{1,0:T(8,128)(2,1)}, f32[16,1024]{1,0:T(8,128)}) conditional(s32[]{:T(128)} %bitcast.12, (s32[1]{0:T(128)}, s32[64,512]{1,0:T(8,128)S(1)}, bf16[512,512]{1,0:T(8,128)(2,1)S(1)}, bf16[512,1024]{1,0:T(8,128)(2,1)S(1)}, f32[1024]{0:T(1024)S(1)}, /*index=5*/bf16[1024,512]{1,0:T(8,128)(2,1)}, f32[512]{0:T(512)S(1)}) %tuple.30, ...), branch_computations={%region_1.0_spmd, %region_3.0_spmd} | conditional | flops 2218278912 | bytes 22862300
  34.9 4.1 %branch_1_fun.4 = (bf16[512,1024]{1,0:T(8,128)(2,1)S(1)}, bf16[512,512]{1,0:T(8,128)(2,1)}) custom-call(f32[32,128]{1,0:T(8,128)S(1)} %get-tuple-element.44.packed, s32[2,512,128]{2,1,0:T(8,128)S(1)} %get-tuple-element.45.maps, f32[1,1024]{1,0:T(1,128)S(1)} %bitcast.32, bf16[1024,512]{1,0:T(8,128)(2,1)} %get-tuple-element.47.weight), custom_call_target="tpu_custom_call" | custom-call | flops 536870912 | bytes 3166208 | tf_op jit(solution)/shard_map/cond/branch_1_fun/pallas_call | solution.py:192
  39.0 6.8 %all-to-all-start.4 = ((bf16[16,32,512]{2,1,0:T(8,128)(2,1)}), bf16[16,32,512]{2,1,0:T(8,128)(2,1)S(1)}, u32[]{:S(2)}, u32[]{:S(2)}) async-start(bf16[16,32,512]{2,1,0:T(8,128)(2,1)} %bitcast.7), calls=%async_computation.4 | async-start | bytes 1048576 | tf_op jit(solution)/shard_map/cond/branch_1_fun/all_to_all | solution.py:206
  45.8 10.4 %all-to-all-done.4.recs = bf16[16,32,512]{2,1,0:T(8,128)(2,1)S(1)} async-done(((bf16[16,32,512]{2,1,0:T(8,128)(2,1)}), bf16[16,32,512]{2,1,0:T(8,128)(2,1)S(1)}, u32[]{:S(2)}, u32[]{:S(2)}) %all-to-all-start.4) | async-done | bytes 524320 | tf_op jit(solution)/shard_map/cond/branch_1_fun/all_to_all | solution.py:206
  56.1 1.0 %branch_1_fun.5 = bf16[16,32,512]{2,1,0:T(8,128)(2,1)} custom-call(bf16[16,32,512]{2,1,0:T(8,128)(2,1)S(1)} %all-to-all-done.4.recs, bf16[32,512]{1,0:T(8,128)(2,1)S(1)} %constant_dynamic-slice_fusion.3.act, f32[1,512]{1,0:T(1,128)S(1)} %bitcast.28), custom_call_target="tpu_custom_call" | custom-call | flops 2097152 | bytes 1083392 | tf_op jit(solution)/shard_map/cond/branch_1_fun/pallas_call | solution.py:192
  57.1 0.0 copy-start.4
  57.1 3.9 %all-to-all-start.5 = ((bf16[16,32,512]{2,1,0:T(8,128)(2,1)}), bf16[16,32,512]{2,1,0:T(8,128)(2,1)S(1)}, u32[]{:S(2)}, u32[]{:S(2)}) async-start(bf16[16,32,512]{2,1,0:T(8,128)(2,1)} %branch_1_fun.5), calls=%async_computation.5 | async-start | bytes 1048576 | tf_op jit(solution)/shard_map/cond/branch_1_fun/all_to_all | solution.py:206
  61.0 9.2 %all-to-all-done.5 = bf16[16,32,512]{2,1,0:T(8,128)(2,1)S(1)} async-done(((bf16[16,32,512]{2,1,0:T(8,128)(2,1)}), bf16[16,32,512]{2,1,0:T(8,128)(2,1)S(1)}, u32[]{:S(2)}, u32[]{:S(2)}) %all-to-all-start.5) | async-done | bytes 524320 | tf_op jit(solution)/shard_map/cond/branch_1_fun/all_to_all | solution.py:206
  70.2 0.0 copy-done.4
  70.2 2.3 %branch_1_fun.6 = f32[32,1,128]{2,1,0:T(1,128)} custom-call(bf16[512,512]{1,0:T(8,128)(2,1)S(1)} %bitcast.21, bf16[1024,512]{1,0:T(8,128)(2,1)S(1)} %copy-done.4, s32[512,128]{1,0:T(8,128)S(1)} %get-tuple-element.52.slots), custom_call_target="tpu_custom_call" | custom-call | flops 536870912 | bytes 1851392 | tf_op jit(solution)/shard_map/cond/branch_1_fun/pallas_call | solution.py:192
  72.5 15.6 %all-to-all-start.6 = ((f32[32,1,128]{2,1,0:T(1,128)}), f32[32,1,128]{2,1,0:T(1,128)S(1)}, u32[]{:S(2)}, u32[]{:S(2)}) async-start(f32[32,1,128]{2,1,0:T(1,128)} %branch_1_fun.6), calls=%async_computation.6 | async-start | bytes 32768 | tf_op jit(solution)/shard_map/cond/branch_1_fun/all_to_all | solution.py:212
  88.1 1.7 %fusion.5 = bf16[1024,512]{1,0:T(8,128)(2,1)} fusion(bf16[512,1024]{1,0:T(8,128)(2,1)S(1)} %get-tuple-element.48, bf16[512,512]{1,0:T(8,128)(2,1)S(1)} %bitcast.22), kind=kOutput, calls=%fused_computation.13 | convolution fusion | flops 536870912 | bytes 2621440 | tf_op jit(solution)/shard_map/cond/branch_1_fun/dot_general | solution.py:285
  89.9 0.3 all-to-all-done.6.pieces
  90.2 0.8 branch_1_fun.7
  (4 shorter events, 0.0 us)
Async XLA Ops:
  0.6 33.6 %copy-start.2 = (bf16[512,1024]{1,0:T(8,128)(2,1)S(1)}, bf16[512,1024]{1,0:T(8,128)(2,1)}, u32[]{:S(2)}) copy-start(bf16[512,1024]{1,0:T(8,128)(2,1)} %weight.1) | copy-start | bytes 3145732
  5.7 28.6 %copy-start.1 = (bf16[512,512]{1,0:T(8,128)(2,1)S(1)}, bf16[512,512]{1,0:T(8,128)(2,1)}, u32[]{:S(2)}) copy-start(bf16[512,512]{1,0:T(8,128)(2,1)} %act.1) | copy-start | bytes 1572868
  14.9 17.0 %all-to-all-start.7 = ((bf16[16,16,128]{2,1,0:T(8,128)(2,1)}), bf16[16,16,128]{2,1,0:T(8,128)(2,1)S(1)}, u32[]{:S(2)}, u32[]{:S(2)}) async-start(bf16[16,16,128]{2,1,0:T(8,128)(2,1)} %broadcast_in_dim.33), calls=%async_computation.7 | async-start | bytes 131072 | tf_op jit(solution)/shard_map/all_to_all | solution.py:212
  28.4 5.8 %copy-start.5 = (s32[512,64]{0,1:T(8,128)S(1)}, s32[512,64]{0,1:T(8,128)}, u32[]{:S(2)}) copy-start(s32[512,64]{0,1:T(8,128)} %param.13) | copy-start | bytes 393220
  31.9 2.4 %copy-start.6 = (f32[1024]{0:T(1024)S(1)}, f32[1024]{0:T(1024)}, u32[]{:S(2)}) copy-start(f32[1024]{0:T(1024)} %param.10) | copy-start | bytes 12292
  34.2 0.7 copy-start
  39.0 17.1 %all-to-all-start.4 = ((bf16[16,32,512]{2,1,0:T(8,128)(2,1)}), bf16[16,32,512]{2,1,0:T(8,128)(2,1)S(1)}, u32[]{:S(2)}, u32[]{:S(2)}) async-start(bf16[16,32,512]{2,1,0:T(8,128)(2,1)} %bitcast.7), calls=%async_computation.4 | async-start | bytes 1048576 | tf_op jit(solution)/shard_map/cond/branch_1_fun/all_to_all | solution.py:206
  57.1 13.1 %copy-start.4 = (bf16[1024,512]{1,0:T(8,128)(2,1)S(1)}, bf16[1024,512]{1,0:T(8,128)(2,1)}, u32[]{:S(2)}) copy-start(bf16[1024,512]{1,0:T(8,128)(2,1)} %get-tuple-element.47.weight) | copy-start | bytes 3145732 | tf_op jit(solution)/shard_map/conditional
  57.1 13.1 %all-to-all-start.5 = ((bf16[16,32,512]{2,1,0:T(8,128)(2,1)}), bf16[16,32,512]{2,1,0:T(8,128)(2,1)S(1)}, u32[]{:S(2)}, u32[]{:S(2)}) async-start(bf16[16,32,512]{2,1,0:T(8,128)(2,1)} %branch_1_fun.5), calls=%async_computation.5 | async-start | bytes 1048576 | tf_op jit(solution)/shard_map/cond/branch_1_fun/all_to_all | solution.py:206
  72.5 17.7 %all-to-all-start.6 = ((f32[32,1,128]{2,1,0:T(1,128)}), f32[32,1,128]{2,1,0:T(1,128)S(1)}, u32[]{:S(2)}, u32[]{:S(2)}) async-start(f32[32,1,128]{2,1,0:T(1,128)} %branch_1_fun.6), calls=%async_computation.6 | async-start | bytes 32768 | tf_op jit(solution)/shard_map/cond/branch_1_fun/all_to_all | solution.py:212

commit v5 on v4

--- a/solution.py
+++ b/solution.py
@@ -155,20 +155,21 @@
         rec[rows, :] = jnp.dot(latents[rows, :], weight[...], preferred_element_type=F32).astype(rec.dtype)
 
 
-def mix_kernel(recs, act, bias, out):
+def mix_kernel(sizes, recs, act, bias, out):
     groups = recs.shape[0]
+    at_group = [turned(g, sizes) for g in range(groups)]
     for r in range(0, recs.shape[1], 16):
         for c in range(0, recs.shape[2], LANES):
             at = (pl.ds(r, 16), pl.ds(c, LANES))
             err = bias[:, pl.ds(c, LANES)] - act[at].astype(F32)
             errs = []
             for g in range(groups):
-                err = err + recs[(g, *at)].astype(F32)
+                err = err + recs[(at_group[g], *at)].astype(F32)
                 errs.append(err)
             suffix = jnp.zeros_like(err)
             for g in reversed(range(groups)):
                 suffix = suffix + errs[g]
-                out[(g, *at)] = (suffix * (1.0 / groups)).astype(out.dtype)
+                out[(at_group[g], *at)] = (suffix * (1.0 / groups)).astype(out.dtype)
 
 
 def grad_kernel(few, back, weight, slots, out):
@@ -202,13 +203,20 @@
     return jax.ShapeDtypeStruct(shape, dtype)
 
 
-def swap(pieces, axes):
-    return lax.all_to_all(pieces, axes, 0, 0)
-
-
-def swap_from_half(pieces, axes):
-    size = lax.axis_size(axes)
-    order = [[(i + size // 2) % size for i in range(size)]]
+def turned(place, sizes):
+    out, step = 0, 1
+    for size in reversed(sizes):
+        out = out + (place // step % size + size // 2) % size * step
+        step = step * size
+    return out
+
+
+def sizes_of(axes):
+    return [lax.axis_size(a) for a in axes]
+
+
+def swap_from_far(pieces, axes, sizes):
+    order = [[turned(i, sizes) for i in range(pieces.shape[0])]]
     return lax.all_to_all(pieces, axes, 0, 0, axis_index_groups=order)
 
 
@@ -218,7 +226,8 @@
     both = lax.all_gather(partial, core)
     half = lax.dynamic_slice_in_dim(both, lax.axis_index(core) * rows, rows, 1)
     half = (half[0] + half[1]).astype(BF16)
-    pieces = swap_from_half(jnp.broadcast_to(half[None], (lax.axis_size(ring), *half.shape)), ring)
+    size = lax.axis_size(ring)
+    pieces = swap_from_far(jnp.broadcast_to(half[None], (size, *half.shape)), ring, [size])
     return lax.all_gather(jnp.sum(pieces.astype(F32), axis=0), core, tiled=True)
 
 
@@ -269,10 +278,18 @@
         dec_weight,
     )
     rows = tokens // groups
-    recs = swap(rec.reshape(groups, rows, channels), NARROW)
-    act_rows = lax.dynamic_slice_in_dim(activations, group * rows, rows, 0)
-    mixed = call(mix_kernel, array(recs.shape, BF16), 8 * recs.size, recs, act_rows, dec_bias[None])
-    back = swap(mixed, NARROW).reshape(tokens, channels)
+    sizes = sizes_of(NARROW)
+    recs = swap_from_far(rec.reshape(groups, rows, channels), NARROW, sizes)
+    act_rows = lax.dynamic_slice_in_dim(activations, turned(group, sizes) * rows, rows, 0)
+    mixed = call(
+        functools.partial(mix_kernel, sizes),
+        array(recs.shape, BF16),
+        8 * recs.size,
+        recs,
+        act_rows,
+        dec_bias[None],
+    )
+    back = swap_from_far(mixed, NARROW, sizes).reshape(tokens, channels)
     grads = call(
         functools.partial(grad_kernel, few),
         array((wide, 1 if few else 8, LANES), F32),
@@ -281,7 +298,7 @@
         dec_weight,
         slots,
     )
-    parts = swap_from_half(grads, WIDE)
+    parts = swap_from_far(grads, WIDE, [wide])
     dec_grad = lax.dot_general(
         latents, back, (((0,), (0,)), ((), ())), preferred_element_type=F32
     ).astype(BF16)

time: 91.6 us -> 88.8 us (0.969)
  waiting for transfers between devices: 21.9 us -> 14.8 us
  starting transfers between devices: 39.2 us -> 43.6 us
    all_to_all x4, waiting for transfers between devices: 21.9 us -> 14.8 us  [swap_from_far(): return lax.all_to_all(pieces, axes, 0, 0, axis_index_groups=order)]
    all_to_all x4, starting transfers between devices: 39.2 us -> 43.6 us  [swap_from_far(): return lax.all_to_all(pieces, axes, 0, 0, axis_index_groups=order)]
  transfers between devices with their start and end apart: 4 -> 4, of which waited for: 4 -> 4; matrix products, arithmetic and copies ran while one was open for 2% -> 2% of each run, Pallas kernels for 1% -> 2%
where the time goes in v5:
time: 88.8 us; the launch traced here: 88.2 us
  starting transfers between devices  43.6 us (49%)
  waiting for transfers between devices  14.8 us (17%)
  Pallas kernels  14.5 us (16%)
  blocking collectives  10.8 us (12%)
  matrix products  1.72 us (2%)
  between operations  1.36 us (2%)
  local copies, waits for them, and re-layouts  1.33 us (1%)
    all_to_all x4, starting transfers between devices, swap_from_far(): return lax.all_to_all(pieces, axes, 0, 0, axis_index_groups=order)  43.6 us
    all_to_all x4, waiting for transfers between devices, swap_from_far(): return lax.all_to_all(pieces, axes, 0, 0, axis_index_groups=order)  14.8 us
    pallas_call x6, Pallas kernels, call(): pl.pallas_call(kernel, out_shape=shapes, compiler_params=pltpu.CompilerPa...  14.5 us
    all_gather x1, blocking collectives, summed_over_wide(): both = lax.all_gather(partial, core)  8.5 us
    all_gather x1, blocking collectives, summed_over_wide(): return lax.all_gather(jnp.sum(pieces.astype(F32), axis=0), core, tiled=True)  2.34 us
  transfers between devices with their start and end apart: 4, of which 4 were waited for; matrix products, arithmetic and copies ran while one was open for 2% of the time, Pallas kernels for 2%

profile of v5, /device:TPU:1, one launch (start us, length us, event | category | flops | bytes accessed | tf_op | source)
XLA Modules:
  0.0 88.2 jit_solution(6147758441762645389)
XLA Ops:
  0.6 0.0 copy-start.2
  0.6 5.0 %shard_map.77 = (f32[32,128]{1,0:T(8,128)S(1)}, s32[16,512]{1,0:T(8,128)S(1)}, s32[512,128]{1,0:T(8,128)S(1)}, s32[8,512]{1,0:T(8,128)S(1)}, s32[1]{0:T(128)}) custom-call(s32[1]{0:T(128)} %bitcast.10.group, s32[64,512]{1,0:T(8,128)} %bitcast.29, bf16[512,512]{1,0:T(8,128)(2,1)} %act.1, bf16[512,1024]{1,0:T(8,128)(2,1)} %weight.1), custom_call_target="tpu_custom_call" | custom-call | flops 536870912 | bytes 2031624 | tf_op jit(solution)/shard_map/pallas_call | solution.py:193
  5.7 0.0 copy-start.1
  5.7 8.5 %all-gather.1 = f32[64,128]{1,0:T(8,128)S(1)} all-gather(f32[32,128]{1,0:T(8,128)S(1)} %get-tuple-element.63), channel_id=3, replica_groups=mesh['wide_0'=16,'wide_1'=2,'narrow_0'=4,'narrow_1'=4] {'wide_1'}, dimensions={0}, use_global_device_ids=true | all-gather | bytes 49152 | tf_op jit(solution)/shard_map/all_gather | solution.py:226
  14.2 0.6 broadcast_in_dim.33
  14.9 12.9 %all-to-all-start.7 = ((bf16[16,16,128]{2,1,0:T(8,128)(2,1)}), bf16[16,16,128]{2,1,0:T(8,128)(2,1)S(1)}, u32[]{:S(2)}, u32[]{:S(2)}) async-start(bf16[16,16,128]{2,1,0:T(8,128)(2,1)} %broadcast_in_dim.33), calls=%async_computation.7 | async-start | bytes 131072 | tf_op jit(solution)/shard_map/all_to_all | solution.py:220
  28.4 0.0 copy-start.5
  28.4 1.3 %shard_map.78 = s32[2,512,128]{2,1,0:T(8,128)S(1)} custom-call(s32[16,512]{1,0:T(8,128)S(1)} %get-tuple-element.64.named, s32[8,512]{1,0:T(8,128)S(1)} %get-tuple-element.65.base), custom_call_target="tpu_custom_call" | custom-call | flops 67108864 | bytes 573440 | tf_op jit(solution)/shard_map/pallas_call | solution.py:193
  29.8 2.1 %all-to-all-done.7 = bf16[16,16,128]{2,1,0:T(8,128)(2,1)S(1)} async-done(((bf16[16,16,128]{2,1,0:T(8,128)(2,1)}), bf16[16,16,128]{2,1,0:T(8,128)(2,1)S(1)}, u32[]{:S(2)}, u32[]{:S(2)}) %all-to-all-start.7) | async-done | bytes 65568 | tf_op jit(solution)/shard_map/all_to_all | solution.py:220
  31.9 0.0 copy-start.6
  31.9 2.3 %all_gather.20 = f32[32,128]{1,0:T(8,128)S(1)} all-gather(f32[16,128]{1,0:T(8,128)S(1)} %convert_reduce_fusion.1), channel_id=1, replica_groups=mesh['wide_0'=16,'wide_1'=2,'narrow_0'=4,'narrow_1'=4] {'wide_1'}, dimensions={0}, use_global_device_ids=true | all-gather | bytes 24576 | tf_op jit(solution)/shard_map/all_gather | solution.py:231
  34.2 0.0 copy-start
  34.2 0.0 copy-done.2
  34.2 0.0 copy-done.1
  34.2 0.0 copy-done.5
  34.2 0.0 copy-done.6
  34.3 0.7 copy-done
  34.9 53.3 %conditional.2 = (bf16[1024,512]{1,0:T(8,128)(2,1)}, f32[16,1024]{1,0:T(8,128)}) conditional(s32[]{:T(128)} %bitcast.12, (s32[1]{0:T(128)}, s32[64,512]{1,0:T(8,128)S(1)}, bf16[512,512]{1,0:T(8,128)(2,1)S(1)}, bf16[512,1024]{1,0:T(8,128)(2,1)S(1)}, f32[1024]{0:T(1024)S(1)}, /*index=5*/bf16[1024,512]{1,0:T(8,128)(2,1)}, f32[512]{0:T(512)S(1)}) %tuple.30, ...), branch_computations={%region_1.3_spmd, %region_3.4_spmd} | conditional | flops 2218278912 | bytes 22862864
  34.9 4.1 %branch_1_fun.4 = (bf16[512,1024]{1,0:T(8,128)(2,1)S(1)}, bf16[512,512]{1,0:T(8,128)(2,1)}) custom-call(f32[32,128]{1,0:T(8,128)S(1)} %get-tuple-element.44.packed, s32[2,512,128]{2,1,0:T(8,128)S(1)} %get-tuple-element.45.maps, f32[1,1024]{1,0:T(1,128)S(1)} %bitcast.32, bf16[1024,512]{1,0:T(8,128)(2,1)} %get-tuple-element.47.weight), custom_call_target="tpu_custom_call" | custom-call | flops 536870912 | bytes 3166208 | tf_op jit(solution)/shard_map/cond/branch_1_fun/pallas_call | solution.py:193
  39.0 8.8 %all-to-all-start.4 = ((bf16[16,32,512]{2,1,0:T(8,128)(2,1)}), bf16[16,32,512]{2,1,0:T(8,128)(2,1)S(1)}, u32[]{:S(2)}, u32[]{:S(2)}) async-start(bf16[16,32,512]{2,1,0:T(8,128)(2,1)} %bitcast.7), calls=%async_computation.4 | async-start | bytes 1048576 | tf_op jit(solution)/shard_map/cond/branch_1_fun/all_to_all | solution.py:220
  47.8 6.9 %all-to-all-done.4.recs = bf16[16,32,512]{2,1,0:T(8,128)(2,1)S(1)} async-done(((bf16[16,32,512]{2,1,0:T(8,128)(2,1)}), bf16[16,32,512]{2,1,0:T(8,128)(2,1)S(1)}, u32[]{:S(2)}, u32[]{:S(2)}) %all-to-all-start.4) | async-done | bytes 524320 | tf_op jit(solution)/shard_map/cond/branch_1_fun/all_to_all | solution.py:220
  54.7 1.0 %branch_1_fun.5 = bf16[16,32,512]{2,1,0:T(8,128)(2,1)} custom-call(bf16[16,32,512]{2,1,0:T(8,128)(2,1)S(1)} %all-to-all-done.4.recs, bf16[32,512]{1,0:T(8,128)(2,1)S(1)} %constant_dynamic-slice_fusion.3.act, f32[1,512]{1,0:T(1,128)S(1)} %bitcast.28), custom_call_target="tpu_custom_call" | custom-call | flops 2097152 | bytes 1083392 | tf_op jit(solution)/shard_map/cond/branch_1_fun/pallas_call | solution.py:193
  55.7 0.0 copy-start.4
  55.7 6.9 %all-to-all-start.5 = ((bf16[16,32,512]{2,1,0:T(8,128)(2,1)}), bf16[16,32,512]{2,1,0:T(8,128)(2,1)S(1)}, u32[]{:S(2)}, u32[]{:S(2)}) async-start(bf16[16,32,512]{2,1,0:T(8,128)(2,1)} %branch_1_fun.5), calls=%async_computation.5 | async-start | bytes 1048576 | tf_op jit(solution)/shard_map/cond/branch_1_fun/all_to_all | solution.py:220
  62.6 5.5 %all-to-all-done.5 = bf16[16,32,512]{2,1,0:T(8,128)(2,1)S(1)} async-done(((bf16[16,32,512]{2,1,0:T(8,128)(2,1)}), bf16[16,32,512]{2,1,0:T(8,128)(2,1)S(1)}, u32[]{:S(2)}, u32[]{:S(2)}) %all-to-all-start.5) | async-done | bytes 524320 | tf_op jit(solution)/shard_map/cond/branch_1_fun/all_to_all | solution.py:220
  68.1 0.0 copy-done.4
  68.1 2.3 %branch_1_fun.6 = f32[32,1,128]{2,1,0:T(1,128)} custom-call(bf16[512,512]{1,0:T(8,128)(2,1)S(1)} %bitcast.21, bf16[1024,512]{1,0:T(8,128)(2,1)S(1)} %copy-done.4, s32[512,128]{1,0:T(8,128)S(1)} %get-tuple-element.52.slots), custom_call_target="tpu_custom_call" | custom-call | flops 536870912 | bytes 1851392 | tf_op jit(solution)/shard_map/cond/branch_1_fun/pallas_call | solution.py:193
  70.4 15.0 %all-to-all-start.6 = ((f32[32,1,128]{2,1,0:T(1,128)}), f32[32,1,128]{2,1,0:T(1,128)S(1)}, u32[]{:S(2)}, u32[]{:S(2)}) async-start(f32[32,1,128]{2,1,0:T(1,128)} %branch_1_fun.6), calls=%async_computation.6 | async-start | bytes 32768 | tf_op jit(solution)/shard_map/cond/branch_1_fun/all_to_all | solution.py:220
  85.4 1.7 %fusion.5 = bf16[1024,512]{1,0:T(8,128)(2,1)} fusion(bf16[512,1024]{1,0:T(8,128)(2,1)S(1)} %get-tuple-element.48, bf16[512,512]{1,0:T(8,128)(2,1)S(1)} %bitcast.22), kind=kOutput, calls=%fused_computation.13 | convolution fusion | flops 536870912 | bytes 2621440 | tf_op jit(solution)/shard_map/cond/branch_1_fun/dot_general | solution.py:302
  87.1 0.3 all-to-all-done.6.pieces
  87.4 0.8 branch_1_fun.7
  (4 shorter events, 0.0 us)
Async XLA Ops:
  0.6 33.6 %copy-start.2 = (bf16[512,1024]{1,0:T(8,128)(2,1)S(1)}, bf16[512,1024]{1,0:T(8,128)(2,1)}, u32[]{:S(2)}) copy-start(bf16[512,1024]{1,0:T(8,128)(2,1)} %weight.1) | copy-start | bytes 3145732
  5.7 28.6 %copy-start.1 = (bf16[512,512]{1,0:T(8,128)(2,1)S(1)}, bf16[512,512]{1,0:T(8,128)(2,1)}, u32[]{:S(2)}) copy-start(bf16[512,512]{1,0:T(8,128)(2,1)} %act.1) | copy-start | bytes 1572868
  14.9 17.0 %all-to-all-start.7 = ((bf16[16,16,128]{2,1,0:T(8,128)(2,1)}), bf16[16,16,128]{2,1,0:T(8,128)(2,1)S(1)}, u32[]{:S(2)}, u32[]{:S(2)}) async-start(bf16[16,16,128]{2,1,0:T(8,128)(2,1)} %broadcast_in_dim.33), calls=%async_computation.7 | async-start | bytes 131072 | tf_op jit(solution)/shard_map/all_to_all | solution.py:220
  28.4 5.8 %copy-start.5 = (s32[512,64]{0,1:T(8,128)S(1)}, s32[512,64]{0,1:T(8,128)}, u32[]{:S(2)}) copy-start(s32[512,64]{0,1:T(8,128)} %param.13) | copy-start | bytes 393220
  31.9 2.4 %copy-start.6 = (f32[1024]{0:T(1024)S(1)}, f32[1024]{0:T(1024)}, u32[]{:S(2)}) copy-start(f32[1024]{0:T(1024)} %param.10) | copy-start | bytes 12292
  34.2 0.7 copy-start
  39.0 15.7 %all-to-all-start.4 = ((bf16[16,32,512]{2,1,0:T(8,128)(2,1)}), bf16[16,32,512]{2,1,0:T(8,128)(2,1)S(1)}, u32[]{:S(2)}, u32[]{:S(2)}) async-start(bf16[16,32,512]{2,1,0:T(8,128)(2,1)} %bitcast.7), calls=%async_computation.4 | async-start | bytes 1048576 | tf_op jit(solution)/shard_map/cond/branch_1_fun/all_to_all | solution.py:220
  55.7 12.4 %copy-start.4 = (bf16[1024,512]{1,0:T(8,128)(2,1)S(1)}, bf16[1024,512]{1,0:T(8,128)(2,1)}, u32[]{:S(2)}) copy-start(bf16[1024,512]{1,0:T(8,128)(2,1)} %get-tuple-element.47.weight) | copy-start | bytes 3145732 | tf_op jit(solution)/shard_map/conditional
  55.7 12.4 %all-to-all-start.5 = ((bf16[16,32,512]{2,1,0:T(8,128)(2,1)}), bf16[16,32,512]{2,1,0:T(8,128)(2,1)S(1)}, u32[]{:S(2)}, u32[]{:S(2)}) async-start(bf16[16,32,512]{2,1,0:T(8,128)(2,1)} %branch_1_fun.5), calls=%async_computation.5 | async-start | bytes 1048576 | tf_op jit(solution)/shard_map/cond/branch_1_fun/all_to_all | solution.py:220
  70.4 17.1 %all-to-all-start.6 = ((f32[32,1,128]{2,1,0:T(1,128)}), f32[32,1,128]{2,1,0:T(1,128)S(1)}, u32[]{:S(2)}, u32[]{:S(2)}) async-start(f32[32,1,128]{2,1,0:T(1,128)} %branch_1_fun.6), calls=%async_computation.6 | async-start | bytes 32768 | tf_op jit(solution)/shard_map/cond/branch_1_fun/all_to_all | solution.py:220

commit v6 on v5

--- a/solution.py
+++ b/solution.py
@@ -47,51 +47,73 @@
     return jnp.where(lanes > 0, placed, 0.0)
 
 
-def fill_slots(few, group, width, ids, named, slots, base, most):
+def up_to(counts):
+    at = lax.broadcasted_iota(jnp.int32, counts.shape, 1) & (CHUNK - 1)
+    for s in (1, 2, 4, 8):
+        counts = counts + jnp.where(at >= s, pltpu.roll(counts, s, axis=1), 0)
+    return counts
+
+
+def fill_slots(few, group, width, ids, named, slots, base):
+    count, tokens = ids.shape
     lane = lax.broadcasted_iota(jnp.int32, (1, LANES), 1)
     line = lax.broadcasted_iota(jnp.int32, (LANES, LANES), 0)
-    entry = lax.broadcasted_iota(jnp.int32, (FEW, LANES), 0)
-    every = lax.broadcasted_iota(jnp.int32, (16, LANES), 0)
-    shift = width.bit_length() - 1
-    needed = jnp.zeros((16, LANES), jnp.int32)
-
-    def up_to(counts):
-        at = lax.broadcasted_iota(jnp.int32, counts.shape, 1) & (CHUNK - 1)
-        for s in (1, 2, 4, 8):
-            counts = counts + jnp.where(at >= s, pltpu.roll(counts, s, axis=1), 0)
-        return counts
-
-    for i in range(ids.shape[1] // LANES):
+    within = ids[...] - group * width
+    mine = (within >= 0) & (within < width)
+    if few:
+        entry = lax.broadcasted_iota(jnp.int32, (FEW, tokens), 0)
+        earlier = lax.broadcasted_iota(jnp.int32, (count, count), 0) > lax.broadcasted_iota(jnp.int32, (count, count), 1)
+        ones = jnp.where(mine, 1.0, 0.0)
+        rank = jnp.dot(
+            jnp.where(earlier, 1.0, 0.0).astype(BF16), ones.astype(BF16), preferred_element_type=F32
+        )
+        taken = (rank[count - 1 :] + ones[count - 1 :]).astype(jnp.int32)
+        place_of = jnp.where(mine, rank.astype(jnp.int32), FEW)
+        held = jnp.full((FEW, tokens), -1, jnp.int32)
+        for k in range(count):
+            held = jnp.where(entry == place_of[k : k + 1], within[k : k + 1], held)
+    else:
+        held = jnp.where(mine, within, -1)
+    named[...] = held
+    for i in range(tokens // LANES):
         cols = pl.ds(i * LANES, LANES)
-        theirs = ids[:, cols]
-        within = theirs - group * width
-        mine = (within >= 0) & (within < width)
+        block = held[:, i * LANES : (i + 1) * LANES]
         if few:
-            owner = theirs >> shift
-            held = jnp.full((FEW, LANES), -1, jnp.int32)
-            taken = jnp.zeros((1, LANES), jnp.int32)
-            tally = jnp.zeros((16, LANES), jnp.int32)
-            for k in range(ids.shape[0]):
-                here = mine[k : k + 1]
-                held = jnp.where(entry == jnp.where(here, taken, FEW), within[k : k + 1], held)
-                taken = taken + jnp.where(here, 1, 0)
-                tally = tally + jnp.where(every == owner[k : k + 1], 1, 0)
-            needed = jnp.maximum(needed, jnp.maximum(tally * (LANES // FEW), up_to(tally)))
-            counts = jnp.broadcast_to(taken, (8, LANES))
+            counts = jnp.broadcast_to(taken[:, i * LANES : (i + 1) * LANES], (8, LANES))
             first = up_to(counts) - counts
             spread = jnp.full((LANES, LANES), -1, jnp.int32)
             for k in range(FEW):
-                at = jnp.where(held[k : k + 1] >= 0, first[:1] + k, -1)
-                spread = jnp.where(line == at, held[k : k + 1], spread)
+                at = jnp.where(block[k : k + 1] >= 0, first[:1] + k, -1)
+                spread = jnp.where(line == at, block[k : k + 1], spread)
         else:
-            held = jnp.where(mine, within, -1)
             first = jnp.broadcast_to(64 * ((lane >> 3) & 1), (8, LANES))
-            spread = jnp.concatenate([held, held], axis=0)
+            spread = jnp.concatenate([block, block], axis=0)
             spread = jnp.where(line >> 6 == (lane >> 3) & 1, spread, -1)
-        named[:, cols] = held
         base[:, cols] = first
         slots[cols, :] = spread.T
+
+
+def count_kernel(width, ids, most):
+    every = lax.broadcasted_iota(jnp.int32, (16, LANES), 0)
+    needed = jnp.zeros((16, LANES), jnp.int32)
+    for i in range(ids.shape[1] // LANES):
+        owner = ids[:, pl.ds(i * LANES, LANES)] >> (width.bit_length() - 1)
+        tally = jnp.zeros((16, LANES), jnp.int32)
+        for k in range(ids.shape[0]):
+            tally = tally + jnp.where(every == owner[k : k + 1], 1, 0)
+        needed = jnp.maximum(needed, jnp.maximum(tally * (LANES // FEW), up_to(tally)))
     most[0] = jnp.max(needed)
+
+
+def target_kernel(place_of, act, bias, out):
+    rows = out.shape[0]
+    first = pl.multiple_of(place_of[0] * rows, rows)
+    out[...] = bias[...] - act[pl.ds(first, rows), :].astype(F32)
+
+
+def turn_kernel(weight, out):
+    for r in range(0, weight.shape[0], 256):
+        out[:, pl.ds(r, 256)] = weight[pl.ds(r, 256), :].T
 
 
 def maps_kernel(named, base, out):
@@ -122,14 +144,14 @@
             out[m, cols, :] = maps[m].T
 
 
-def encode_kernel(few, group, ids, act, weight, packed, named, slots, base, most, act_here, weight_here, arrived):
+def encode_kernel(few, group, ids, act, weight, packed, named, slots, base, act_here, weight_here, arrived):
     copies = [
         pltpu.make_async_copy(act, act_here, arrived.at[0]),
         pltpu.make_async_copy(weight, weight_here, arrived.at[1]),
     ]
     for copy in copies:
         copy.start()
-    fill_slots(few, group[0], weight.shape[1], ids, named, slots, base, most)
+    fill_slots(few, group[0], weight.shape[1], ids, named, slots, base)
     for copy in copies:
         copy.wait()
     step = 8 * CHUNK
@@ -149,19 +171,21 @@
         chunks = [unpack_rows(packed[pl.ds((8 * i + q) * depth, depth), :], few) for q in range(8)]
         values = jnp.concatenate(chunks, axis=0)
         mine = [maps[0, rows, :], maps[1, rows, :]]
-        for c in range(latents.shape[1] // LANES):
-            cols = pl.ds(c * LANES, LANES)
-            latents[rows, cols] = place(values, mine, c, bias[:, cols]).astype(BF16)
-        rec[rows, :] = jnp.dot(latents[rows, :], weight[...], preferred_element_type=F32).astype(rec.dtype)
-
-
-def mix_kernel(sizes, recs, act, bias, out):
+        blocks = [
+            place(values, mine, c, bias[:, pl.ds(c * LANES, LANES)]) for c in range(latents.shape[1] // LANES)
+        ]
+        here = jnp.concatenate(blocks, axis=1).astype(BF16)
+        latents[rows, :] = here
+        rec[rows, :] = jnp.dot(here, weight[...], preferred_element_type=F32).astype(rec.dtype)
+
+
+def mix_kernel(sizes, recs, target, out):
     groups = recs.shape[0]
     at_group = [turned(g, sizes) for g in range(groups)]
     for r in range(0, recs.shape[1], 16):
         for c in range(0, recs.shape[2], LANES):
             at = (pl.ds(r, 16), pl.ds(c, LANES))
-            err = bias[:, pl.ds(c, LANES)] - act[at].astype(F32)
+            err = target[at]
             errs = []
             for g in range(groups):
                 err = err + recs[(at_group[g], *at)].astype(F32)
@@ -172,11 +196,11 @@
                 out[(at_group[g], *at)] = (suffix * (1.0 / groups)).astype(out.dtype)
 
 
-def grad_kernel(few, back, weight, slots, out):
+def grad_kernel(few, back, turned_weight, slots, out):
     step = 8 * CHUNK
     for i in range(back.shape[0] // step):
         rows = pl.ds(i * step, step)
-        part = lax.dot_general(back[rows, :], weight[...], (((1,), (1,)), ((), ())), preferred_element_type=F32)
+        part = jnp.dot(back[rows, :], turned_weight[...], preferred_element_type=F32)
         first = (8 * i + out.shape[0] // 2) % out.shape[0]
         out[pl.ds(first, 8)] = pick_slots(part, slots[rows, :], few)
 
@@ -231,27 +255,28 @@
     return lax.all_gather(jnp.sum(pieces.astype(F32), axis=0), core, tiled=True)
 
 
+def specs(*spaces):
+    return [pl.BlockSpec(memory_space=m) for m in spaces]
+
+
 def encode(few, group, ids, activations, enc_weight):
     tokens, channels = activations.shape
     width = enc_weight.shape[1]
     depth = tokens // CHUNK * (1 if few else 8)
-    vmem, smem = (pl.BlockSpec(memory_space=m) for m in (pltpu.VMEM, pltpu.SMEM))
-    partial, named, slots, base, most = call(
+    partial, named, slots, base = call(
         functools.partial(encode_kernel, few),
         (
             array((depth, LANES), F32),
             array((FEW if few else ids.shape[0], tokens), jnp.int32),
             array((tokens, LANES), jnp.int32),
             array((8, tokens), jnp.int32),
-            array((1,), jnp.int32),
         ),
         2 * tokens * channels * width,
         group,
         ids,
         activations,
         enc_weight,
-        in_specs=[smem, vmem, pl.BlockSpec(memory_space=pl.ANY), pl.BlockSpec(memory_space=pl.ANY)],
-        out_specs=(vmem, vmem, vmem, vmem, smem),
+        in_specs=specs(pltpu.SMEM, pltpu.VMEM, pl.ANY, pl.ANY),
         scratch_shapes=[
             pltpu.VMEM(activations.shape, BF16),
             pltpu.VMEM(enc_weight.shape, BF16),
@@ -259,71 +284,92 @@
         ],
     )
     maps = call(maps_kernel, array((2, tokens, LANES), jnp.int32), 1 << 26, named, base)
-    return summed_over_wide(partial), slots, maps, most[0]
-
-
-def decode(few, preact, slots, maps, activations, enc_bias, dec_weight, dec_bias):
-    tokens, channels = activations.shape
-    width = dec_weight.shape[0]
-    groups, wide = lax.axis_size(NARROW), lax.axis_size(WIDE)
-    group = lax.axis_index(NARROW)
-    work = 2 * tokens * channels * width
+    return summed_over_wide(partial), slots, maps
+
+
+def decode(few, preact, maps, target, enc_bias, dec_weight):
+    width, channels = dec_weight.shape
+    tokens = maps.shape[1]
     latents, rec = call(
         functools.partial(decode_kernel, few),
         (array((tokens, width), BF16), array((tokens, channels), BF16)),
-        work,
+        2 * tokens * channels * width,
         preact,
         maps,
         enc_bias[None],
         dec_weight,
     )
-    rows = tokens // groups
     sizes = sizes_of(NARROW)
-    recs = swap_from_far(rec.reshape(groups, rows, channels), NARROW, sizes)
-    act_rows = lax.dynamic_slice_in_dim(activations, turned(group, sizes) * rows, rows, 0)
-    mixed = call(
-        functools.partial(mix_kernel, sizes),
-        array(recs.shape, BF16),
-        8 * recs.size,
-        recs,
-        act_rows,
-        dec_bias[None],
-    )
-    back = swap_from_far(mixed, NARROW, sizes).reshape(tokens, channels)
-    grads = call(
+    recs = swap_from_far(rec.reshape(-1, *target.shape), NARROW, sizes)
+    mixed = call(functools.partial(mix_kernel, sizes), array(recs.shape, BF16), 8 * recs.size, recs, target)
+    return latents, swap_from_far(mixed, NARROW, sizes).reshape(tokens, channels)
+
+
+def latent_parts(few, back, turned_weight, slots):
+    return call(
         functools.partial(grad_kernel, few),
-        array((wide, 1 if few else 8, LANES), F32),
-        work,
+        array((lax.axis_size(WIDE), 1 if few else 8, LANES), F32),
+        2 * back.size * turned_weight.shape[1],
         back,
-        dec_weight,
+        turned_weight,
         slots,
     )
+
+
+def finish(few, grads, back, latents, maps):
+    wide = lax.axis_size(WIDE)
     parts = swap_from_far(grads, WIDE, [wide])
     dec_grad = lax.dot_general(
         latents, back, (((0,), (0,)), ((), ())), preferred_element_type=F32
     ).astype(BF16)
-    own_rows = tokens // wide
+    own_rows = maps.shape[1] // wide
     own_maps = lax.dynamic_slice_in_dim(maps, lax.axis_index(WIDE) * own_rows, own_rows, 1)
     latent_grad = call(
-        functools.partial(own_kernel, few), array((own_rows, width), F32), 1 << 20, parts, own_maps
+        functools.partial(own_kernel, few),
+        array((own_rows, latents.shape[1]), F32),
+        1 << 20,
+        parts,
+        own_maps,
     )
     return dec_grad, latent_grad
 
 
 def local(activations, enc_weight, enc_bias, dec_weight, dec_bias, active_ids):
-    group = lax.axis_index(NARROW)[None]
+    tokens, channels = activations.shape
+    width = enc_weight.shape[1]
+    group = lax.axis_index(NARROW)
     ids = active_ids.T
-    rest = (activations, enc_bias, dec_weight, dec_bias)
-    preact, slots, maps, needed = encode(True, group, ids, activations, enc_weight)
+    preact, slots, maps = encode(True, group[None], ids, activations, enc_weight)
+    needed = call(
+        functools.partial(count_kernel, width),
+        array((1,), jnp.int32),
+        1 << 24,
+        ids,
+        out_specs=specs(pltpu.SMEM)[0],
+    )
+    target = call(
+        target_kernel,
+        array((tokens // lax.axis_size(NARROW), channels), F32),
+        1 << 20,
+        turned(group, sizes_of(NARROW))[None],
+        activations,
+        dec_bias[None],
+        in_specs=specs(pltpu.SMEM, pltpu.VMEM, pltpu.VMEM),
+    )
+    turned_weight = call(turn_kernel, array((channels, width), BF16), 1 << 26, dec_weight)
+    latents, back = decode(True, preact, maps, target, enc_bias, dec_weight)
+
+    grads = latent_parts(True, back, turned_weight, slots)
 
     def few():
-        return decode(True, preact, slots, maps, *rest)
+        return finish(True, grads, back, latents, maps)
 
     def many():
-        preact, slots, maps, _ = encode(False, group, ids, activations, enc_weight)
-        return decode(False, preact, slots, maps, *rest)
-
-    return lax.cond(needed <= LANES, few, many)
+        preact, slots, maps = encode(False, group[None], ids, activations, enc_weight)
+        latents, back = decode(False, preact, maps, target, enc_bias, dec_weight)
+        return finish(False, latent_parts(False, back, turned_weight, slots), back, latents, maps)
+
+    return lax.cond(needed[0] <= LANES, few, many)
 
 
 def solution(mesh):

time: 88.8 us -> 87.9 us (0.990)
  waiting for transfers between devices: 14.8 us -> 12.1 us
  matrix products: 1.72 us -> 3.07 us
    all_to_all x4, waiting for transfers between devices: 14.8 us -> 12.1 us  [swap_from_far(): return lax.all_to_all(pieces, axes, 0, 0, axis_index_groups=order)]
    dot_general x1, matrix products: 1.72 us -> 3.07 us  [finish(): lax.dot_general(latents, back, (((0,), (0,)), ((), ())), preferred_elemen...]
    pallas_call x6 -> x9, Pallas kernels: 14.5 us -> 15 us  [call(): pl.pallas_call(kernel, out_shape=shapes, compiler_params=pltpu.CompilerPa...]
  transfers between devices with their start and end apart: 4 -> 4, of which waited for: 4 -> 3; matrix products, arithmetic and copies ran while one was open for 2% -> 4% of each run, Pallas kernels for 2% -> 3%
where the time goes in v6:
time: 87.9 us; the launch traced here: 87.3 us
  starting transfers between devices  43.7 us (50%)
  Pallas kernels  15 us (17%)
  waiting for transfers between devices  12.1 us (14%)
  blocking collectives  10.7 us (12%)
  matrix products  3.07 us (3%)
  between operations  1.37 us (2%)
  local copies, waits for them, and re-layouts  1.33 us (2%)
    all_to_all x4, starting transfers between devices, swap_from_far(): return lax.all_to_all(pieces, axes, 0, 0, axis_index_groups=order)  43.7 us
    pallas_call x9, Pallas kernels, call(): pl.pallas_call(kernel, out_shape=shapes, compiler_params=pltpu.CompilerPa...  15 us
    all_to_all x4, waiting for transfers between devices, swap_from_far(): return lax.all_to_all(pieces, axes, 0, 0, axis_index_groups=order)  12.1 us
    all_gather x1, blocking collectives, summed_over_wide(): both = lax.all_gather(partial, core)  8.37 us
    dot_general x1, matrix products, finish(): lax.dot_general(latents, back, (((0,), (0,)), ((), ())), preferred_elemen...  3.07 us
    all_gather x1, blocking collectives, summed_over_wide(): return lax.all_gather(jnp.sum(pieces.astype(F32), axis=0), core, tiled=True)  2.34 us
  transfers between devices with their start and end apart: 4, of which 3 were waited for; matrix products, arithmetic and copies ran while one was open for 4% of the time, Pallas kernels for 3%

profile of v6, /device:TPU:1, one launch (start us, length us, event | category | flops | bytes accessed | tf_op | source)
XLA Modules:
  0.0 87.3 jit_solution(10493675186872264819)
XLA Ops:
  0.6 0.0 copy-start.1
  0.6 4.4 %shard_map.80 = (f32[32,128]{1,0:T(8,128)S(1)}, s32[16,512]{1,0:T(8,128)S(1)}, s32[512,128]{1,0:T(8,128)S(1)}, s32[8,512]{1,0:T(8,128)S(1)}) custom-call(s32[1]{0:T(128)} %bitcast.10.group, s32[64,512]{1,0:T(8,128)} %bitcast.27, bf16[512,512]{1,0:T(8,128)(2,1)} %act.3, bf16[512,1024]{1,0:T(8,128)(2,1)} %weight.4), custom_call_target="tpu_custom_call" | custom-call | flops 536870912 | bytes 2031620 | tf_op jit(solution)/shard_map/pallas_call | solution.py:217
  5.0 8.4 %all-gather.1 = f32[64,128]{1,0:T(8,128)S(1)} all-gather(f32[32,128]{1,0:T(8,128)S(1)} %get-tuple-element.55), channel_id=3, replica_groups=mesh['wide_0'=16,'wide_1'=2,'narrow_0'=4,'narrow_1'=4] {'wide_1'}, dimensions={0}, use_global_device_ids=true | all-gather | bytes 49152 | tf_op jit(solution)/shard_map/all_gather | solution.py:250
  13.4 0.6 broadcast_in_dim.38
  14.1 12.9 %all-to-all-start.5 = ((bf16[16,16,128]{2,1,0:T(8,128)(2,1)}), bf16[16,16,128]{2,1,0:T(8,128)(2,1)S(1)}, u32[]{:S(2)}, u32[]{:S(2)}) async-start(bf16[16,16,128]{2,1,0:T(8,128)(2,1)} %broadcast_in_dim.38), calls=%async_computation.5 | async-start | bytes 131072 | tf_op jit(solution)/shard_map/all_to_all | solution.py:244
  27.0 1.3 %shard_map.81.maps = s32[2,512,128]{2,1,0:T(8,128)S(1)} custom-call(s32[16,512]{1,0:T(8,128)S(1)} %get-tuple-element.56.named, s32[8,512]{1,0:T(8,128)S(1)} %get-tuple-element.57.base), custom_call_target="tpu_custom_call" | custom-call | flops 67108864 | bytes 573440 | tf_op jit(solution)/shard_map/pallas_call | solution.py:217
  28.3 2.7 %all-to-all-done.5 = bf16[16,16,128]{2,1,0:T(8,128)(2,1)S(1)} async-done(((bf16[16,16,128]{2,1,0:T(8,128)(2,1)}), bf16[16,16,128]{2,1,0:T(8,128)(2,1)S(1)}, u32[]{:S(2)}, u32[]{:S(2)}) %all-to-all-start.5) | async-done | bytes 65568 | tf_op jit(solution)/shard_map/all_to_all | solution.py:244
  31.1 0.0 copy-start.6
  31.1 2.3 %all_gather.20.packed = f32[32,128]{1,0:T(8,128)S(1)} all-gather(f32[16,128]{1,0:T(8,128)S(1)} %convert_reduce_fusion.1), channel_id=1, replica_groups=mesh['wide_0'=16,'wide_1'=2,'narrow_0'=4,'narrow_1'=4] {'wide_1'}, dimensions={0}, use_global_device_ids=true | all-gather | bytes 24576 | tf_op jit(solution)/shard_map/all_gather | solution.py:255
  33.4 0.0 copy-done.1
  33.4 0.0 copy-done.6
  33.4 2.9 %shard_map.82 = (bf16[512,1024]{1,0:T(8,128)(2,1)}, bf16[512,512]{1,0:T(8,128)(2,1)}) custom-call(f32[32,128]{1,0:T(8,128)S(1)} %all_gather.20.packed, s32[2,512,128]{2,1,0:T(8,128)S(1)} %shard_map.81.maps, f32[1,1024]{1,0:T(1,128)S(1)} %bitcast.31, bf16[1024,512]{1,0:T(8,128)(2,1)S(1)} %copy-done.1), custom_call_target="tpu_custom_call" | custom-call | flops 536870912 | bytes 3166208 | tf_op jit(solution)/shard_map/pallas_call | solution.py:217
  36.3 0.0 copy-start.4
  36.3 8.9 %all-to-all-start.6 = ((bf16[16,32,512]{2,1,0:T(8,128)(2,1)}), bf16[16,32,512]{2,1,0:T(8,128)(2,1)S(1)}, u32[]{:S(2)}, u32[]{:S(2)}) async-start(bf16[16,32,512]{2,1,0:T(8,128)(2,1)} %bitcast.14), calls=%async_computation.6 | async-start | bytes 1048576 | tf_op jit(solution)/shard_map/all_to_all | solution.py:244
  45.2 0.0 copy-start
  45.2 0.0 copy-done.4
  45.2 0.7 copy-done
  45.9 6.3 %all-to-all-done.6.recs = bf16[16,32,512]{2,1,0:T(8,128)(2,1)S(1)} async-done(((bf16[16,32,512]{2,1,0:T(8,128)(2,1)}), bf16[16,32,512]{2,1,0:T(8,128)(2,1)S(1)}, u32[]{:S(2)}, u32[]{:S(2)}) %all-to-all-start.6) | async-done | bytes 524320 | tf_op jit(solution)/shard_map/all_to_all | solution.py:244
  52.2 1.0 %shard_map.83 = bf16[16,32,512]{2,1,0:T(8,128)(2,1)} custom-call(bf16[16,32,512]{2,1,0:T(8,128)(2,1)S(1)} %all-to-all-done.6.recs, f32[32,512]{1,0:T(8,128)S(1)} %shard_map.78.target), custom_call_target="tpu_custom_call" | custom-call | flops 2097152 | bytes 1114112 | tf_op jit(solution)/shard_map/pallas_call | solution.py:217
  53.1 0.0 copy-start.5
  53.2 6.9 %all-to-all-start.7 = ((bf16[16,32,512]{2,1,0:T(8,128)(2,1)}), bf16[16,32,512]{2,1,0:T(8,128)(2,1)}, u32[]{:S(2)}, u32[]{:S(2)}) async-start(bf16[16,32,512]{2,1,0:T(8,128)(2,1)} %shard_map.83), calls=%async_computation.7 | async-start | bytes 1048576 | tf_op jit(solution)/shard_map/all_to_all | solution.py:244
  60.0 0.0 copy-done.5
  60.1 1.3 %shard_map.77 = s32[1]{0:T(128)} custom-call(s32[64,512]{1,0:T(8,128)S(1)} %bitcast.29), custom_call_target="tpu_custom_call" | custom-call | flops 16777216 | bytes 131076 | tf_op jit(solution)/shard_map/pallas_call | solution.py:217
  62.0 0.3 shard_map.79.turned_weight
  62.3 3.1 %all-to-all-done.7 = bf16[16,32,512]{2,1,0:T(8,128)(2,1)} async-done(((bf16[16,32,512]{2,1,0:T(8,128)(2,1)}), bf16[16,32,512]{2,1,0:T(8,128)(2,1)}, u32[]{:S(2)}, u32[]{:S(2)}) %all-to-all-start.7) | async-done | bytes 524320 | tf_op jit(solution)/shard_map/all_to_all | solution.py:244
  65.4 3.0 %shard_map.84 = f32[32,1,128]{2,1,0:T(1,128)} custom-call(bf16[512,512]{1,0:T(8,128)(2,1)} %bitcast.15.back, bf16[512,1024]{1,0:T(8,128)(2,1)S(1)} %shard_map.79.turned_weight, s32[512,128]{1,0:T(8,128)S(1)} %get-tuple-element.60.slots), custom_call_target="tpu_custom_call" | custom-call | flops 536870912 | bytes 1851392 | tf_op jit(solution)/shard_map/pallas_call | solution.py:217
  68.5 18.9 %conditional.2 = (bf16[1024,512]{1,0:T(8,128)(2,1)}, f32[16,1024]{1,0:T(8,128)}) conditional(s32[]{:T(128)} %bitcast.7, (s32[]{:T(128)}, s32[64,512]{1,0:T(8,128)}, bf16[512,512]{1,0:T(8,128)(2,1)S(1)}, bf16[512,1024]{1,0:T(8,128)(2,1)}, f32[1024]{0:T(1024)S(1)}, /*index=5*/bf16[1024,512]{1,0:T(8,128)(2,1)S(1)}, f32[32,512]{1,0:T(8,128)S(1)}, ...), branch_computations={%region_1.3_spmd, %region_3.4_spmd} | conditional | flops 2218278912 | bytes 26497368
  68.5 15.0 %all-to-all-start.4 = ((f32[32,1,128]{2,1,0:T(1,128)}), f32[32,1,128]{2,1,0:T(1,128)S(1)}, u32[]{:S(2)}, u32[]{:S(2)}) async-start(f32[32,1,128]{2,1,0:T(1,128)} %get-tuple-element.43), calls=%async_computation.4 | async-start | bytes 32768 | tf_op jit(solution)/shard_map/cond/branch_1_fun/all_to_all | solution.py:244
  83.5 3.1 %fusion.5 = bf16[1024,512]{1,0:T(8,128)(2,1)} fusion(bf16[512,1024]{1,0:T(8,128)(2,1)} %get-tuple-element.41, bf16[512,512]{1,0:T(8,128)(2,1)} %get-tuple-element.42), kind=kOutput, calls=%fused_computation.11 | convolution fusion | flops 536870912 | bytes 2621440 | tf_op jit(solution)/shard_map/cond/branch_1_fun/dot_general | solution.py:322
  86.5 0.0 all-to-all-done.4.pieces
  86.6 0.8 branch_1_fun.1
  (4 shorter events, 0.0 us)
Async XLA Ops:
  0.6 32.8 %copy-start.1 = (bf16[1024,512]{1,0:T(8,128)(2,1)S(1)}, bf16[1024,512]{1,0:T(8,128)(2,1)}, u32[]{:S(2)}) copy-start(bf16[1024,512]{1,0:T(8,128)(2,1)} %weight.5) | copy-start | bytes 3145732
  14.1 17.0 %all-to-all-start.5 = ((bf16[16,16,128]{2,1,0:T(8,128)(2,1)}), bf16[16,16,128]{2,1,0:T(8,128)(2,1)S(1)}, u32[]{:S(2)}, u32[]{:S(2)}) async-start(bf16[16,16,128]{2,1,0:T(8,128)(2,1)} %broadcast_in_dim.38), calls=%async_computation.5 | async-start | bytes 131072 | tf_op jit(solution)/shard_map/all_to_all | solution.py:244
  31.1 2.4 %copy-start.6 = (f32[1024]{0:T(1024)S(1)}, f32[1024]{0:T(1024)}, u32[]{:S(2)}) copy-start(f32[1024]{0:T(1024)} %param.10) | copy-start | bytes 12292
  36.3 8.9 %copy-start.4 = (bf16[512,512]{1,0:T(8,128)(2,1)S(1)}, bf16[512,512]{1,0:T(8,128)(2,1)}, u32[]{:S(2)}) copy-start(bf16[512,512]{1,0:T(8,128)(2,1)} %act.3) | copy-start | bytes 1572868
  36.3 15.9 %all-to-all-start.6 = ((bf16[16,32,512]{2,1,0:T(8,128)(2,1)}), bf16[16,32,512]{2,1,0:T(8,128)(2,1)S(1)}, u32[]{:S(2)}, u32[]{:S(2)}) async-start(bf16[16,32,512]{2,1,0:T(8,128)(2,1)} %bitcast.14), calls=%async_computation.6 | async-start | bytes 1048576 | tf_op jit(solution)/shard_map/all_to_all | solution.py:244
  45.2 0.7 copy-start
  53.1 6.9 %copy-start.5 = (s32[512,64]{0,1:T(8,128)S(1)}, s32[512,64]{0,1:T(8,128)}, u32[]{:S(2)}) copy-start(s32[512,64]{0,1:T(8,128)} %param.13) | copy-start | bytes 393220
  53.2 12.3 %all-to-all-start.7 = ((bf16[16,32,512]{2,1,0:T(8,128)(2,1)}), bf16[16,32,512]{2,1,0:T(8,128)(2,1)}, u32[]{:S(2)}, u32[]{:S(2)}) async-start(bf16[16,32,512]{2,1,0:T(8,128)(2,1)} %shard_map.83), calls=%async_computation.7 | async-start | bytes 1048576 | tf_op jit(solution)/shard_map/all_to_all | solution.py:244
  68.5 18.1 %all-to-all-start.4 = ((f32[32,1,128]{2,1,0:T(1,128)}), f32[32,1,128]{2,1,0:T(1,128)S(1)}, u32[]{:S(2)}, u32[]{:S(2)}) async-start(f32[32,1,128]{2,1,0:T(1,128)} %get-tuple-element.43), calls=%async_computation.4 | async-start | bytes 32768 | tf_op jit(solution)/shard_map/cond/branch_1_fun/all_to_all | solution.py:244

commit v7 on v6

--- a/solution.py
+++ b/solution.py
@@ -93,7 +93,11 @@
         slots[cols, :] = spread.T
 
 
-def count_kernel(width, ids, most):
+def target_kernel(width, place_of, act, bias, ids, out, most, here, arrived):
+    rows = out.shape[0]
+    first = pl.multiple_of(place_of[0] * rows, rows)
+    copy = pltpu.make_async_copy(act.at[pl.ds(first, rows)], here, arrived)
+    copy.start()
     every = lax.broadcasted_iota(jnp.int32, (16, LANES), 0)
     needed = jnp.zeros((16, LANES), jnp.int32)
     for i in range(ids.shape[1] // LANES):
@@ -103,20 +107,11 @@
             tally = tally + jnp.where(every == owner[k : k + 1], 1, 0)
         needed = jnp.maximum(needed, jnp.maximum(tally * (LANES // FEW), up_to(tally)))
     most[0] = jnp.max(needed)
-
-
-def target_kernel(place_of, act, bias, out):
-    rows = out.shape[0]
-    first = pl.multiple_of(place_of[0] * rows, rows)
-    out[...] = bias[...] - act[pl.ds(first, rows), :].astype(F32)
-
-
-def turn_kernel(weight, out):
-    for r in range(0, weight.shape[0], 256):
-        out[:, pl.ds(r, 256)] = weight[pl.ds(r, 256), :].T
-
-
-def maps_kernel(named, base, out):
+    copy.wait()
+    out[...] = bias[...] - here[...].astype(F32)
+
+
+def maps_kernel(owner, named, base, weight, out, own, turned_weight):
     count, tokens = named.shape
     line = lax.broadcasted_iota(jnp.int32, (LANES, LANES), 0)
     for i in range(tokens // LANES):
@@ -142,15 +137,19 @@
         maps = lax.fori_loop(0, count // 8, body, (zero, zero))
         for m in range(2):
             out[m, cols, :] = maps[m].T
+    own[...] = out[:, pl.ds(pl.multiple_of(owner[0] * CHUNK, CHUNK), CHUNK), :]
+    for r in range(0, weight.shape[0], 256):
+        turned_weight[:, pl.ds(r, 256)] = weight[pl.ds(r, 256), :].T
 
 
 def encode_kernel(few, group, ids, act, weight, packed, named, slots, base, act_here, weight_here, arrived):
-    copies = [
-        pltpu.make_async_copy(act, act_here, arrived.at[0]),
-        pltpu.make_async_copy(weight, weight_here, arrived.at[1]),
-    ]
-    for copy in copies:
-        copy.start()
+    copies = []
+    for n, (array, here) in enumerate(((act, act_here), (weight, weight_here))):
+        step = array.shape[0] // 4
+        for i in range(4):
+            rows = pl.ds(i * step, step)
+            copies.append(pltpu.make_async_copy(array.at[rows], here.at[rows], arrived.at[4 * n + i]))
+            copies[-1].start()
     fill_slots(few, group[0], weight.shape[1], ids, named, slots, base)
     for copy in copies:
         copy.wait()
@@ -163,10 +162,19 @@
         packed[pl.ds(i * depth, depth), :] = picked.reshape(depth, LANES)
 
 
-def decode_kernel(few, packed, maps, bias, weight, latents, rec):
+def decode_kernel(few, packed, maps, bias, weight, latents, rec, weight_here, rec_here, arrived, sent):
     step = 8 * CHUNK
     depth = 1 if few else 8
-    for i in range(latents.shape[0] // step):
+    steps = latents.shape[0] // step
+    part = weight.shape[0] // 4
+    coming = [
+        pltpu.make_async_copy(weight.at[pl.ds(i * part, part)], weight_here.at[pl.ds(i * part, part)], arrived.at[i])
+        for i in range(4)
+    ]
+    for copy in coming:
+        copy.start()
+
+    def fill(i):
         rows = pl.ds(i * step, step)
         chunks = [unpack_rows(packed[pl.ds((8 * i + q) * depth, depth), :], few) for q in range(8)]
         values = jnp.concatenate(chunks, axis=0)
@@ -174,9 +182,23 @@
         blocks = [
             place(values, mine, c, bias[:, pl.ds(c * LANES, LANES)]) for c in range(latents.shape[1] // LANES)
         ]
-        here = jnp.concatenate(blocks, axis=1).astype(BF16)
-        latents[rows, :] = here
-        rec[rows, :] = jnp.dot(here, weight[...], preferred_element_type=F32).astype(rec.dtype)
+        latents[rows, :] = jnp.concatenate(blocks, axis=1).astype(BF16)
+
+    ahead = 2
+    for i in range(ahead):
+        fill(i)
+    for copy in coming:
+        copy.wait()
+    going = []
+    for i in range(steps):
+        rows = pl.ds(i * step, step)
+        rec_here[rows, :] = jnp.dot(latents[rows, :], weight_here[...], preferred_element_type=F32).astype(rec.dtype)
+        going.append(pltpu.make_async_copy(rec_here.at[rows], rec.at[rows], sent.at[i]))
+        going[-1].start()
+        if i + ahead < steps:
+            fill(i + ahead)
+    for copy in going:
+        copy.wait()
 
 
 def mix_kernel(sizes, recs, target, out):
@@ -203,6 +225,24 @@
         part = jnp.dot(back[rows, :], turned_weight[...], preferred_element_type=F32)
         first = (8 * i + out.shape[0] // 2) % out.shape[0]
         out[pl.ds(first, 8)] = pick_slots(part, slots[rows, :], few)
+
+
+def outer_kernel(latents, back, out, here, sent):
+    step = 256
+    copies = []
+    for i in range(out.shape[0] // step):
+        rows = pl.ds(i * step, step)
+        part = lax.dot_general(
+            latents[:, i * step : (i + 1) * step],
+            back[...],
+            (((0,), (0,)), ((), ())),
+            preferred_element_type=F32,
+        )
+        here[rows, :] = part.astype(out.dtype)
+        copies.append(pltpu.make_async_copy(here.at[rows], out.at[rows], sent.at[i]))
+        copies[-1].start()
+    for copy in copies:
+        copy.wait()
 
 
 def own_kernel(few, pieces, maps, out):
@@ -280,11 +320,28 @@
         scratch_shapes=[
             pltpu.VMEM(activations.shape, BF16),
             pltpu.VMEM(enc_weight.shape, BF16),
-            pltpu.SemaphoreType.DMA((2,)),
+            pltpu.SemaphoreType.DMA((8,)),
         ],
     )
-    maps = call(maps_kernel, array((2, tokens, LANES), jnp.int32), 1 << 26, named, base)
-    return summed_over_wide(partial), slots, maps
+    return partial, named, slots, base
+
+
+def find(named, base, dec_weight):
+    tokens = named.shape[1]
+    return call(
+        maps_kernel,
+        (
+            array((2, tokens, LANES), jnp.int32),
+            array((2, CHUNK, LANES), jnp.int32),
+            array(dec_weight.shape[::-1], BF16),
+        ),
+        1 << 26,
+        lax.axis_index(WIDE)[None],
+        named,
+        base,
+        dec_weight,
+        in_specs=specs(pltpu.SMEM, pltpu.VMEM, pltpu.VMEM, pltpu.VMEM),
+    )
 
 
 def decode(few, preact, maps, target, enc_bias, dec_weight):
@@ -298,10 +355,24 @@
         maps,
         enc_bias[None],
         dec_weight,
+        in_specs=specs(pltpu.VMEM, pltpu.VMEM, pltpu.VMEM, pl.ANY),
+        out_specs=specs(pltpu.VMEM, pl.ANY),
+        scratch_shapes=[
+            pltpu.VMEM(dec_weight.shape, BF16),
+            pltpu.VMEM((tokens, channels), BF16),
+            pltpu.SemaphoreType.DMA((4,)),
+            pltpu.SemaphoreType.DMA((4,)),
+        ],
     )
     sizes = sizes_of(NARROW)
     recs = swap_from_far(rec.reshape(-1, *target.shape), NARROW, sizes)
-    mixed = call(functools.partial(mix_kernel, sizes), array(recs.shape, BF16), 8 * recs.size, recs, target)
+    mixed = call(
+        functools.partial(mix_kernel, sizes),
+        array(recs.shape, BF16),
+        8 * recs.size,
+        recs,
+        target,
+    )
     return latents, swap_from_far(mixed, NARROW, sizes).reshape(tokens, channels)
 
 
@@ -316,22 +387,21 @@
     )
 
 
-def finish(few, grads, back, latents, maps):
-    wide = lax.axis_size(WIDE)
-    parts = swap_from_far(grads, WIDE, [wide])
-    dec_grad = lax.dot_general(
-        latents, back, (((0,), (0,)), ((), ())), preferred_element_type=F32
-    ).astype(BF16)
-    own_rows = maps.shape[1] // wide
-    own_maps = lax.dynamic_slice_in_dim(maps, lax.axis_index(WIDE) * own_rows, own_rows, 1)
-    latent_grad = call(
-        functools.partial(own_kernel, few),
-        array((own_rows, latents.shape[1]), F32),
-        1 << 20,
-        parts,
-        own_maps,
-    )
-    return dec_grad, latent_grad
+def outer(latents, back):
+    shape = (latents.shape[1], back.shape[1])
+    return call(
+        outer_kernel,
+        array(shape, BF16),
+        2 * latents.size * back.shape[1],
+        latents,
+        back,
+        out_specs=specs(pl.ANY)[0],
+        scratch_shapes=[pltpu.VMEM(shape, BF16), pltpu.SemaphoreType.DMA((4,))],
+    )
+
+
+def own_gradient(few, parts, own, width):
+    return call(functools.partial(own_kernel, few), array((CHUNK, width), F32), 1 << 20, parts, own)
 
 
 def local(activations, enc_weight, enc_bias, dec_weight, dec_bias, active_ids):
@@ -339,35 +409,37 @@
     width = enc_weight.shape[1]
     group = lax.axis_index(NARROW)
     ids = active_ids.T
-    preact, slots, maps = encode(True, group[None], ids, activations, enc_weight)
-    needed = call(
-        functools.partial(count_kernel, width),
-        array((1,), jnp.int32),
+    partial, named, slots, base = encode(True, group[None], ids, activations, enc_weight)
+    preact = summed_over_wide(partial)
+    maps, own, turned_weight = find(named, base, dec_weight)
+    rows = tokens // lax.axis_size(NARROW)
+    target, needed = call(
+        functools.partial(target_kernel, width),
+        (array((rows, channels), F32), array((1,), jnp.int32)),
         1 << 24,
-        ids,
-        out_specs=specs(pltpu.SMEM)[0],
-    )
-    target = call(
-        target_kernel,
-        array((tokens // lax.axis_size(NARROW), channels), F32),
-        1 << 20,
         turned(group, sizes_of(NARROW))[None],
         activations,
         dec_bias[None],
-        in_specs=specs(pltpu.SMEM, pltpu.VMEM, pltpu.VMEM),
-    )
-    turned_weight = call(turn_kernel, array((channels, width), BF16), 1 << 26, dec_weight)
+        ids,
+        in_specs=specs(pltpu.SMEM, pl.ANY, pltpu.VMEM, pltpu.VMEM),
+        out_specs=specs(pltpu.VMEM, pltpu.SMEM),
+        scratch_shapes=[pltpu.VMEM((rows, channels), BF16), pltpu.SemaphoreType.DMA],
+    )
+    wide = [lax.axis_size(WIDE)]
     latents, back = decode(True, preact, maps, target, enc_bias, dec_weight)
-
-    grads = latent_parts(True, back, turned_weight, slots)
+    parts = swap_from_far(latent_parts(True, back, turned_weight, slots), WIDE, wide)
+    dec_grad = outer(latents, back)
 
     def few():
-        return finish(True, grads, back, latents, maps)
+        return dec_grad, own_gradient(True, parts, own, width)
 
     def many():
-        preact, slots, maps = encode(False, group[None], ids, activations, enc_weight)
+        partial, named, slots, base = encode(False, group[None], ids, activations, enc_weight)
+        preact = summed_over_wide(partial)
+        maps, own, turned_weight = find(named, base, dec_weight)
         latents, back = decode(False, preact, maps, target, enc_bias, dec_weight)
-        return finish(False, latent_parts(False, back, turned_weight, slots), back, latents, maps)
+        parts = swap_from_far(latent_parts(False, back, turned_weight, slots), WIDE, wide)
+        return outer(latents, back), own_gradient(False, parts, own, width)
 
     return lax.cond(needed[0] <= LANES, few, many)
 

time: 87.9 us -> 85.2 us (0.969)
  blocking collectives: 10.7 us -> 22.7 us
  waiting for transfers between devices: 12.1 us -> 5.28 us
  starting transfers between devices: 43.7 us -> 36.9 us
  matrix products: 3.07 us -> 0 us
  Pallas kernels: 15 us -> 16.9 us
    all_to_all x0 -> x1, blocking collectives: none -> 12 us  [swap_from_far(): return lax.all_to_all(pieces, axes, 0, 0, axis_index_groups=order)]
    all_to_all x4 -> x3, starting transfers between devices: 43.7 us -> 36.9 us  [swap_from_far(): return lax.all_to_all(pieces, axes, 0, 0, axis_index_groups=order)]
    all_to_all x4 -> x3, waiting for transfers between devices: 12.1 us -> 5.28 us  [swap_from_far(): return lax.all_to_all(pieces, axes, 0, 0, axis_index_groups=order)]
    dot_general x1 -> x0, matrix products: 3.07 us -> none  [finish(): lax.dot_general(latents, back, (((0,), (0,)), ((), ())), preferred_elemen...]
    pallas_call x9 -> x8, Pallas kernels: 15 us -> 16.9 us  [call(): pl.pallas_call(kernel, out_shape=shapes, compiler_params=pltpu.CompilerPa...]
  transfers between devices with their start and end apart: 4 -> 3, of which waited for: 3 -> 2; matrix products, arithmetic and copies ran while one was open for 4% -> 0% of each run, Pallas kernels for 3% -> 8%
where the time goes in v7:
time: 85.2 us; the launch traced here: 84.7 us
  starting transfers between devices  36.9 us (43%)
  blocking collectives  22.7 us (27%)
  Pallas kernels  16.9 us (20%)
  waiting for transfers between devices  5.28 us (6%)
  local copies, waits for them, and re-layouts  1.33 us (2%)
  between operations  1.3 us (2%)
    all_to_all x3, starting transfers between devices, swap_from_far(): return lax.all_to_all(pieces, axes, 0, 0, axis_index_groups=order)  36.9 us
    pallas_call x8, Pallas kernels, call(): pl.pallas_call(kernel, out_shape=shapes, compiler_params=pltpu.CompilerPa...  16.9 us
    all_to_all x1, blocking collectives, swap_from_far(): return lax.all_to_all(pieces, axes, 0, 0, axis_index_groups=order)  12 us
    all_gather x1, blocking collectives, summed_over_wide(): both = lax.all_gather(partial, core)  8.37 us
    all_to_all x3, waiting for transfers between devices, swap_from_far(): return lax.all_to_all(pieces, axes, 0, 0, axis_index_groups=order)  5.28 us
    all_gather x1, blocking collectives, summed_over_wide(): return lax.all_gather(jnp.sum(pieces.astype(F32), axis=0), core, tiled=True)  2.34 us
  transfers between devices with their start and end apart: 3, of which 2 were waited for; matrix products, arithmetic and copies ran while one was open for 0% of the time, Pallas kernels for 8%

profile of v7, /device:TPU:1, one launch (start us, length us, event | category | flops | bytes accessed | tf_op | source)
XLA Modules:
  0.0 84.7 jit_solution(11260403284811241199)
XLA Ops:
  0.6 4.6 %shard_map.82 = (f32[32,128]{1,0:T(8,128)S(1)}, s32[16,512]{1,0:T(8,128)S(1)}, s32[512,128]{1,0:T(8,128)S(1)}, s32[8,512]{1,0:T(8,128)S(1)}) custom-call(s32[1]{0:T(128)} %bitcast.11.group, s32[64,512]{1,0:T(8,128)} %bitcast.27, bf16[512,512]{1,0:T(8,128)(2,1)} %act.3, bf16[512,1024]{1,0:T(8,128)(2,1)} %weight.3), custom_call_target="tpu_custom_call" | custom-call | flops 536870912 | bytes 2031620 | tf_op jit(solution)/shard_map/pallas_call | solution.py:257
  5.2 8.4 %all-gather.1 = f32[64,128]{1,0:T(8,128)S(1)} all-gather(f32[32,128]{1,0:T(8,128)S(1)} %get-tuple-element.54), channel_id=3, replica_groups=mesh['wide_0'=16,'wide_1'=2,'narrow_0'=4,'narrow_1'=4] {'wide_1'}, dimensions={0}, use_global_device_ids=true | all-gather | bytes 49152 | tf_op jit(solution)/shard_map/all_gather | solution.py:290
  13.6 0.6 broadcast_in_dim.44
  14.2 12.9 %all-to-all-start.4 = ((bf16[16,16,128]{2,1,0:T(8,128)(2,1)}), bf16[16,16,128]{2,1,0:T(8,128)(2,1)S(1)}, u32[]{:S(2)}, u32[]{:S(2)}) async-start(bf16[16,16,128]{2,1,0:T(8,128)(2,1)} %broadcast_in_dim.44), calls=%async_computation.4 | async-start | bytes 131072 | tf_op jit(solution)/shard_map/all_to_all | solution.py:284
  27.1 2.9 %shard_map.83 = (s32[2,512,128]{2,1,0:T(8,128)S(1)}, s32[2,16,128]{2,1,0:T(8,128)S(1)}, bf16[512,1024]{1,0:T(8,128)(2,1)S(1)}) custom-call(s32[1]{0:T(128)} %bitcast.14.owner, s32[16,512]{1,0:T(8,128)S(1)} %get-tuple-element.55.named, s32[8,512]{1,0:T(8,128)S(1)} %get-tuple-element.56.base, bf16[1024,512]{1,0:T(8,128)(2,1)} %weight.5), custom_call_target="tpu_custom_call" | custom-call | flops 67108864 | bytes 2686980 | tf_op jit(solution)/shard_map/pallas_call | solution.py:257
  30.0 1.2 %all-to-all-done.4 = bf16[16,16,128]{2,1,0:T(8,128)(2,1)S(1)} async-done(((bf16[16,16,128]{2,1,0:T(8,128)(2,1)}), bf16[16,16,128]{2,1,0:T(8,128)(2,1)S(1)}, u32[]{:S(2)}, u32[]{:S(2)}) %all-to-all-start.4) | async-done | bytes 65568 | tf_op jit(solution)/shard_map/all_to_all | solution.py:284
  31.2 0.0 copy-start.3
  31.3 2.3 %all_gather.20.packed = f32[32,128]{1,0:T(8,128)S(1)} all-gather(f32[16,128]{1,0:T(8,128)S(1)} %convert_reduce_fusion.1), channel_id=1, replica_groups=mesh['wide_0'=16,'wide_1'=2,'narrow_0'=4,'narrow_1'=4] {'wide_1'}, dimensions={0}, use_global_device_ids=true | all-gather | bytes 24576 | tf_op jit(solution)/shard_map/all_gather | solution.py:295
  33.6 0.0 copy-done.3
  33.6 2.9 %shard_map.84 = (bf16[512,1024]{1,0:T(8,128)(2,1)S(1)}, bf16[512,512]{1,0:T(8,128)(2,1)}) custom-call(f32[32,128]{1,0:T(8,128)S(1)} %all_gather.20.packed, s32[2,512,128]{2,1,0:T(8,128)S(1)} %get-tuple-element.57.maps, f32[1,1024]{1,0:T(1,128)S(1)} %bitcast.31, bf16[1024,512]{1,0:T(8,128)(2,1)} %weight.5), custom_call_target="tpu_custom_call" | custom-call | flops 536870912 | bytes 3166208 | tf_op jit(solution)/shard_map/pallas_call | solution.py:257
  36.5 0.0 copy-start.1
  36.5 8.9 %all-to-all-start.5 = ((bf16[16,32,512]{2,1,0:T(8,128)(2,1)}), bf16[16,32,512]{2,1,0:T(8,128)(2,1)S(1)}, u32[]{:S(2)}, u32[]{:S(2)}) async-start(bf16[16,32,512]{2,1,0:T(8,128)(2,1)} %bitcast.16), calls=%async_computation.5 | async-start | bytes 1048576 | tf_op jit(solution)/shard_map/all_to_all | solution.py:284
  45.4 0.0 copy-start
  45.4 0.0 copy-done.1
  45.4 0.7 copy-done
  46.1 2.2 %shard_map.81 = (f32[32,512]{1,0:T(8,128)S(1)}, s32[1]{0:T(128)}) custom-call(s32[1]{0:T(128)} %bitcast.7.place_of, bf16[512,512]{1,0:T(8,128)(2,1)S(1)} %copy-done.1, f32[1,512]{1,0:T(1,128)S(1)} %bitcast.25, s32[64,512]{1,0:T(8,128)} %bitcast.28), custom_call_target="tpu_custom_call" | custom-call | flops 16777216 | bytes 722952 | tf_op jit(solution)/shard_map/pallas_call | solution.py:257
  48.3 4.1 %all-to-all-done.5.recs = bf16[16,32,512]{2,1,0:T(8,128)(2,1)S(1)} async-done(((bf16[16,32,512]{2,1,0:T(8,128)(2,1)}), bf16[16,32,512]{2,1,0:T(8,128)(2,1)S(1)}, u32[]{:S(2)}, u32[]{:S(2)}) %all-to-all-start.5) | async-done | bytes 524320 | tf_op jit(solution)/shard_map/all_to_all | solution.py:284
  52.4 0.2 shard_map.85
  52.6 12.0 %all_to_all.38 = bf16[16,32,512]{2,1,0:T(8,128)(2,1)S(1)} all-to-all(bf16[16,32,512]{2,1,0:T(8,128)(2,1)S(1)} %shard_map.85), channel_id=1, replica_groups={{10,11,8,9,14,15,12,13,2,3,0,1,6,7,4,5},{26,27,24,25,30,31,28,29,18,19,..., dimensions={0} | all-to-all | bytes 1048576 | tf_op jit(solution)/shard_map/all_to_all | solution.py:284
  64.6 2.0 %shard_map.86 = f32[32,1,128]{2,1,0:T(1,128)} custom-call(bf16[512,512]{1,0:T(8,128)(2,1)S(1)} %bitcast.20, bf16[512,1024]{1,0:T(8,128)(2,1)S(1)} %get-tuple-element.59.turned_weight, s32[512,128]{1,0:T(8,128)S(1)} %get-tuple-element.60.slots), custom_call_target="tpu_custom_call" | custom-call | flops 536870912 | bytes 1851392 | tf_op jit(solution)/shard_map/pallas_call | solution.py:257
  66.5 15.0 %all-to-all-start.7 = ((f32[32,1,128]{2,1,0:T(1,128)}), f32[32,1,128]{2,1,0:T(1,128)S(1)}, u32[]{:S(2)}, u32[]{:S(2)}) async-start(f32[32,1,128]{2,1,0:T(1,128)} %shard_map.86), calls=%async_computation.7 | async-start | bytes 32768 | tf_op jit(solution)/shard_map/all_to_all | solution.py:284
  82.1 0.0 copy-start.2
  82.1 1.5 %shard_map.87 = bf16[1024,512]{1,0:T(8,128)(2,1)} custom-call(bf16[512,1024]{1,0:T(8,128)(2,1)S(1)} %get-tuple-element.62.latents, bf16[512,512]{1,0:T(8,128)(2,1)S(1)} %bitcast.21), custom_call_target="tpu_custom_call" | custom-call | flops 536870912 | bytes 2621440 | tf_op jit(solution)/shard_map/pallas_call | solution.py:257
  83.6 0.0 all-to-all-done.7
  83.6 0.0 copy-done.2
  83.6 1.0 %conditional.1 = (bf16[1024,512]{1,0:T(8,128)(2,1)}, f32[16,1024]{1,0:T(8,128)}) conditional(s32[]{:T(128)} %bitcast.10, (s32[]{:T(128)}, s32[64,512]{1,0:T(8,128)S(1)}, bf16[512,512]{1,0:T(8,128)(2,1)S(1)}, bf16[512,1024]{1,0:T(8,128)(2,1)}, bf16[1024,512]{1,0:T(8,128)(2,1)}, /*index=5*/f32[1024]{0:T(1024)S(1)}, f32[32,512]{1,0:T(8,128)S(1)}) %tuple.25, ...), branch_computations={%region_1.3_spmd, %region_3.4_spmd} | conditional | flops 2218278912 | bytes 20189426 | solution.py:444
  83.9 0.8 branch_1_fun.1
  (2 shorter events, 0.0 us)
Async XLA Ops:
  14.2 17.0 %all-to-all-start.4 = ((bf16[16,16,128]{2,1,0:T(8,128)(2,1)}), bf16[16,16,128]{2,1,0:T(8,128)(2,1)S(1)}, u32[]{:S(2)}, u32[]{:S(2)}) async-start(bf16[16,16,128]{2,1,0:T(8,128)(2,1)} %broadcast_in_dim.44), calls=%async_computation.4 | async-start | bytes 131072 | tf_op jit(solution)/shard_map/all_to_all | solution.py:284
  31.2 2.4 %copy-start.3 = (f32[1024]{0:T(1024)S(1)}, f32[1024]{0:T(1024)}, u32[]{:S(2)}) copy-start(f32[1024]{0:T(1024)} %param.10) | copy-start | bytes 12292
  36.5 9.0 %copy-start.1 = (bf16[512,512]{1,0:T(8,128)(2,1)S(1)}, bf16[512,512]{1,0:T(8,128)(2,1)}, u32[]{:S(2)}) copy-start(bf16[512,512]{1,0:T(8,128)(2,1)} %act.3) | copy-start | bytes 1572868
  36.5 15.9 %all-to-all-start.5 = ((bf16[16,32,512]{2,1,0:T(8,128)(2,1)}), bf16[16,32,512]{2,1,0:T(8,128)(2,1)S(1)}, u32[]{:S(2)}, u32[]{:S(2)}) async-start(bf16[16,32,512]{2,1,0:T(8,128)(2,1)} %bitcast.16), calls=%async_computation.5 | async-start | bytes 1048576 | tf_op jit(solution)/shard_map/all_to_all | solution.py:284
  45.4 0.7 copy-start
  66.5 17.1 %all-to-all-start.7 = ((f32[32,1,128]{2,1,0:T(1,128)}), f32[32,1,128]{2,1,0:T(1,128)S(1)}, u32[]{:S(2)}, u32[]{:S(2)}) async-start(f32[32,1,128]{2,1,0:T(1,128)} %shard_map.86), calls=%async_computation.7 | async-start | bytes 32768 | tf_op jit(solution)/shard_map/all_to_all | solution.py:284
  82.1 1.5 %copy-start.2 = (s32[512,64]{0,1:T(8,128)S(1)}, s32[512,64]{0,1:T(8,128)}, u32[]{:S(2)}) copy-start(s32[512,64]{0,1:T(8,128)} %param.13) | copy-start | bytes 393220

commit v8 on v7

--- a/solution.py
+++ b/solution.py
@@ -23,14 +23,22 @@
     return jnp.take_along_axis(rows, lanes, axis=1, mode="promise_in_bounds")
 
 
-def pick_slots(rows, slots, few):
+def pick_more(picked, rows, first, slots):
     low, high = slots & (LANES - 1), slots >> 7
-    picked = jnp.zeros(slots.shape, F32)
     for c in range(rows.shape[1] // LANES):
-        picked = jnp.where(high == c, lookup(rows[:, c * LANES : (c + 1) * LANES], low), picked)
+        found = lookup(rows[:, c * LANES : (c + 1) * LANES], low)
+        picked = jnp.where(high == first // LANES + c, found, picked)
+    return picked
+
+
+def pack(picked, few):
     picked = picked.reshape(-1, 2, 8, LANES)
     picked = picked[:, 0] + picked[:, 1]
     return jnp.sum(picked, axis=1, keepdims=True) if few else picked
+
+
+def pick_slots(rows, slots, few):
+    return pack(pick_more(jnp.zeros(slots.shape, F32), rows, 0, slots), few)
 
 
 def unpack_rows(packed, few):
@@ -142,24 +150,42 @@
         turned_weight[:, pl.ds(r, 256)] = weight[pl.ds(r, 256), :].T
 
 
-def encode_kernel(few, group, ids, act, weight, packed, named, slots, base, act_here, weight_here, arrived):
-    copies = []
-    for n, (array, here) in enumerate(((act, act_here), (weight, weight_here))):
-        step = array.shape[0] // 4
-        for i in range(4):
+def window_kernel(
+    width, owner, named, base, weight, place_of, act, bias, ids, out, own, turned_weight, target, most, *scratch
+):
+    maps_kernel(owner, named, base, weight, out, own, turned_weight)
+    target_kernel(width, place_of, act, bias, ids, target, most, *scratch)
+
+
+def encode_kernel(
+    few, group, ids, act, weight, packed, named, slots, base, act_here, weight_here, picked, arrived
+):
+    width = weight.shape[1]
+    block = width // 4
+    copies = [pltpu.make_async_copy(act, act_here, arrived.at[4])]
+    for n in range(4):
+        cols = pl.ds(n * block, block)
+        copies.append(pltpu.make_async_copy(weight.at[:, cols], weight_here.at[:, cols], arrived.at[n]))
+    for copy in copies:
+        copy.start()
+    fill_slots(few, group[0], width, ids, named, slots, base)
+    copies[0].wait()
+    step = 8 * CHUNK
+    for n in range(4):
+        copies[n + 1].wait()
+        for i in range(act.shape[0] // step):
             rows = pl.ds(i * step, step)
-            copies.append(pltpu.make_async_copy(array.at[rows], here.at[rows], arrived.at[4 * n + i]))
-            copies[-1].start()
-    fill_slots(few, group[0], weight.shape[1], ids, named, slots, base)
-    for copy in copies:
-        copy.wait()
-    step = 8 * CHUNK
-    for i in range(act.shape[0] // step):
-        rows = pl.ds(i * step, step)
-        part = jnp.dot(act_here[rows, :], weight_here[...], preferred_element_type=F32)
-        picked = pick_slots(part, slots[rows, :], few)
-        depth = 8 * picked.shape[1]
-        packed[pl.ds(i * depth, depth), :] = picked.reshape(depth, LANES)
+            part = jnp.dot(
+                act_here[rows, :], weight_here[:, pl.ds(n * block, block)], preferred_element_type=F32
+            )
+            sofar = picked[rows, :] if n else jnp.zeros((step, LANES), F32)
+            sofar = pick_more(sofar, part, n * block, slots[rows, :])
+            if n < 3:
+                picked[rows, :] = sofar
+            else:
+                done = pack(sofar, few)
+                depth = 8 * done.shape[1]
+                packed[pl.ds(i * depth, depth), :] = done.reshape(depth, LANES)
 
 
 def decode_kernel(few, packed, maps, bias, weight, latents, rec, weight_here, rec_here, arrived, sent):
@@ -316,31 +342,46 @@
         ids,
         activations,
         enc_weight,
-        in_specs=specs(pltpu.SMEM, pltpu.VMEM, pl.ANY, pl.ANY),
+        in_specs=specs(pltpu.SMEM, pltpu.VMEM, pltpu.HBM, pltpu.HBM),
         scratch_shapes=[
             pltpu.VMEM(activations.shape, BF16),
             pltpu.VMEM(enc_weight.shape, BF16),
-            pltpu.SemaphoreType.DMA((8,)),
+            pltpu.VMEM((tokens, LANES), F32),
+            pltpu.SemaphoreType.DMA((5,)),
         ],
     )
     return partial, named, slots, base
 
 
-def find(named, base, dec_weight):
+def find(named, base, dec_weight, *rest):
     tokens = named.shape[1]
+    width, channels = dec_weight.shape
+    shapes = (
+        array((2, tokens, LANES), jnp.int32),
+        array((2, CHUNK, LANES), jnp.int32),
+        array((channels, width), BF16),
+    )
+    ins, outs = [pltpu.SMEM] + [pltpu.VMEM] * 3, [pltpu.VMEM] * 3
+    kernel, scratch = maps_kernel, []
+    if rest:
+        rows = tokens // lax.axis_size(NARROW)
+        shapes += (array((rows, channels), F32), array((1,), jnp.int32))
+        ins += [pltpu.SMEM, pltpu.HBM, pltpu.VMEM, pltpu.VMEM]
+        outs += [pltpu.VMEM, pltpu.SMEM]
+        kernel = functools.partial(window_kernel, width)
+        scratch = [pltpu.VMEM((rows, channels), BF16), pltpu.SemaphoreType.DMA]
     return call(
-        maps_kernel,
-        (
-            array((2, tokens, LANES), jnp.int32),
-            array((2, CHUNK, LANES), jnp.int32),
-            array(dec_weight.shape[::-1], BF16),
-        ),
+        kernel,
+        shapes,
         1 << 26,
         lax.axis_index(WIDE)[None],
         named,
         base,
         dec_weight,
-        in_specs=specs(pltpu.SMEM, pltpu.VMEM, pltpu.VMEM, pltpu.VMEM),
+        *rest,
+        in_specs=specs(*ins),
+        out_specs=specs(*outs),
+        scratch_shapes=scratch,
     )
 
 
@@ -355,7 +396,7 @@
         maps,
         enc_bias[None],
         dec_weight,
-        in_specs=specs(pltpu.VMEM, pltpu.VMEM, pltpu.VMEM, pl.ANY),
+        in_specs=specs(pltpu.VMEM, pltpu.VMEM, pltpu.VMEM, pltpu.HBM),
         out_specs=specs(pltpu.VMEM, pl.ANY),
         scratch_shapes=[
             pltpu.VMEM(dec_weight.shape, BF16),
@@ -405,25 +446,14 @@
 
 
 def local(activations, enc_weight, enc_bias, dec_weight, dec_bias, active_ids):
-    tokens, channels = activations.shape
     width = enc_weight.shape[1]
     group = lax.axis_index(NARROW)
     ids = active_ids.T
     partial, named, slots, base = encode(True, group[None], ids, activations, enc_weight)
     preact = summed_over_wide(partial)
-    maps, own, turned_weight = find(named, base, dec_weight)
-    rows = tokens // lax.axis_size(NARROW)
-    target, needed = call(
-        functools.partial(target_kernel, width),
-        (array((rows, channels), F32), array((1,), jnp.int32)),
-        1 << 24,
-        turned(group, sizes_of(NARROW))[None],
-        activations,
-        dec_bias[None],
-        ids,
-        in_specs=specs(pltpu.SMEM, pl.ANY, pltpu.VMEM, pltpu.VMEM),
-        out_specs=specs(pltpu.VMEM, pltpu.SMEM),
-        scratch_shapes=[pltpu.VMEM((rows, channels), BF16), pltpu.SemaphoreType.DMA],
+    place_of = turned(group, sizes_of(NARROW))[None]
+    maps, own, turned_weight, target, needed = find(
+        named, base, dec_weight, place_of, activations, dec_bias[None], ids
     )
     wide = [lax.axis_size(WIDE)]
     latents, back = decode(True, preact, maps, target, enc_bias, dec_weight)

time: 85.2 us -> 85.2 us (level)
  blocking collectives: 22.7 us -> 37.1 us
  starting transfers between devices: 36.9 us -> 27.8 us
  waiting for transfers between devices: 5.28 us -> 0.01 us
    all_to_all x1 -> x2, blocking collectives: 12 us -> 26.3 us  [swap_from_far(): return lax.all_to_all(pieces, axes, 0, 0, axis_index_groups=order)]
    all_to_all x3 -> x2, starting transfers between devices: 36.9 us -> 27.8 us  [swap_from_far(): return lax.all_to_all(pieces, axes, 0, 0, axis_index_groups=order)]
    all_to_all x3 -> x2, waiting for transfers between devices: 5.28 us -> 0.01 us  [swap_from_far(): return lax.all_to_all(pieces, axes, 0, 0, axis_index_groups=order)]
    pallas_call x8 -> x7, Pallas kernels: 16.9 us -> 16.8 us  [call(): pl.pallas_call(kernel, out_shape=shapes, compiler_params=pltpu.CompilerPa...]
  transfers between devices with their start and end apart: 3 -> 2, of which waited for: 2 -> 0; matrix products, arithmetic and copies ran while one was open for 0% -> 0% of each run, Pallas kernels for 8% -> 7%
where the time goes in v8:
time: 85.2 us; the launch traced here: 84.7 us
  blocking collectives  37.1 us (44%)
  starting transfers between devices  27.8 us (33%)
  Pallas kernels  16.8 us (20%)
  between operations  1.4 us (2%)
  local copies, waits for them, and re-layouts  1.32 us (2%)
    all_to_all x2, starting transfers between devices, swap_from_far(): return lax.all_to_all(pieces, axes, 0, 0, axis_index_groups=order)  27.8 us
    all_to_all x2, blocking collectives, swap_from_far(): return lax.all_to_all(pieces, axes, 0, 0, axis_index_groups=order)  26.3 us
    pallas_call x7, Pallas kernels, call(): pl.pallas_call(kernel, out_shape=shapes, compiler_params=pltpu.CompilerPa...  16.8 us
    all_gather x1, blocking collectives, summed_over_wide(): both = lax.all_gather(partial, core)  8.38 us
    all_gather x1, blocking collectives, summed_over_wide(): return lax.all_gather(jnp.sum(pieces.astype(F32), axis=0), core, tiled=True)  2.39 us
  transfers between devices with their start and end apart: 2, of which 0 were waited for; matrix products, arithmetic and copies ran while one was open for 0% of the time, Pallas kernels for 7%

profile of v8, /device:TPU:1, one launch (start us, length us, event | category | flops | bytes accessed | tf_op | source)
XLA Modules:
  0.0 84.7 jit_solution(6590373591084223501)
XLA Ops:
  0.6 0.0 copy-start.1
  0.6 4.7 %shard_map.81 = (f32[32,128]{1,0:T(8,128)S(1)}, s32[16,512]{1,0:T(8,128)S(1)}, s32[512,128]{1,0:T(8,128)S(1)}, s32[8,512]{1,0:T(8,128)S(1)}) custom-call(s32[1]{0:T(128)} %bitcast.8.group, s32[64,512]{1,0:T(8,128)} %bitcast.28, bf16[512,512]{1,0:T(8,128)(2,1)} %act.3, bf16[512,1024]{1,0:T(8,128)(2,1)} %weight.3), custom_call_target="tpu_custom_call" | custom-call | flops 536870912 | bytes 2031620 | tf_op jit(solution)/shard_map/pallas_call | solution.py:283
  5.4 8.4 %all-gather.1 = f32[64,128]{1,0:T(8,128)S(1)} all-gather(f32[32,128]{1,0:T(8,128)S(1)} %get-tuple-element.56), channel_id=3, replica_groups=mesh['wide_0'=16,'wide_1'=2,'narrow_0'=4,'narrow_1'=4] {'wide_1'}, dimensions={0}, use_global_device_ids=true | all-gather | bytes 49152 | tf_op jit(solution)/shard_map/all_gather | solution.py:316
  13.8 0.6 broadcast_in_dim.45
  14.4 0.0 copy-start.2
  14.4 13.0 %all-to-all-start.4 = ((bf16[16,16,128]{2,1,0:T(8,128)(2,1)}), bf16[16,16,128]{2,1,0:T(8,128)(2,1)S(1)}, u32[]{:S(2)}, u32[]{:S(2)}) async-start(bf16[16,16,128]{2,1,0:T(8,128)(2,1)} %broadcast_in_dim.45), calls=%async_computation.4 | async-start | bytes 131072 | tf_op jit(solution)/shard_map/all_to_all | solution.py:310
  27.5 0.0 copy-start
  27.5 0.0 copy-done.1
  27.5 0.0 copy-done.2
  27.5 0.7 copy-done
  28.1 4.2 %shard_map.82 = (s32[2,512,128]{2,1,0:T(8,128)S(1)}, s32[2,16,128]{2,1,0:T(8,128)S(1)}, bf16[512,1024]{1,0:T(8,128)(2,1)S(1)}, f32[32,512]{1,0:T(8,128)S(1)}, s32[1]{0:T(128)}) custom-call(s32[1]{0:T(128)} %bitcast.7.owner, s32[16,512]{1,0:T(8,128)S(1)} %get-tuple-element.52.named, s32[8,512]{1,0:T(8,128)S(1)} %get-tuple-element.53.base, ...), custom_call_target="tpu_custom_call" | custom-call | flops 67108864 | bytes 3409932 | tf_op jit(solution)/shard_map/pallas_call | solution.py:283
  32.3 0.0 all-to-all-done.4
  32.4 0.0 copy-start.4
  32.4 2.4 %all_gather.20.packed = f32[32,128]{1,0:T(8,128)S(1)} all-gather(f32[16,128]{1,0:T(8,128)S(1)} %convert_reduce_fusion.1), channel_id=1, replica_groups=mesh['wide_0'=16,'wide_1'=2,'narrow_0'=4,'narrow_1'=4] {'wide_1'}, dimensions={0}, use_global_device_ids=true | all-gather | bytes 24576 | tf_op jit(solution)/shard_map/all_gather | solution.py:321
  34.8 0.0 copy-done.4
  34.8 3.5 %shard_map.83 = (bf16[512,1024]{1,0:T(8,128)(2,1)S(1)}, bf16[512,512]{1,0:T(8,128)(2,1)S(1)}) custom-call(f32[32,128]{1,0:T(8,128)S(1)} %all_gather.20.packed, s32[2,512,128]{2,1,0:T(8,128)S(1)} %get-tuple-element.57.maps, f32[1,1024]{1,0:T(1,128)S(1)} %bitcast.32, bf16[1024,512]{1,0:T(8,128)(2,1)} %weight.5), custom_call_target="tpu_custom_call" | custom-call | flops 536870912 | bytes 3166208 | tf_op jit(solution)/shard_map/pallas_call | solution.py:283
  38.3 14.1 %all_to_all.38.recs = bf16[16,32,512]{2,1,0:T(8,128)(2,1)S(1)} all-to-all(bf16[16,32,512]{2,1,0:T(8,128)(2,1)S(1)} %bitcast.24), channel_id=1, replica_groups={{10,11,8,9,14,15,12,13,2,3,0,1,6,7,4,5},{26,27,24,25,30,31,28,29,18,19,..., dimensions={0} | all-to-all | bytes 1048576 | tf_op jit(solution)/shard_map/all_to_all | solution.py:310
  52.4 0.2 shard_map.84
  52.5 12.2 %all_to_all.39 = bf16[16,32,512]{2,1,0:T(8,128)(2,1)S(1)} all-to-all(bf16[16,32,512]{2,1,0:T(8,128)(2,1)S(1)} %shard_map.84), channel_id=1, replica_groups={{10,11,8,9,14,15,12,13,2,3,0,1,6,7,4,5},{26,27,24,25,30,31,28,29,18,19,..., dimensions={0} | all-to-all | bytes 1048576 | tf_op jit(solution)/shard_map/all_to_all | solution.py:310
  64.8 2.0 %shard_map.85 = f32[32,1,128]{2,1,0:T(1,128)} custom-call(bf16[512,512]{1,0:T(8,128)(2,1)S(1)} %bitcast.20, bf16[512,1024]{1,0:T(8,128)(2,1)S(1)} %get-tuple-element.59.turned_weight, s32[512,128]{1,0:T(8,128)S(1)} %get-tuple-element.60.slots), custom_call_target="tpu_custom_call" | custom-call | flops 536870912 | bytes 1851392 | tf_op jit(solution)/shard_map/pallas_call | solution.py:283
  66.7 14.8 %all-to-all-start.7 = ((f32[32,1,128]{2,1,0:T(1,128)}), f32[32,1,128]{2,1,0:T(1,128)S(1)}, u32[]{:S(2)}, u32[]{:S(2)}) async-start(f32[32,1,128]{2,1,0:T(1,128)} %shard_map.85), calls=%async_computation.7 | async-start | bytes 32768 | tf_op jit(solution)/shard_map/all_to_all | solution.py:310
  82.2 0.0 copy-start.3
  82.2 1.5 %shard_map.86 = bf16[1024,512]{1,0:T(8,128)(2,1)} custom-call(bf16[512,1024]{1,0:T(8,128)(2,1)S(1)} %get-tuple-element.62.latents, bf16[512,512]{1,0:T(8,128)(2,1)S(1)} %bitcast.21), custom_call_target="tpu_custom_call" | custom-call | flops 536870912 | bytes 2621440 | tf_op jit(solution)/shard_map/pallas_call | solution.py:283
  83.7 0.0 all-to-all-done.7
  83.7 0.0 copy-done.3
  83.7 1.0 %conditional.1 = (bf16[1024,512]{1,0:T(8,128)(2,1)}, f32[16,1024]{1,0:T(8,128)}) conditional(s32[]{:T(128)} %bitcast.12, (s32[]{:T(128)}, s32[64,512]{1,0:T(8,128)S(1)}, bf16[512,512]{1,0:T(8,128)(2,1)S(1)}, bf16[512,1024]{1,0:T(8,128)(2,1)}, bf16[1024,512]{1,0:T(8,128)(2,1)}, /*index=5*/f32[1024]{0:T(1024)S(1)}, f32[32,512]{1,0:T(8,128)S(1)}) %tuple.25, ...), branch_computations={%region_1.3_spmd, %region_3.4_spmd} | conditional | flops 2218278912 | bytes 20189426 | solution.py:474
  83.9 0.8 branch_1_fun.1
  (2 shorter events, 0.0 us)
Async XLA Ops:
  0.6 26.8 %copy-start.1 = (bf16[512,512]{1,0:T(8,128)(2,1)S(1)}, bf16[512,512]{1,0:T(8,128)(2,1)}, u32[]{:S(2)}) copy-start(bf16[512,512]{1,0:T(8,128)(2,1)} %act.3) | copy-start | bytes 1572868
  14.4 13.1 %copy-start.2 = (s32[512,64]{0,1:T(8,128)S(1)}, s32[512,64]{0,1:T(8,128)}, u32[]{:S(2)}) copy-start(s32[512,64]{0,1:T(8,128)} %param.13) | copy-start | bytes 393220
  14.4 17.9 %all-to-all-start.4 = ((bf16[16,16,128]{2,1,0:T(8,128)(2,1)}), bf16[16,16,128]{2,1,0:T(8,128)(2,1)S(1)}, u32[]{:S(2)}, u32[]{:S(2)}) async-start(bf16[16,16,128]{2,1,0:T(8,128)(2,1)} %broadcast_in_dim.45), calls=%async_computation.4 | async-start | bytes 131072 | tf_op jit(solution)/shard_map/all_to_all | solution.py:310
  27.5 0.7 copy-start
  32.4 2.4 %copy-start.4 = (f32[1024]{0:T(1024)S(1)}, f32[1024]{0:T(1024)}, u32[]{:S(2)}) copy-start(f32[1024]{0:T(1024)} %param.10) | copy-start | bytes 12292
  66.7 17.0 %all-to-all-start.7 = ((f32[32,1,128]{2,1,0:T(1,128)}), f32[32,1,128]{2,1,0:T(1,128)S(1)}, u32[]{:S(2)}, u32[]{:S(2)}) async-start(f32[32,1,128]{2,1,0:T(1,128)} %shard_map.85), calls=%async_computation.7 | async-start | bytes 32768 | tf_op jit(solution)/shard_map/all_to_all | solution.py:310
  82.2 1.5 %copy-start.3 = (s32[512,64]{0,1:T(8,128)S(1)}, s32[512,64]{0,1:T(8,128)}, u32[]{:S(2)}) copy-start(s32[512,64]{0,1:T(8,128)} %param.13) | copy-start | bytes 393220

commit v9 on v8

--- a/solution.py
+++ b/solution.py
@@ -101,11 +101,7 @@
         slots[cols, :] = spread.T
 
 
-def target_kernel(width, place_of, act, bias, ids, out, most, here, arrived):
-    rows = out.shape[0]
-    first = pl.multiple_of(place_of[0] * rows, rows)
-    copy = pltpu.make_async_copy(act.at[pl.ds(first, rows)], here, arrived)
-    copy.start()
+def count_needed(width, ids, most):
     every = lax.broadcasted_iota(jnp.int32, (16, LANES), 0)
     needed = jnp.zeros((16, LANES), jnp.int32)
     for i in range(ids.shape[1] // LANES):
@@ -115,8 +111,6 @@
             tally = tally + jnp.where(every == owner[k : k + 1], 1, 0)
         needed = jnp.maximum(needed, jnp.maximum(tally * (LANES // FEW), up_to(tally)))
     most[0] = jnp.max(needed)
-    copy.wait()
-    out[...] = bias[...] - here[...].astype(F32)
 
 
 def maps_kernel(owner, named, base, weight, out, own, turned_weight):
@@ -150,22 +144,36 @@
         turned_weight[:, pl.ds(r, 256)] = weight[pl.ds(r, 256), :].T
 
 
-def window_kernel(
-    width, owner, named, base, weight, place_of, act, bias, ids, out, own, turned_weight, target, most, *scratch
-):
+def window_kernel(width, owner, named, base, weight, ids, out, own, turned_weight, most):
     maps_kernel(owner, named, base, weight, out, own, turned_weight)
-    target_kernel(width, place_of, act, bias, ids, target, most, *scratch)
+    count_needed(width, ids, most)
 
 
 def encode_kernel(
-    few, group, ids, act, weight, packed, named, slots, base, act_here, weight_here, picked, arrived
+    few,
+    group,
+    place_of,
+    ids,
+    act,
+    weight,
+    bias,
+    packed,
+    named,
+    slots,
+    base,
+    target,
+    act_here,
+    weight_here,
+    picked,
+    arrived,
 ):
     width = weight.shape[1]
     block = width // 4
-    copies = [pltpu.make_async_copy(act, act_here, arrived.at[4])]
+    pairs = [(act, act_here)]
     for n in range(4):
         cols = pl.ds(n * block, block)
-        copies.append(pltpu.make_async_copy(weight.at[:, cols], weight_here.at[:, cols], arrived.at[n]))
+        pairs.append((weight.at[:, cols], weight_here.at[:, cols]))
+    copies = [pltpu.make_async_copy(*pair, arrived.at[n]) for n, pair in enumerate(pairs)]
     for copy in copies:
         copy.start()
     fill_slots(few, group[0], width, ids, named, slots, base)
@@ -186,9 +194,12 @@
                 done = pack(sofar, few)
                 depth = 8 * done.shape[1]
                 packed[pl.ds(i * depth, depth), :] = done.reshape(depth, LANES)
-
-
-def decode_kernel(few, packed, maps, bias, weight, latents, rec, weight_here, rec_here, arrived, sent):
+    mixed = target.shape[0]
+    first = pl.multiple_of(place_of[0] * mixed, mixed)
+    target[...] = bias[...] - act_here[pl.ds(first, mixed), :].astype(F32)
+
+
+def decode_kernel(few, packed, maps, bias, weight, latents, rec, weight_here, arrived):
     step = 8 * CHUNK
     depth = 1 if few else 8
     steps = latents.shape[0] // step
@@ -215,16 +226,11 @@
         fill(i)
     for copy in coming:
         copy.wait()
-    going = []
     for i in range(steps):
         rows = pl.ds(i * step, step)
-        rec_here[rows, :] = jnp.dot(latents[rows, :], weight_here[...], preferred_element_type=F32).astype(rec.dtype)
-        going.append(pltpu.make_async_copy(rec_here.at[rows], rec.at[rows], sent.at[i]))
-        going[-1].start()
+        rec[rows, :] = jnp.dot(latents[rows, :], weight_here[...], preferred_element_type=F32).astype(rec.dtype)
         if i + ahead < steps:
             fill(i + ahead)
-    for copy in going:
-        copy.wait()
 
 
 def mix_kernel(sizes, recs, target, out):
@@ -325,24 +331,28 @@
     return [pl.BlockSpec(memory_space=m) for m in spaces]
 
 
-def encode(few, group, ids, activations, enc_weight):
+def encode(few, ids, activations, enc_weight, dec_bias):
+    group = lax.axis_index(NARROW)
     tokens, channels = activations.shape
     width = enc_weight.shape[1]
     depth = tokens // CHUNK * (1 if few else 8)
-    partial, named, slots, base = call(
+    return call(
         functools.partial(encode_kernel, few),
         (
             array((depth, LANES), F32),
             array((FEW if few else ids.shape[0], tokens), jnp.int32),
             array((tokens, LANES), jnp.int32),
             array((8, tokens), jnp.int32),
+            array((tokens // lax.axis_size(NARROW), channels), F32),
         ),
         2 * tokens * channels * width,
-        group,
+        group[None],
+        turned(group, sizes_of(NARROW))[None],
         ids,
         activations,
         enc_weight,
-        in_specs=specs(pltpu.SMEM, pltpu.VMEM, pltpu.HBM, pltpu.HBM),
+        dec_bias[None],
+        in_specs=specs(pltpu.SMEM, pltpu.SMEM, pltpu.VMEM, pl.ANY, pl.ANY, pltpu.VMEM),
         scratch_shapes=[
             pltpu.VMEM(activations.shape, BF16),
             pltpu.VMEM(enc_weight.shape, BF16),
@@ -350,10 +360,9 @@
             pltpu.SemaphoreType.DMA((5,)),
         ],
     )
-    return partial, named, slots, base
-
-
-def find(named, base, dec_weight, *rest):
+
+
+def find(named, base, dec_weight, ids=None):
     tokens = named.shape[1]
     width, channels = dec_weight.shape
     shapes = (
@@ -361,28 +370,14 @@
         array((2, CHUNK, LANES), jnp.int32),
         array((channels, width), BF16),
     )
-    ins, outs = [pltpu.SMEM] + [pltpu.VMEM] * 3, [pltpu.VMEM] * 3
-    kernel, scratch = maps_kernel, []
-    if rest:
-        rows = tokens // lax.axis_size(NARROW)
-        shapes += (array((rows, channels), F32), array((1,), jnp.int32))
-        ins += [pltpu.SMEM, pltpu.HBM, pltpu.VMEM, pltpu.VMEM]
-        outs += [pltpu.VMEM, pltpu.SMEM]
+    args, outs, kernel = [lax.axis_index(WIDE)[None], named, base, dec_weight], [pltpu.VMEM] * 3, maps_kernel
+    if ids is not None:
+        args.append(ids)
+        shapes += (array((1,), jnp.int32),)
+        outs.append(pltpu.SMEM)
         kernel = functools.partial(window_kernel, width)
-        scratch = [pltpu.VMEM((rows, channels), BF16), pltpu.SemaphoreType.DMA]
-    return call(
-        kernel,
-        shapes,
-        1 << 26,
-        lax.axis_index(WIDE)[None],
-        named,
-        base,
-        dec_weight,
-        *rest,
-        in_specs=specs(*ins),
-        out_specs=specs(*outs),
-        scratch_shapes=scratch,
-    )
+    ins = [pltpu.SMEM] + [pltpu.VMEM] * (len(args) - 1)
+    return call(kernel, shapes, 1 << 26, *args, in_specs=specs(*ins), out_specs=specs(*outs))
 
 
 def decode(few, preact, maps, target, enc_bias, dec_weight):
@@ -396,14 +391,8 @@
         maps,
         enc_bias[None],
         dec_weight,
-        in_specs=specs(pltpu.VMEM, pltpu.VMEM, pltpu.VMEM, pltpu.HBM),
-        out_specs=specs(pltpu.VMEM, pl.ANY),
-        scratch_shapes=[
-            pltpu.VMEM(dec_weight.shape, BF16),
-            pltpu.VMEM((tokens, channels), BF16),
-            pltpu.SemaphoreType.DMA((4,)),
-            pltpu.SemaphoreType.DMA((4,)),
-        ],
+        in_specs=specs(pltpu.VMEM, pltpu.VMEM, pltpu.VMEM, pl.ANY),
+        scratch_shapes=[pltpu.VMEM(dec_weight.shape, BF16), pltpu.SemaphoreType.DMA((4,))],
     )
     sizes = sizes_of(NARROW)
     recs = swap_from_far(rec.reshape(-1, *target.shape), NARROW, sizes)
@@ -447,14 +436,10 @@
 
 def local(activations, enc_weight, enc_bias, dec_weight, dec_bias, active_ids):
     width = enc_weight.shape[1]
-    group = lax.axis_index(NARROW)
     ids = active_ids.T
-    partial, named, slots, base = encode(True, group[None], ids, activations, enc_weight)
+    partial, named, slots, base, target = encode(True, ids, activations, enc_weight, dec_bias)
     preact = summed_over_wide(partial)
-    place_of = turned(group, sizes_of(NARROW))[None]
-    maps, own, turned_weight, target, needed = find(
-        named, base, dec_weight, place_of, activations, dec_bias[None], ids
-    )
+    maps, own, turned_weight, needed = find(named, base, dec_weight, ids)
     wide = [lax.axis_size(WIDE)]
     latents, back = decode(True, preact, maps, target, enc_bias, dec_weight)
     parts = swap_from_far(latent_parts(True, back, turned_weight, slots), WIDE, wide)
@@ -464,7 +449,8 @@
         return dec_grad, own_gradient(True, parts, own, width)
 
     def many():
-        partial, named, slots, base = encode(False, group[None], ids, activations, enc_weight)
+        no_bias = jnp.zeros_like(dec_bias)
+        partial, named, slots, base, _ = encode(False, ids, activations, enc_weight, no_bias)
         preact = summed_over_wide(partial)
         maps, own, turned_weight = find(named, base, dec_weight)
         latents, back = decode(False, preact, maps, target, enc_bias, dec_weight)

time: 85.2 us -> 83.9 us (0.985)
  Pallas kernels: 16.8 us -> 14.7 us
    pallas_call x7, Pallas kernels: 16.8 us -> 14.7 us  [call(): pl.pallas_call(kernel, out_shape=shapes, compiler_params=pltpu.CompilerPa...]
  transfers between devices with their start and end apart: 2 -> 2, of which waited for: 0 -> 1; matrix products, arithmetic and copies ran while one was open for 0% -> 0% of each run, Pallas kernels for 7% -> 6%
where the time goes in v9:
time: 83.9 us; the launch traced here: 83.5 us
  blocking collectives  37 us (44%)
  starting transfers between devices  28.3 us (34%)
  Pallas kernels  14.7 us (18%)
  local copies, waits for them, and re-layouts  1.47 us (2%)
  between operations  1.43 us (2%)
    all_to_all x2, starting transfers between devices, swap_from_far(): return lax.all_to_all(pieces, axes, 0, 0, axis_index_groups=order)  28.3 us
    all_to_all x2, blocking collectives, swap_from_far(): return lax.all_to_all(pieces, axes, 0, 0, axis_index_groups=order)  26.3 us
    pallas_call x7, Pallas kernels, call(): pl.pallas_call(kernel, out_shape=shapes, compiler_params=pltpu.CompilerPa...  14.7 us
    all_gather x1, blocking collectives, summed_over_wide(): both = lax.all_gather(partial, core)  8.37 us
    all_gather x1, blocking collectives, summed_over_wide(): return lax.all_gather(jnp.sum(pieces.astype(F32), axis=0), core, tiled=True)  2.34 us
  transfers between devices with their start and end apart: 2, of which 1 were waited for; matrix products, arithmetic and copies ran while one was open for 0% of the time, Pallas kernels for 6%

profile of v9, /device:TPU:1, one launch (start us, length us, event | category | flops | bytes accessed | tf_op | source)
XLA Modules:
  0.0 83.5 jit_solution(17703740434109731883)
XLA Ops:
  0.6 0.0 copy-start.1
  0.7 0.0 copy-start
  0.7 0.8 copy-done.1
  1.5 0.0 copy-done
  1.5 4.3 %shard_map.81 = (f32[32,128]{1,0:T(8,128)S(1)}, s32[16,512]{1,0:T(8,128)S(1)}, s32[512,128]{1,0:T(8,128)S(1)}, s32[8,512]{1,0:T(8,128)S(1)}, f32[32,512]{1,0:T(8,128)S(1)}) custom-call(s32[1]{0:T(128)} %bitcast.9.group, s32[1]{0:T(128)} %bitcast.10.place_of, s32[64,512]{1,0:T(8,128)S(1)} %bitcast.29, bf16[512,512]{1,0:T(8,128)(2,1)} %act.1, ...), custom_call_target="tpu_custom_call" | custom-call | flops 536870912 | bytes 2099208 | tf_op jit(solution)/shard_map/pallas_call | solution.py:289
  5.9 8.4 %all-gather.1 = f32[64,128]{1,0:T(8,128)S(1)} all-gather(f32[32,128]{1,0:T(8,128)S(1)} %get-tuple-element.53), channel_id=3, replica_groups=mesh['wide_0'=16,'wide_1'=2,'narrow_0'=4,'narrow_1'=4] {'wide_1'}, dimensions={0}, use_global_device_ids=true | all-gather | bytes 49152 | tf_op jit(solution)/shard_map/all_gather | solution.py:322
  14.3 0.6 broadcast_in_dim.48
  14.9 12.9 %all-to-all-start.4 = ((bf16[16,16,128]{2,1,0:T(8,128)(2,1)}), bf16[16,16,128]{2,1,0:T(8,128)(2,1)S(1)}, u32[]{:S(2)}, u32[]{:S(2)}) async-start(bf16[16,16,128]{2,1,0:T(8,128)(2,1)} %broadcast_in_dim.48), calls=%async_computation.4 | async-start | bytes 131072 | tf_op jit(solution)/shard_map/all_to_all | solution.py:316
  27.8 3.8 %shard_map.82 = (s32[2,512,128]{2,1,0:T(8,128)S(1)}, s32[2,16,128]{2,1,0:T(8,128)S(1)}, bf16[512,1024]{1,0:T(8,128)(2,1)S(1)}, s32[1]{0:T(128)}) custom-call(s32[1]{0:T(128)} %bitcast.8.owner, s32[16,512]{1,0:T(8,128)S(1)} %get-tuple-element.49.named, s32[8,512]{1,0:T(8,128)S(1)} %get-tuple-element.50.base, bf16[1024,512]{1,0:T(8,128)(2,1)} %weight.5, ...), custom_call_target="tpu_custom_call" | custom-call | flops 67108864 | bytes 2818056 | tf_op jit(solution)/shard_map/pallas_call | solution.py:289
  31.6 0.3 all-to-all-done.4
  31.9 0.0 copy-start.3
  31.9 2.3 %all_gather.20.packed = f32[32,128]{1,0:T(8,128)S(1)} all-gather(f32[16,128]{1,0:T(8,128)S(1)} %convert_reduce_fusion.1), channel_id=1, replica_groups=mesh['wide_0'=16,'wide_1'=2,'narrow_0'=4,'narrow_1'=4] {'wide_1'}, dimensions={0}, use_global_device_ids=true | all-gather | bytes 24576 | tf_op jit(solution)/shard_map/all_gather | solution.py:327
  34.3 0.0 copy-done.3
  34.3 2.2 %shard_map.83 = (bf16[512,1024]{1,0:T(8,128)(2,1)S(1)}, bf16[512,512]{1,0:T(8,128)(2,1)S(1)}) custom-call(f32[32,128]{1,0:T(8,128)S(1)} %all_gather.20.packed, s32[2,512,128]{2,1,0:T(8,128)S(1)} %get-tuple-element.54.maps, f32[1,1024]{1,0:T(1,128)S(1)} %bitcast.33, bf16[1024,512]{1,0:T(8,128)(2,1)} %weight.5), custom_call_target="tpu_custom_call" | custom-call | flops 536870912 | bytes 3166208 | tf_op jit(solution)/shard_map/pallas_call | solution.py:289
  36.5 14.1 %all_to_all.38.recs = bf16[16,32,512]{2,1,0:T(8,128)(2,1)S(1)} all-to-all(bf16[16,32,512]{2,1,0:T(8,128)(2,1)S(1)} %bitcast.25), channel_id=1, replica_groups={{10,11,8,9,14,15,12,13,2,3,0,1,6,7,4,5},{26,27,24,25,30,31,28,29,18,19,..., dimensions={0} | all-to-all | bytes 1048576 | tf_op jit(solution)/shard_map/all_to_all | solution.py:316
  50.5 0.2 shard_map.84
  50.7 12.2 %all_to_all.39 = bf16[16,32,512]{2,1,0:T(8,128)(2,1)S(1)} all-to-all(bf16[16,32,512]{2,1,0:T(8,128)(2,1)S(1)} %shard_map.84), channel_id=1, replica_groups={{10,11,8,9,14,15,12,13,2,3,0,1,6,7,4,5},{26,27,24,25,30,31,28,29,18,19,..., dimensions={0} | all-to-all | bytes 1048576 | tf_op jit(solution)/shard_map/all_to_all | solution.py:316
  62.9 1.9 %shard_map.85 = f32[32,1,128]{2,1,0:T(1,128)} custom-call(bf16[512,512]{1,0:T(8,128)(2,1)S(1)} %bitcast.21, bf16[512,1024]{1,0:T(8,128)(2,1)S(1)} %get-tuple-element.56.turned_weight, s32[512,128]{1,0:T(8,128)S(1)} %get-tuple-element.57.slots), custom_call_target="tpu_custom_call" | custom-call | flops 536870912 | bytes 1851392 | tf_op jit(solution)/shard_map/pallas_call | solution.py:289
  64.9 15.4 %all-to-all-start.7 = ((f32[32,1,128]{2,1,0:T(1,128)}), f32[32,1,128]{2,1,0:T(1,128)S(1)}, u32[]{:S(2)}, u32[]{:S(2)}) async-start(f32[32,1,128]{2,1,0:T(1,128)} %shard_map.85), calls=%async_computation.7 | async-start | bytes 32768 | tf_op jit(solution)/shard_map/all_to_all | solution.py:316
  80.9 0.0 copy-start.2
  80.9 1.5 %shard_map.86 = bf16[1024,512]{1,0:T(8,128)(2,1)} custom-call(bf16[512,1024]{1,0:T(8,128)(2,1)S(1)} %get-tuple-element.59.latents, bf16[512,512]{1,0:T(8,128)(2,1)S(1)} %bitcast.22), custom_call_target="tpu_custom_call" | custom-call | flops 536870912 | bytes 2621440 | tf_op jit(solution)/shard_map/pallas_call | solution.py:289
  82.4 0.0 all-to-all-done.7
  82.4 0.0 copy-done.2
  82.4 1.0 %conditional.1 = (bf16[1024,512]{1,0:T(8,128)(2,1)}, f32[16,1024]{1,0:T(8,128)}) conditional(s32[]{:T(128)} %bitcast.13, (s32[64,512]{1,0:T(8,128)S(1)}, bf16[512,512]{1,0:T(8,128)(2,1)}, bf16[512,1024]{1,0:T(8,128)(2,1)S(1)}, bf16[1024,512]{1,0:T(8,128)(2,1)}, f32[1024]{0:T(1024)S(1)}, /*index=5*/f32[32,512]{1,0:T(8,128)S(1)}) %tuple.25, ...), branch_computations={%region_1.3_spmd, %region_3.4_spmd} | conditional | flops 2218278912 | bytes 20259704 | solution.py:460
  82.7 0.8 branch_1_fun.1
  (2 shorter events, 0.0 us)
Async XLA Ops:
  0.6 0.9 %copy-start.1 = (s32[512,64]{0,1:T(8,128)S(1)}, s32[512,64]{0,1:T(8,128)}, u32[]{:S(2)}) copy-start(s32[512,64]{0,1:T(8,128)} %param.13) | copy-start | bytes 393220
  0.7 0.8 copy-start
  14.9 17.0 %all-to-all-start.4 = ((bf16[16,16,128]{2,1,0:T(8,128)(2,1)}), bf16[16,16,128]{2,1,0:T(8,128)(2,1)S(1)}, u32[]{:S(2)}, u32[]{:S(2)}) async-start(bf16[16,16,128]{2,1,0:T(8,128)(2,1)} %broadcast_in_dim.48), calls=%async_computation.4 | async-start | bytes 131072 | tf_op jit(solution)/shard_map/all_to_all | solution.py:316
  31.9 2.4 %copy-start.3 = (f32[1024]{0:T(1024)S(1)}, f32[1024]{0:T(1024)}, u32[]{:S(2)}) copy-start(f32[1024]{0:T(1024)} %param.10) | copy-start | bytes 12292
  64.9 17.5 %all-to-all-start.7 = ((f32[32,1,128]{2,1,0:T(1,128)}), f32[32,1,128]{2,1,0:T(1,128)S(1)}, u32[]{:S(2)}, u32[]{:S(2)}) async-start(f32[32,1,128]{2,1,0:T(1,128)} %shard_map.85), calls=%async_computation.7 | async-start | bytes 32768 | tf_op jit(solution)/shard_map/all_to_all | solution.py:316
  80.9 1.5 %copy-start.2 = (bf16[512,1024]{1,0:T(8,128)(2,1)S(1)}, bf16[512,1024]{1,0:T(8,128)(2,1)}, u32[]{:S(2)}) copy-start(bf16[512,1024]{1,0:T(8,128)(2,1)} %weight.3) | copy-start | bytes 3145732

commit v10 on v9

--- a/solution.py
+++ b/solution.py
@@ -113,7 +113,7 @@
     most[0] = jnp.max(needed)
 
 
-def maps_kernel(owner, named, base, weight, out, own, turned_weight):
+def maps_kernel(owner, named, base, weight, out, own, turned_weight, early):
     count, tokens = named.shape
     line = lax.broadcasted_iota(jnp.int32, (LANES, LANES), 0)
     for i in range(tokens // LANES):
@@ -139,13 +139,14 @@
         maps = lax.fori_loop(0, count // 8, body, (zero, zero))
         for m in range(2):
             out[m, cols, :] = maps[m].T
+    early[0] = jnp.where(owner[0] < 2, 1, 0)
     own[...] = out[:, pl.ds(pl.multiple_of(owner[0] * CHUNK, CHUNK), CHUNK), :]
     for r in range(0, weight.shape[0], 256):
         turned_weight[:, pl.ds(r, 256)] = weight[pl.ds(r, 256), :].T
 
 
-def window_kernel(width, owner, named, base, weight, ids, out, own, turned_weight, most):
-    maps_kernel(owner, named, base, weight, out, own, turned_weight)
+def window_kernel(width, owner, named, base, weight, ids, out, own, turned_weight, early, most):
+    maps_kernel(owner, named, base, weight, out, own, turned_weight, early)
     count_needed(width, ids, most)
 
 
@@ -167,33 +168,34 @@
     picked,
     arrived,
 ):
-    width = weight.shape[1]
-    block = width // 4
+    depth, width = weight.shape
+    half, block = width // 2, depth // 4
     pairs = [(act, act_here)]
-    for n in range(4):
-        cols = pl.ds(n * block, block)
-        pairs.append((weight.at[:, cols], weight_here.at[:, cols]))
+    for n in range(8):
+        at = (pl.ds(n % 4 * block, block), pl.ds(n // 4 * half, half))
+        pairs.append((weight.at[at], weight_here.at[at]))
     copies = [pltpu.make_async_copy(*pair, arrived.at[n]) for n, pair in enumerate(pairs)]
     for copy in copies:
         copy.start()
     fill_slots(few, group[0], width, ids, named, slots, base)
     copies[0].wait()
     step = 8 * CHUNK
-    for n in range(4):
-        copies[n + 1].wait()
+    for n in range(2):
+        for copy in copies[4 * n + 1 : 4 * n + 5]:
+            copy.wait()
         for i in range(act.shape[0] // step):
             rows = pl.ds(i * step, step)
             part = jnp.dot(
-                act_here[rows, :], weight_here[:, pl.ds(n * block, block)], preferred_element_type=F32
+                act_here[rows, :], weight_here[:, pl.ds(n * half, half)], preferred_element_type=F32
             )
             sofar = picked[rows, :] if n else jnp.zeros((step, LANES), F32)
-            sofar = pick_more(sofar, part, n * block, slots[rows, :])
-            if n < 3:
+            sofar = pick_more(sofar, part, n * half, slots[rows, :])
+            if n:
+                done = pack(sofar, few)
+                lines = 8 * done.shape[1]
+                packed[pl.ds(i * lines, lines), :] = done.reshape(lines, LANES)
+            else:
                 picked[rows, :] = sofar
-            else:
-                done = pack(sofar, few)
-                depth = 8 * done.shape[1]
-                packed[pl.ds(i * depth, depth), :] = done.reshape(depth, LANES)
     mixed = target.shape[0]
     first = pl.multiple_of(place_of[0] * mixed, mixed)
     target[...] = bias[...] - act_here[pl.ds(first, mixed), :].astype(F32)
@@ -250,16 +252,7 @@
                 out[(at_group[g], *at)] = (suffix * (1.0 / groups)).astype(out.dtype)
 
 
-def grad_kernel(few, back, turned_weight, slots, out):
-    step = 8 * CHUNK
-    for i in range(back.shape[0] // step):
-        rows = pl.ds(i * step, step)
-        part = jnp.dot(back[rows, :], turned_weight[...], preferred_element_type=F32)
-        first = (8 * i + out.shape[0] // 2) % out.shape[0]
-        out[pl.ds(first, 8)] = pick_slots(part, slots[rows, :], few)
-
-
-def outer_kernel(latents, back, out, here, sent):
+def outer_into(latents, back, out, here, sent):
     step = 256
     copies = []
     for i in range(out.shape[0] // step):
@@ -275,6 +268,25 @@
         copies[-1].start()
     for copy in copies:
         copy.wait()
+
+
+def grad_kernel(few, early, back, turned_weight, slots, latents, grads, out, here, sent):
+    step = 8 * CHUNK
+    for i in range(back.shape[0] // step):
+        rows = pl.ds(i * step, step)
+        part = jnp.dot(back[rows, :], turned_weight[...], preferred_element_type=F32)
+        first = (8 * i + grads.shape[0] // 2) % grads.shape[0]
+        grads[pl.ds(first, 8)] = pick_slots(part, slots[rows, :], few)
+
+    @pl.when(early[0] == 1)
+    def _():
+        outer_into(latents, back, out, here, sent)
+
+
+def outer_kernel(early, latents, back, before, out, here, sent):
+    @pl.when(early[0] == 0)
+    def _():
+        outer_into(latents, back, out, here, sent)
 
 
 def own_kernel(few, pieces, maps, out):
@@ -357,7 +369,7 @@
             pltpu.VMEM(activations.shape, BF16),
             pltpu.VMEM(enc_weight.shape, BF16),
             pltpu.VMEM((tokens, LANES), F32),
-            pltpu.SemaphoreType.DMA((5,)),
+            pltpu.SemaphoreType.DMA((9,)),
         ],
     )
 
@@ -369,8 +381,10 @@
         array((2, tokens, LANES), jnp.int32),
         array((2, CHUNK, LANES), jnp.int32),
         array((channels, width), BF16),
-    )
-    args, outs, kernel = [lax.axis_index(WIDE)[None], named, base, dec_weight], [pltpu.VMEM] * 3, maps_kernel
+        array((1,), jnp.int32),
+    )
+    args, kernel = [lax.axis_index(WIDE)[None], named, base, dec_weight], maps_kernel
+    outs = [pltpu.VMEM] * 3 + [pltpu.SMEM]
     if ids is not None:
         args.append(ids)
         shapes += (array((1,), jnp.int32),)
@@ -406,28 +420,37 @@
     return latents, swap_from_far(mixed, NARROW, sizes).reshape(tokens, channels)
 
 
-def latent_parts(few, back, turned_weight, slots):
-    return call(
+def decoder_side(few, early, back, latents, turned_weight, slots):
+    wide, width, channels = lax.axis_size(WIDE), latents.shape[1], back.shape[1]
+    scratch = [pltpu.VMEM((width, channels), BF16), pltpu.SemaphoreType.DMA((4,))]
+    grads, dec_grad = call(
         functools.partial(grad_kernel, few),
-        array((lax.axis_size(WIDE), 1 if few else 8, LANES), F32),
-        2 * back.size * turned_weight.shape[1],
+        (array((wide, 1 if few else 8, LANES), F32), array((width, channels), BF16)),
+        2 * back.size * width,
+        early,
         back,
         turned_weight,
         slots,
-    )
-
-
-def outer(latents, back):
-    shape = (latents.shape[1], back.shape[1])
-    return call(
+        latents,
+        in_specs=specs(pltpu.SMEM, pltpu.VMEM, pltpu.VMEM, pltpu.VMEM, pltpu.VMEM),
+        out_specs=specs(pltpu.VMEM, pl.ANY),
+        scratch_shapes=scratch,
+    )
+    parts = swap_from_far(grads, WIDE, [wide])
+    dec_grad = call(
         outer_kernel,
-        array(shape, BF16),
-        2 * latents.size * back.shape[1],
+        array((width, channels), BF16),
+        2 * back.size * width,
+        early,
         latents,
         back,
+        dec_grad,
+        in_specs=specs(pltpu.SMEM, pltpu.VMEM, pltpu.VMEM, pl.ANY),
         out_specs=specs(pl.ANY)[0],
-        scratch_shapes=[pltpu.VMEM(shape, BF16), pltpu.SemaphoreType.DMA((4,))],
-    )
+        scratch_shapes=scratch,
+        input_output_aliases={3: 0},
+    )
+    return parts, dec_grad
 
 
 def own_gradient(few, parts, own, width):
@@ -439,11 +462,9 @@
     ids = active_ids.T
     partial, named, slots, base, target = encode(True, ids, activations, enc_weight, dec_bias)
     preact = summed_over_wide(partial)
-    maps, own, turned_weight, needed = find(named, base, dec_weight, ids)
-    wide = [lax.axis_size(WIDE)]
+    maps, own, turned_weight, early, needed = find(named, base, dec_weight, ids)
     latents, back = decode(True, preact, maps, target, enc_bias, dec_weight)
-    parts = swap_from_far(latent_parts(True, back, turned_weight, slots), WIDE, wide)
-    dec_grad = outer(latents, back)
+    parts, dec_grad = decoder_side(True, early, back, latents, turned_weight, slots)
 
     def few():
         return dec_grad, own_gradient(True, parts, own, width)
@@ -452,10 +473,10 @@
         no_bias = jnp.zeros_like(dec_bias)
         partial, named, slots, base, _ = encode(False, ids, activations, enc_weight, no_bias)
         preact = summed_over_wide(partial)
-        maps, own, turned_weight = find(named, base, dec_weight)
+        maps, own, turned_weight, early = find(named, base, dec_weight)
         latents, back = decode(False, preact, maps, target, enc_bias, dec_weight)
-        parts = swap_from_far(latent_parts(False, back, turned_weight, slots), WIDE, wide)
-        return outer(latents, back), own_gradient(False, parts, own, width)
+        parts, dec_grad = decoder_side(False, early, back, latents, turned_weight, slots)
+        return dec_grad, own_gradient(False, parts, own, width)
 
     return lax.cond(needed[0] <= LANES, few, many)
 

time: 83.9 us -> 84.5 us (level)
  transfers between devices with their start and end apart: 2 -> 2, of which waited for: 1 -> 2; matrix products, arithmetic and copies ran while one was open for 0% -> 0% of each run, Pallas kernels for 6% -> 5%
where the time goes in v10:
time: 84.5 us; the launch traced here: 84 us
  blocking collectives  37 us (44%)
  starting transfers between devices  27.7 us (33%)
  Pallas kernels  15.4 us (18%)
  local copies, waits for them, and re-layouts  1.47 us (2%)
  between operations  1.34 us (2%)
  waiting for transfers between devices  1.06 us (1%)
    all_to_all x2, starting transfers between devices, swap_from_far(): return lax.all_to_all(pieces, axes, 0, 0, axis_index_groups=order)  27.7 us
    all_to_all x2, blocking collectives, swap_from_far(): return lax.all_to_all(pieces, axes, 0, 0, axis_index_groups=order)  26.3 us
    pallas_call x7, Pallas kernels, call(): pl.pallas_call(kernel, out_shape=shapes, compiler_params=pltpu.CompilerPa...  15.4 us
    all_gather x1, blocking collectives, summed_over_wide(): both = lax.all_gather(partial, core)  8.37 us
    all_gather x1, blocking collectives, summed_over_wide(): return lax.all_gather(jnp.sum(pieces.astype(F32), axis=0), core, tiled=True)  2.34 us
  transfers between devices with their start and end apart: 2, of which 2 were waited for; matrix products, arithmetic and copies ran while one was open for 0% of the time, Pallas kernels for 5%

profile of v10, /device:TPU:1, one launch (start us, length us, event | category | flops | bytes accessed | tf_op | source)
XLA Modules:
  0.0 84.0 jit_solution(10896939631011047491)
XLA Ops:
  0.6 0.0 copy-start.1
  0.7 0.0 copy-start
  0.7 0.8 copy-done.1
  1.5 0.0 copy-done
  1.5 3.6 %shard_map.81 = (f32[32,128]{1,0:T(8,128)S(1)}, s32[16,512]{1,0:T(8,128)S(1)}, s32[512,128]{1,0:T(8,128)S(1)}, s32[8,512]{1,0:T(8,128)S(1)}, f32[32,512]{1,0:T(8,128)S(1)}) custom-call(s32[1]{0:T(128)} %bitcast.9.group, s32[1]{0:T(128)} %bitcast.10.place_of, s32[64,512]{1,0:T(8,128)S(1)} %bitcast.29, bf16[512,512]{1,0:T(8,128)(2,1)} %act.1, ...), custom_call_target="tpu_custom_call" | custom-call | flops 536870912 | bytes 2099208 | tf_op jit(solution)/shard_map/pallas_call | solution.py:301
  5.2 8.4 %all-gather.1 = f32[64,128]{1,0:T(8,128)S(1)} all-gather(f32[32,128]{1,0:T(8,128)S(1)} %get-tuple-element.60), channel_id=3, replica_groups=mesh['wide_0'=16,'wide_1'=2,'narrow_0'=4,'narrow_1'=4] {'wide_1'}, dimensions={0}, use_global_device_ids=true | all-gather | bytes 49152 | tf_op jit(solution)/shard_map/all_gather | solution.py:334
  13.6 0.6 broadcast_in_dim.48
  14.2 12.9 %all-to-all-start.4 = ((bf16[16,16,128]{2,1,0:T(8,128)(2,1)}), bf16[16,16,128]{2,1,0:T(8,128)(2,1)S(1)}, u32[]{:S(2)}, u32[]{:S(2)}) async-start(bf16[16,16,128]{2,1,0:T(8,128)(2,1)} %broadcast_in_dim.48), calls=%async_computation.4 | async-start | bytes 131072 | tf_op jit(solution)/shard_map/all_to_all | solution.py:328
  27.1 3.8 %shard_map.82 = (s32[2,512,128]{2,1,0:T(8,128)S(1)}, s32[2,16,128]{2,1,0:T(8,128)S(1)}, bf16[512,1024]{1,0:T(8,128)(2,1)S(1)}, s32[1]{0:T(128)}, s32[1]{0:T(128)}) custom-call(s32[1]{0:T(128)} %bitcast.8.owner, s32[16,512]{1,0:T(8,128)S(1)} %get-tuple-element.55.named, s32[8,512]{1,0:T(8,128)S(1)} %get-tuple-element.56.base, bf16[1024,512]{1,0:T(8,128)(2,1)} %weight.5, ...), custom_call_target="tpu_custom_call" | custom-call | flops 67108864 | bytes 2818060 | tf_op jit(solution)/shard_map/pallas_call | solution.py:301
  30.9 0.3 all-to-all-done.4
  31.2 0.0 copy-start.3
  31.2 2.3 %all_gather.20.packed = f32[32,128]{1,0:T(8,128)S(1)} all-gather(f32[16,128]{1,0:T(8,128)S(1)} %convert_reduce_fusion.1), channel_id=1, replica_groups=mesh['wide_0'=16,'wide_1'=2,'narrow_0'=4,'narrow_1'=4] {'wide_1'}, dimensions={0}, use_global_device_ids=true | all-gather | bytes 24576 | tf_op jit(solution)/shard_map/all_gather | solution.py:339
  33.6 0.0 copy-done.3
  33.6 2.2 %shard_map.83 = (bf16[512,1024]{1,0:T(8,128)(2,1)S(1)}, bf16[512,512]{1,0:T(8,128)(2,1)S(1)}) custom-call(f32[32,128]{1,0:T(8,128)S(1)} %all_gather.20.packed, s32[2,512,128]{2,1,0:T(8,128)S(1)} %get-tuple-element.61.maps, f32[1,1024]{1,0:T(1,128)S(1)} %bitcast.33, bf16[1024,512]{1,0:T(8,128)(2,1)} %weight.5), custom_call_target="tpu_custom_call" | custom-call | flops 536870912 | bytes 3166208 | tf_op jit(solution)/shard_map/pallas_call | solution.py:301
  35.8 14.1 %all_to_all.38.recs = bf16[16,32,512]{2,1,0:T(8,128)(2,1)S(1)} all-to-all(bf16[16,32,512]{2,1,0:T(8,128)(2,1)S(1)} %bitcast.25), channel_id=1, replica_groups={{10,11,8,9,14,15,12,13,2,3,0,1,6,7,4,5},{26,27,24,25,30,31,28,29,18,19,..., dimensions={0} | all-to-all | bytes 1048576 | tf_op jit(solution)/shard_map/all_to_all | solution.py:328
  49.8 0.2 shard_map.84
  50.0 12.2 %all_to_all.39 = bf16[16,32,512]{2,1,0:T(8,128)(2,1)S(1)} all-to-all(bf16[16,32,512]{2,1,0:T(8,128)(2,1)S(1)} %shard_map.84), channel_id=1, replica_groups={{10,11,8,9,14,15,12,13,2,3,0,1,6,7,4,5},{26,27,24,25,30,31,28,29,18,19,..., dimensions={0} | all-to-all | bytes 1048576 | tf_op jit(solution)/shard_map/all_to_all | solution.py:328
  62.2 4.1 %shard_map.85 = (f32[32,1,128]{2,1,0:T(1,128)}, bf16[1024,512]{1,0:T(8,128)(2,1)}) custom-call(s32[1]{0:T(128)} %get-tuple-element.59.early, bf16[512,512]{1,0:T(8,128)(2,1)S(1)} %bitcast.21, bf16[512,1024]{1,0:T(8,128)(2,1)S(1)} %get-tuple-element.63.turned_weight, s32[512,128]{1,0:T(8,128)S(1)} %get-tuple-element.64.slots, ...), custom_call_target="tpu_custom_call" | custom-call | flops 536870912 | bytes 3948548 | tf_op jit(solution)/shard_map/pallas_call | solution.py:301
  66.3 14.8 %all-to-all-start.7 = ((f32[32,1,128]{2,1,0:T(1,128)}), f32[32,1,128]{2,1,0:T(1,128)S(1)}, u32[]{:S(2)}, u32[]{:S(2)}) async-start(f32[32,1,128]{2,1,0:T(1,128)} %get-tuple-element.66), calls=%async_computation.7 | async-start | bytes 32768 | tf_op jit(solution)/shard_map/all_to_all | solution.py:328
  81.7 0.0 copy-start.2
  81.7 0.7 shard_map.86
  82.4 0.8 all-to-all-done.7
  83.2 0.0 copy-done.2
  83.2 0.8 conditional.1
  83.2 0.8 branch_1_fun.1
  (2 shorter events, 0.0 us)
Async XLA Ops:
  0.6 0.9 %copy-start.1 = (s32[512,64]{0,1:T(8,128)S(1)}, s32[512,64]{0,1:T(8,128)}, u32[]{:S(2)}) copy-start(s32[512,64]{0,1:T(8,128)} %param.13) | copy-start | bytes 393220
  0.7 0.8 copy-start
  14.2 17.0 %all-to-all-start.4 = ((bf16[16,16,128]{2,1,0:T(8,128)(2,1)}), bf16[16,16,128]{2,1,0:T(8,128)(2,1)S(1)}, u32[]{:S(2)}, u32[]{:S(2)}) async-start(bf16[16,16,128]{2,1,0:T(8,128)(2,1)} %broadcast_in_dim.48), calls=%async_computation.4 | async-start | bytes 131072 | tf_op jit(solution)/shard_map/all_to_all | solution.py:328
  31.2 2.4 %copy-start.3 = (f32[1024]{0:T(1024)S(1)}, f32[1024]{0:T(1024)}, u32[]{:S(2)}) copy-start(f32[1024]{0:T(1024)} %param.10) | copy-start | bytes 12292
  66.3 16.9 %all-to-all-start.7 = ((f32[32,1,128]{2,1,0:T(1,128)}), f32[32,1,128]{2,1,0:T(1,128)S(1)}, u32[]{:S(2)}, u32[]{:S(2)}) async-start(f32[32,1,128]{2,1,0:T(1,128)} %get-tuple-element.66), calls=%async_computation.7 | async-start | bytes 32768 | tf_op jit(solution)/shard_map/all_to_all | solution.py:328
  81.7 1.6 %copy-start.2 = (bf16[512,512]{1,0:T(8,128)(2,1)S(1)}, bf16[512,512]{1,0:T(8,128)(2,1)}, u32[]{:S(2)}) copy-start(bf16[512,512]{1,0:T(8,128)(2,1)} %act.1) | copy-start | bytes 1572868

commit v11 on v9

--- a/solution.py
+++ b/solution.py
@@ -167,33 +167,34 @@
     picked,
     arrived,
 ):
-    width = weight.shape[1]
-    block = width // 4
+    depth, width = weight.shape
+    half, block = width // 2, depth // 4
     pairs = [(act, act_here)]
-    for n in range(4):
-        cols = pl.ds(n * block, block)
-        pairs.append((weight.at[:, cols], weight_here.at[:, cols]))
+    for n in range(8):
+        at = (pl.ds(n % 4 * block, block), pl.ds(n // 4 * half, half))
+        pairs.append((weight.at[at], weight_here.at[at]))
     copies = [pltpu.make_async_copy(*pair, arrived.at[n]) for n, pair in enumerate(pairs)]
     for copy in copies:
         copy.start()
     fill_slots(few, group[0], width, ids, named, slots, base)
     copies[0].wait()
     step = 8 * CHUNK
-    for n in range(4):
-        copies[n + 1].wait()
+    for n in range(2):
+        for copy in copies[4 * n + 1 : 4 * n + 5]:
+            copy.wait()
         for i in range(act.shape[0] // step):
             rows = pl.ds(i * step, step)
             part = jnp.dot(
-                act_here[rows, :], weight_here[:, pl.ds(n * block, block)], preferred_element_type=F32
+                act_here[rows, :], weight_here[:, pl.ds(n * half, half)], preferred_element_type=F32
             )
             sofar = picked[rows, :] if n else jnp.zeros((step, LANES), F32)
-            sofar = pick_more(sofar, part, n * block, slots[rows, :])
-            if n < 3:
+            sofar = pick_more(sofar, part, n * half, slots[rows, :])
+            if n:
+                done = pack(sofar, few)
+                lines = 8 * done.shape[1]
+                packed[pl.ds(i * lines, lines), :] = done.reshape(lines, LANES)
+            else:
                 picked[rows, :] = sofar
-            else:
-                done = pack(sofar, few)
-                depth = 8 * done.shape[1]
-                packed[pl.ds(i * depth, depth), :] = done.reshape(depth, LANES)
     mixed = target.shape[0]
     first = pl.multiple_of(place_of[0] * mixed, mixed)
     target[...] = bias[...] - act_here[pl.ds(first, mixed), :].astype(F32)
@@ -357,7 +358,7 @@
             pltpu.VMEM(activations.shape, BF16),
             pltpu.VMEM(enc_weight.shape, BF16),
             pltpu.VMEM((tokens, LANES), F32),
-            pltpu.SemaphoreType.DMA((5,)),
+            pltpu.SemaphoreType.DMA((9,)),
         ],
     )
 

time: 83.9 us -> 83.2 us (level)
  no operation moved by 1% of the time
where the time goes in v11:
time: 83.2 us; the launch traced here: 82.8 us
  blocking collectives  37 us (44%)
  starting transfers between devices  28.3 us (34%)
  Pallas kernels  14 us (17%)
  local copies, waits for them, and re-layouts  1.47 us (2%)
  between operations  1.43 us (2%)
    all_to_all x2, starting transfers between devices, swap_from_far(): return lax.all_to_all(pieces, axes, 0, 0, axis_index_groups=order)  28.3 us
    all_to_all x2, blocking collectives, swap_from_far(): return lax.all_to_all(pieces, axes, 0, 0, axis_index_groups=order)  26.3 us
    pallas_call x7, Pallas kernels, call(): pl.pallas_call(kernel, out_shape=shapes, compiler_params=pltpu.CompilerPa...  14 us
    all_gather x1, blocking collectives, summed_over_wide(): both = lax.all_gather(partial, core)  8.37 us
    all_gather x1, blocking collectives, summed_over_wide(): return lax.all_gather(jnp.sum(pieces.astype(F32), axis=0), core, tiled=True)  2.34 us
  transfers between devices with their start and end apart: 2, of which 1 were waited for; matrix products, arithmetic and copies ran while one was open for 0% of the time, Pallas kernels for 6%

profile of v11, /device:TPU:1, one launch (start us, length us, event | category | flops | bytes accessed | tf_op | source)
XLA Modules:
  0.0 82.8 jit_solution(12909299846858989538)
XLA Ops:
  0.6 0.0 copy-start.1
  0.7 0.0 copy-start
  0.7 0.8 copy-done.1
  1.5 0.0 copy-done
  1.5 3.6 %shard_map.81 = (f32[32,128]{1,0:T(8,128)S(1)}, s32[16,512]{1,0:T(8,128)S(1)}, s32[512,128]{1,0:T(8,128)S(1)}, s32[8,512]{1,0:T(8,128)S(1)}, f32[32,512]{1,0:T(8,128)S(1)}) custom-call(s32[1]{0:T(128)} %bitcast.9.group, s32[1]{0:T(128)} %bitcast.10.place_of, s32[64,512]{1,0:T(8,128)S(1)} %bitcast.29, bf16[512,512]{1,0:T(8,128)(2,1)} %act.1, ...), custom_call_target="tpu_custom_call" | custom-call | flops 536870912 | bytes 2099208 | tf_op jit(solution)/shard_map/pallas_call | solution.py:290
  5.2 8.4 %all-gather.1 = f32[64,128]{1,0:T(8,128)S(1)} all-gather(f32[32,128]{1,0:T(8,128)S(1)} %get-tuple-element.53), channel_id=3, replica_groups=mesh['wide_0'=16,'wide_1'=2,'narrow_0'=4,'narrow_1'=4] {'wide_1'}, dimensions={0}, use_global_device_ids=true | all-gather | bytes 49152 | tf_op jit(solution)/shard_map/all_gather | solution.py:323
  13.6 0.6 broadcast_in_dim.48
  14.2 12.9 %all-to-all-start.4 = ((bf16[16,16,128]{2,1,0:T(8,128)(2,1)}), bf16[16,16,128]{2,1,0:T(8,128)(2,1)S(1)}, u32[]{:S(2)}, u32[]{:S(2)}) async-start(bf16[16,16,128]{2,1,0:T(8,128)(2,1)} %broadcast_in_dim.48), calls=%async_computation.4 | async-start | bytes 131072 | tf_op jit(solution)/shard_map/all_to_all | solution.py:317
  27.1 3.8 %shard_map.82 = (s32[2,512,128]{2,1,0:T(8,128)S(1)}, s32[2,16,128]{2,1,0:T(8,128)S(1)}, bf16[512,1024]{1,0:T(8,128)(2,1)S(1)}, s32[1]{0:T(128)}) custom-call(s32[1]{0:T(128)} %bitcast.8.owner, s32[16,512]{1,0:T(8,128)S(1)} %get-tuple-element.49.named, s32[8,512]{1,0:T(8,128)S(1)} %get-tuple-element.50.base, bf16[1024,512]{1,0:T(8,128)(2,1)} %weight.5, ...), custom_call_target="tpu_custom_call" | custom-call | flops 67108864 | bytes 2818056 | tf_op jit(solution)/shard_map/pallas_call | solution.py:290
  30.9 0.3 all-to-all-done.4
  31.2 0.0 copy-start.3
  31.2 2.3 %all_gather.20.packed = f32[32,128]{1,0:T(8,128)S(1)} all-gather(f32[16,128]{1,0:T(8,128)S(1)} %convert_reduce_fusion.1), channel_id=1, replica_groups=mesh['wide_0'=16,'wide_1'=2,'narrow_0'=4,'narrow_1'=4] {'wide_1'}, dimensions={0}, use_global_device_ids=true | all-gather | bytes 24576 | tf_op jit(solution)/shard_map/all_gather | solution.py:328
  33.6 0.0 copy-done.3
  33.6 2.2 %shard_map.83 = (bf16[512,1024]{1,0:T(8,128)(2,1)S(1)}, bf16[512,512]{1,0:T(8,128)(2,1)S(1)}) custom-call(f32[32,128]{1,0:T(8,128)S(1)} %all_gather.20.packed, s32[2,512,128]{2,1,0:T(8,128)S(1)} %get-tuple-element.54.maps, f32[1,1024]{1,0:T(1,128)S(1)} %bitcast.33, bf16[1024,512]{1,0:T(8,128)(2,1)} %weight.5), custom_call_target="tpu_custom_call" | custom-call | flops 536870912 | bytes 3166208 | tf_op jit(solution)/shard_map/pallas_call | solution.py:290
  35.8 14.1 %all_to_all.38.recs = bf16[16,32,512]{2,1,0:T(8,128)(2,1)S(1)} all-to-all(bf16[16,32,512]{2,1,0:T(8,128)(2,1)S(1)} %bitcast.25), channel_id=1, replica_groups={{10,11,8,9,14,15,12,13,2,3,0,1,6,7,4,5},{26,27,24,25,30,31,28,29,18,19,..., dimensions={0} | all-to-all | bytes 1048576 | tf_op jit(solution)/shard_map/all_to_all | solution.py:317
  49.9 0.2 shard_map.84
  50.1 12.2 %all_to_all.39 = bf16[16,32,512]{2,1,0:T(8,128)(2,1)S(1)} all-to-all(bf16[16,32,512]{2,1,0:T(8,128)(2,1)S(1)} %shard_map.84), channel_id=1, replica_groups={{10,11,8,9,14,15,12,13,2,3,0,1,6,7,4,5},{26,27,24,25,30,31,28,29,18,19,..., dimensions={0} | all-to-all | bytes 1048576 | tf_op jit(solution)/shard_map/all_to_all | solution.py:317
  62.3 2.0 %shard_map.85 = f32[32,1,128]{2,1,0:T(1,128)} custom-call(bf16[512,512]{1,0:T(8,128)(2,1)S(1)} %bitcast.21, bf16[512,1024]{1,0:T(8,128)(2,1)S(1)} %get-tuple-element.56.turned_weight, s32[512,128]{1,0:T(8,128)S(1)} %get-tuple-element.57.slots), custom_call_target="tpu_custom_call" | custom-call | flops 536870912 | bytes 1851392 | tf_op jit(solution)/shard_map/pallas_call | solution.py:290
  64.2 15.4 %all-to-all-start.7 = ((f32[32,1,128]{2,1,0:T(1,128)}), f32[32,1,128]{2,1,0:T(1,128)S(1)}, u32[]{:S(2)}, u32[]{:S(2)}) async-start(f32[32,1,128]{2,1,0:T(1,128)} %shard_map.85), calls=%async_computation.7 | async-start | bytes 32768 | tf_op jit(solution)/shard_map/all_to_all | solution.py:317
  80.2 0.0 copy-start.2
  80.2 1.5 %shard_map.86 = bf16[1024,512]{1,0:T(8,128)(2,1)} custom-call(bf16[512,1024]{1,0:T(8,128)(2,1)S(1)} %get-tuple-element.59.latents, bf16[512,512]{1,0:T(8,128)(2,1)S(1)} %bitcast.22), custom_call_target="tpu_custom_call" | custom-call | flops 536870912 | bytes 2621440 | tf_op jit(solution)/shard_map/pallas_call | solution.py:290
  81.7 0.0 all-to-all-done.7
  81.7 0.0 copy-done.2
  81.7 1.0 %conditional.1 = (bf16[1024,512]{1,0:T(8,128)(2,1)}, f32[16,1024]{1,0:T(8,128)}) conditional(s32[]{:T(128)} %bitcast.13, (s32[64,512]{1,0:T(8,128)S(1)}, bf16[512,512]{1,0:T(8,128)(2,1)}, bf16[512,1024]{1,0:T(8,128)(2,1)S(1)}, bf16[1024,512]{1,0:T(8,128)(2,1)}, f32[1024]{0:T(1024)S(1)}, /*index=5*/f32[32,512]{1,0:T(8,128)S(1)}) %tuple.25, ...), branch_computations={%region_1.3_spmd, %region_3.4_spmd} | conditional | flops 2218278912 | bytes 20259704 | solution.py:461
  82.0 0.8 branch_1_fun.1
  (2 shorter events, 0.0 us)
Async XLA Ops:
  0.6 0.9 %copy-start.1 = (s32[512,64]{0,1:T(8,128)S(1)}, s32[512,64]{0,1:T(8,128)}, u32[]{:S(2)}) copy-start(s32[512,64]{0,1:T(8,128)} %param.13) | copy-start | bytes 393220
  0.7 0.8 copy-start
  14.2 17.0 %all-to-all-start.4 = ((bf16[16,16,128]{2,1,0:T(8,128)(2,1)}), bf16[16,16,128]{2,1,0:T(8,128)(2,1)S(1)}, u32[]{:S(2)}, u32[]{:S(2)}) async-start(bf16[16,16,128]{2,1,0:T(8,128)(2,1)} %broadcast_in_dim.48), calls=%async_computation.4 | async-start | bytes 131072 | tf_op jit(solution)/shard_map/all_to_all | solution.py:317
  31.2 2.4 %copy-start.3 = (f32[1024]{0:T(1024)S(1)}, f32[1024]{0:T(1024)}, u32[]{:S(2)}) copy-start(f32[1024]{0:T(1024)} %param.10) | copy-start | bytes 12292
  64.2 17.5 %all-to-all-start.7 = ((f32[32,1,128]{2,1,0:T(1,128)}), f32[32,1,128]{2,1,0:T(1,128)S(1)}, u32[]{:S(2)}, u32[]{:S(2)}) async-start(f32[32,1,128]{2,1,0:T(1,128)} %shard_map.85), calls=%async_computation.7 | async-start | bytes 32768 | tf_op jit(solution)/shard_map/all_to_all | solution.py:317
  80.2 1.5 %copy-start.2 = (bf16[512,1024]{1,0:T(8,128)(2,1)S(1)}, bf16[512,1024]{1,0:T(8,128)(2,1)}, u32[]{:S(2)}) copy-start(bf16[512,1024]{1,0:T(8,128)(2,1)} %weight.3) | copy-start | bytes 3145732

commit v12 on v11

--- a/solution.py
+++ b/solution.py
@@ -324,7 +324,10 @@
     half = lax.dynamic_slice_in_dim(both, lax.axis_index(core) * rows, rows, 1)
     half = (half[0] + half[1]).astype(BF16)
     size = lax.axis_size(ring)
-    pieces = swap_from_far(jnp.broadcast_to(half[None], (size, *half.shape)), ring, [size])
+    order = [[(i + 3 * size // 8) % size for i in range(size)]]
+    pieces = lax.all_to_all(
+        jnp.broadcast_to(half[None], (size, *half.shape)), ring, 0, 0, axis_index_groups=order
+    )
     return lax.all_gather(jnp.sum(pieces.astype(F32), axis=0), core, tiled=True)
 
 

time: 83.2 us -> 85.2 us (1.024)
  waiting for transfers between devices: 0.26 us -> 2.36 us
  starting transfers between devices: 28.3 us -> 27.3 us
  blocking collectives: 37 us -> 37.9 us
    all_to_all x2 -> x1, starting transfers between devices: 28.3 us -> 14.8 us  [swap_from_far(): return lax.all_to_all(pieces, axes, 0, 0, axis_index_groups=order)]
    all_to_all x0 -> x1, starting transfers between devices: none -> 12.5 us  [summed_over_wide(): lax.all_to_all(jnp.broadcast_to(half[None], (size, *half.shape)), ring, 0...]
    all_to_all x0 -> x1, waiting for transfers between devices: none -> 2.35 us  [summed_over_wide(): lax.all_to_all(jnp.broadcast_to(half[None], (size, *half.shape)), ring, 0...]
    all_gather x1, blocking collectives: 2.34 us -> 3.25 us  [summed_over_wide(): return lax.all_gather(jnp.sum(pieces.astype(F32), axis=0), core, tiled=True)]
where the time goes in v12:
time: 85.2 us; the launch traced here: 84.7 us
  blocking collectives  37.9 us (44%)
  starting transfers between devices  27.3 us (32%)
  Pallas kernels  14 us (16%)
  waiting for transfers between devices  2.36 us (3%)
  local copies, waits for them, and re-layouts  1.47 us (2%)
  between operations  1.43 us (2%)
    all_to_all x2, blocking collectives, swap_from_far(): return lax.all_to_all(pieces, axes, 0, 0, axis_index_groups=order)  26.3 us
    all_to_all x1, starting transfers between devices, swap_from_far(): return lax.all_to_all(pieces, axes, 0, 0, axis_index_groups=order)  14.8 us
    pallas_call x7, Pallas kernels, call(): pl.pallas_call(kernel, out_shape=shapes, compiler_params=pltpu.CompilerPa...  14 us
    all_to_all x1, starting transfers between devices, summed_over_wide(): lax.all_to_all(jnp.broadcast_to(half[None], (size, *half.shape)), ring, 0...  12.5 us
    all_gather x1, blocking collectives, summed_over_wide(): both = lax.all_gather(partial, core)  8.37 us
    all_gather x1, blocking collectives, summed_over_wide(): return lax.all_gather(jnp.sum(pieces.astype(F32), axis=0), core, tiled=True)  3.25 us
    all_to_all x1, waiting for transfers between devices, summed_over_wide(): lax.all_to_all(jnp.broadcast_to(half[None], (size, *half.shape)), ring, 0...  2.35 us
  transfers between devices with their start and end apart: 2, of which 1 were waited for; matrix products, arithmetic and copies ran while one was open for 0% of the time, Pallas kernels for 6%

profile of v12, /device:TPU:1, one launch (start us, length us, event | category | flops | bytes accessed | tf_op | source)
XLA Modules:
  0.0 84.7 jit_solution(15283978225109544112)
XLA Ops:
  0.6 0.0 copy-start.1
  0.7 0.0 copy-start
  0.7 0.8 copy-done.1
  1.5 0.0 copy-done
  1.5 3.6 %shard_map.81 = (f32[32,128]{1,0:T(8,128)S(1)}, s32[16,512]{1,0:T(8,128)S(1)}, s32[512,128]{1,0:T(8,128)S(1)}, s32[8,512]{1,0:T(8,128)S(1)}, f32[32,512]{1,0:T(8,128)S(1)}) custom-call(s32[1]{0:T(128)} %bitcast.9.group, s32[1]{0:T(128)} %bitcast.10.place_of, s32[64,512]{1,0:T(8,128)S(1)} %bitcast.29, bf16[512,512]{1,0:T(8,128)(2,1)} %act.1, ...), custom_call_target="tpu_custom_call" | custom-call | flops 536870912 | bytes 2099208 | tf_op jit(solution)/shard_map/pallas_call | solution.py:290
  5.2 8.4 %all-gather.1 = f32[64,128]{1,0:T(8,128)S(1)} all-gather(f32[32,128]{1,0:T(8,128)S(1)} %get-tuple-element.53), channel_id=3, replica_groups=mesh['wide_0'=16,'wide_1'=2,'narrow_0'=4,'narrow_1'=4] {'wide_1'}, dimensions={0}, use_global_device_ids=true | all-gather | bytes 49152 | tf_op jit(solution)/shard_map/all_gather | solution.py:323
  13.6 0.6 broadcast_in_dim.48
  14.2 12.5 %all-to-all-start.4 = ((bf16[16,16,128]{2,1,0:T(8,128)(2,1)}), bf16[16,16,128]{2,1,0:T(8,128)(2,1)S(1)}, u32[]{:S(2)}, u32[]{:S(2)}) async-start(bf16[16,16,128]{2,1,0:T(8,128)(2,1)} %broadcast_in_dim.48), calls=%async_computation.4 | async-start | bytes 131072 | tf_op jit(solution)/shard_map/all_to_all | solution.py:328
  26.7 3.8 %shard_map.82 = (s32[2,512,128]{2,1,0:T(8,128)S(1)}, s32[2,16,128]{2,1,0:T(8,128)S(1)}, bf16[512,1024]{1,0:T(8,128)(2,1)S(1)}, s32[1]{0:T(128)}) custom-call(s32[1]{0:T(128)} %bitcast.8.owner, s32[16,512]{1,0:T(8,128)S(1)} %get-tuple-element.49.named, s32[8,512]{1,0:T(8,128)S(1)} %get-tuple-element.50.base, bf16[1024,512]{1,0:T(8,128)(2,1)} %weight.5, ...), custom_call_target="tpu_custom_call" | custom-call | flops 67108864 | bytes 2818056 | tf_op jit(solution)/shard_map/pallas_call | solution.py:290
  30.5 2.4 %all-to-all-done.4 = bf16[16,16,128]{2,1,0:T(8,128)(2,1)S(1)} async-done(((bf16[16,16,128]{2,1,0:T(8,128)(2,1)}), bf16[16,16,128]{2,1,0:T(8,128)(2,1)S(1)}, u32[]{:S(2)}, u32[]{:S(2)}) %all-to-all-start.4) | async-done | bytes 65568 | tf_op jit(solution)/shard_map/all_to_all | solution.py:328
  32.9 0.0 copy-start.3
  32.9 3.2 %all_gather.20.packed = f32[32,128]{1,0:T(8,128)S(1)} all-gather(f32[16,128]{1,0:T(8,128)S(1)} %convert_reduce_fusion.1), channel_id=1, replica_groups=mesh['wide_0'=16,'wide_1'=2,'narrow_0'=4,'narrow_1'=4] {'wide_1'}, dimensions={0}, use_global_device_ids=true | all-gather | bytes 24576 | tf_op jit(solution)/shard_map/all_gather | solution.py:331
  36.1 0.0 copy-done.3
  36.1 2.2 %shard_map.83 = (bf16[512,1024]{1,0:T(8,128)(2,1)S(1)}, bf16[512,512]{1,0:T(8,128)(2,1)S(1)}) custom-call(f32[32,128]{1,0:T(8,128)S(1)} %all_gather.20.packed, s32[2,512,128]{2,1,0:T(8,128)S(1)} %get-tuple-element.54.maps, f32[1,1024]{1,0:T(1,128)S(1)} %bitcast.33, bf16[1024,512]{1,0:T(8,128)(2,1)} %weight.5), custom_call_target="tpu_custom_call" | custom-call | flops 536870912 | bytes 3166208 | tf_op jit(solution)/shard_map/pallas_call | solution.py:290
  38.3 14.1 %all_to_all.38.recs = bf16[16,32,512]{2,1,0:T(8,128)(2,1)S(1)} all-to-all(bf16[16,32,512]{2,1,0:T(8,128)(2,1)S(1)} %bitcast.25), channel_id=1, replica_groups={{10,11,8,9,14,15,12,13,2,3,0,1,6,7,4,5},{26,27,24,25,30,31,28,29,18,19,..., dimensions={0} | all-to-all | bytes 1048576 | tf_op jit(solution)/shard_map/all_to_all | solution.py:317
  52.4 0.2 shard_map.84
  52.6 12.2 %all_to_all.39 = bf16[16,32,512]{2,1,0:T(8,128)(2,1)S(1)} all-to-all(bf16[16,32,512]{2,1,0:T(8,128)(2,1)S(1)} %shard_map.84), channel_id=1, replica_groups={{10,11,8,9,14,15,12,13,2,3,0,1,6,7,4,5},{26,27,24,25,30,31,28,29,18,19,..., dimensions={0} | all-to-all | bytes 1048576 | tf_op jit(solution)/shard_map/all_to_all | solution.py:317
  64.8 2.0 %shard_map.85 = f32[32,1,128]{2,1,0:T(1,128)} custom-call(bf16[512,512]{1,0:T(8,128)(2,1)S(1)} %bitcast.21, bf16[512,1024]{1,0:T(8,128)(2,1)S(1)} %get-tuple-element.56.turned_weight, s32[512,128]{1,0:T(8,128)S(1)} %get-tuple-element.57.slots), custom_call_target="tpu_custom_call" | custom-call | flops 536870912 | bytes 1851392 | tf_op jit(solution)/shard_map/pallas_call | solution.py:290
  66.8 14.8 %all-to-all-start.7 = ((f32[32,1,128]{2,1,0:T(1,128)}), f32[32,1,128]{2,1,0:T(1,128)S(1)}, u32[]{:S(2)}, u32[]{:S(2)}) async-start(f32[32,1,128]{2,1,0:T(1,128)} %shard_map.85), calls=%async_computation.7 | async-start | bytes 32768 | tf_op jit(solution)/shard_map/all_to_all | solution.py:317
  82.2 0.0 copy-start.2
  82.2 1.5 %shard_map.86 = bf16[1024,512]{1,0:T(8,128)(2,1)} custom-call(bf16[512,1024]{1,0:T(8,128)(2,1)S(1)} %get-tuple-element.59.latents, bf16[512,512]{1,0:T(8,128)(2,1)S(1)} %bitcast.22), custom_call_target="tpu_custom_call" | custom-call | flops 536870912 | bytes 2621440 | tf_op jit(solution)/shard_map/pallas_call | solution.py:290
  83.7 0.0 all-to-all-done.7
  83.7 0.0 copy-done.2
  83.7 1.0 %conditional.1 = (bf16[1024,512]{1,0:T(8,128)(2,1)}, f32[16,1024]{1,0:T(8,128)}) conditional(s32[]{:T(128)} %bitcast.13, (s32[64,512]{1,0:T(8,128)S(1)}, bf16[512,512]{1,0:T(8,128)(2,1)}, bf16[512,1024]{1,0:T(8,128)(2,1)S(1)}, bf16[1024,512]{1,0:T(8,128)(2,1)}, f32[1024]{0:T(1024)S(1)}, /*index=5*/f32[32,512]{1,0:T(8,128)S(1)}) %tuple.25, ...), branch_computations={%region_1.3_spmd, %region_3.4_spmd} | conditional | flops 2218278912 | bytes 20259704 | solution.py:464
  84.0 0.8 branch_1_fun.1
  (2 shorter events, 0.0 us)
Async XLA Ops:
  0.6 0.9 %copy-start.1 = (s32[512,64]{0,1:T(8,128)S(1)}, s32[512,64]{0,1:T(8,128)}, u32[]{:S(2)}) copy-start(s32[512,64]{0,1:T(8,128)} %param.13) | copy-start | bytes 393220
  0.7 0.8 copy-start
  14.2 18.7 %all-to-all-start.4 = ((bf16[16,16,128]{2,1,0:T(8,128)(2,1)}), bf16[16,16,128]{2,1,0:T(8,128)(2,1)S(1)}, u32[]{:S(2)}, u32[]{:S(2)}) async-start(bf16[16,16,128]{2,1,0:T(8,128)(2,1)} %broadcast_in_dim.48), calls=%async_computation.4 | async-start | bytes 131072 | tf_op jit(solution)/shard_map/all_to_all | solution.py:328
  32.9 3.3 %copy-start.3 = (f32[1024]{0:T(1024)S(1)}, f32[1024]{0:T(1024)}, u32[]{:S(2)}) copy-start(f32[1024]{0:T(1024)} %param.10) | copy-start | bytes 12292
  66.8 16.9 %all-to-all-start.7 = ((f32[32,1,128]{2,1,0:T(1,128)}), f32[32,1,128]{2,1,0:T(1,128)S(1)}, u32[]{:S(2)}, u32[]{:S(2)}) async-start(f32[32,1,128]{2,1,0:T(1,128)} %shard_map.85), calls=%async_computation.7 | async-start | bytes 32768 | tf_op jit(solution)/shard_map/all_to_all | solution.py:317
  82.2 1.5 %copy-start.2 = (bf16[512,1024]{1,0:T(8,128)(2,1)S(1)}, bf16[512,1024]{1,0:T(8,128)(2,1)}, u32[]{:S(2)}) copy-start(bf16[512,1024]{1,0:T(8,128)(2,1)} %weight.3) | copy-start | bytes 3145732

commit v13 on v11

--- a/solution.py
+++ b/solution.py
@@ -113,7 +113,7 @@
     most[0] = jnp.max(needed)
 
 
-def maps_kernel(owner, named, base, weight, out, own, turned_weight):
+def maps_kernel(owner, named, base, weight, out, own, turned_weight, same_weight):
     count, tokens = named.shape
     line = lax.broadcasted_iota(jnp.int32, (LANES, LANES), 0)
     for i in range(tokens // LANES):
@@ -139,13 +139,14 @@
         maps = lax.fori_loop(0, count // 8, body, (zero, zero))
         for m in range(2):
             out[m, cols, :] = maps[m].T
+    same_weight[...] = weight[...]
     own[...] = out[:, pl.ds(pl.multiple_of(owner[0] * CHUNK, CHUNK), CHUNK), :]
     for r in range(0, weight.shape[0], 256):
         turned_weight[:, pl.ds(r, 256)] = weight[pl.ds(r, 256), :].T
 
 
-def window_kernel(width, owner, named, base, weight, ids, out, own, turned_weight, most):
-    maps_kernel(owner, named, base, weight, out, own, turned_weight)
+def window_kernel(width, owner, named, base, weight, ids, out, own, turned_weight, same_weight, most):
+    maps_kernel(owner, named, base, weight, out, own, turned_weight, same_weight)
     count_needed(width, ids, most)
 
 
@@ -200,18 +201,10 @@
     target[...] = bias[...] - act_here[pl.ds(first, mixed), :].astype(F32)
 
 
-def decode_kernel(few, packed, maps, bias, weight, latents, rec, weight_here, arrived):
+def decode_kernel(few, packed, maps, bias, weight, latents, rec):
     step = 8 * CHUNK
     depth = 1 if few else 8
     steps = latents.shape[0] // step
-    part = weight.shape[0] // 4
-    coming = [
-        pltpu.make_async_copy(weight.at[pl.ds(i * part, part)], weight_here.at[pl.ds(i * part, part)], arrived.at[i])
-        for i in range(4)
-    ]
-    for copy in coming:
-        copy.start()
-
     def fill(i):
         rows = pl.ds(i * step, step)
         chunks = [unpack_rows(packed[pl.ds((8 * i + q) * depth, depth), :], few) for q in range(8)]
@@ -222,16 +215,10 @@
         ]
         latents[rows, :] = jnp.concatenate(blocks, axis=1).astype(BF16)
 
-    ahead = 2
-    for i in range(ahead):
-        fill(i)
-    for copy in coming:
-        copy.wait()
     for i in range(steps):
         rows = pl.ds(i * step, step)
-        rec[rows, :] = jnp.dot(latents[rows, :], weight_here[...], preferred_element_type=F32).astype(rec.dtype)
-        if i + ahead < steps:
-            fill(i + ahead)
+        fill(i)
+        rec[rows, :] = jnp.dot(latents[rows, :], weight[...], preferred_element_type=F32).astype(rec.dtype)
 
 
 def mix_kernel(sizes, recs, target, out):
@@ -370,8 +357,9 @@
         array((2, tokens, LANES), jnp.int32),
         array((2, CHUNK, LANES), jnp.int32),
         array((channels, width), BF16),
-    )
-    args, outs, kernel = [lax.axis_index(WIDE)[None], named, base, dec_weight], [pltpu.VMEM] * 3, maps_kernel
+        array((width, channels), BF16),
+    )
+    args, outs, kernel = [lax.axis_index(WIDE)[None], named, base, dec_weight], [pltpu.VMEM] * 4, maps_kernel
     if ids is not None:
         args.append(ids)
         shapes += (array((1,), jnp.int32),)
@@ -392,8 +380,6 @@
         maps,
         enc_bias[None],
         dec_weight,
-        in_specs=specs(pltpu.VMEM, pltpu.VMEM, pltpu.VMEM, pl.ANY),
-        scratch_shapes=[pltpu.VMEM(dec_weight.shape, BF16), pltpu.SemaphoreType.DMA((4,))],
     )
     sizes = sizes_of(NARROW)
     recs = swap_from_far(rec.reshape(-1, *target.shape), NARROW, sizes)
@@ -440,9 +426,9 @@
     ids = active_ids.T
     partial, named, slots, base, target = encode(True, ids, activations, enc_weight, dec_bias)
     preact = summed_over_wide(partial)
-    maps, own, turned_weight, needed = find(named, base, dec_weight, ids)
+    maps, own, turned_weight, same_weight, needed = find(named, base, dec_weight, ids)
     wide = [lax.axis_size(WIDE)]
-    latents, back = decode(True, preact, maps, target, enc_bias, dec_weight)
+    latents, back = decode(True, preact, maps, target, enc_bias, same_weight)
     parts = swap_from_far(latent_parts(True, back, turned_weight, slots), WIDE, wide)
     dec_grad = outer(latents, back)
 
@@ -453,8 +439,8 @@
         no_bias = jnp.zeros_like(dec_bias)
         partial, named, slots, base, _ = encode(False, ids, activations, enc_weight, no_bias)
         preact = summed_over_wide(partial)
-        maps, own, turned_weight = find(named, base, dec_weight)
-        latents, back = decode(False, preact, maps, target, enc_bias, dec_weight)
+        maps, own, turned_weight, same_weight = find(named, base, dec_weight)
+        latents, back = decode(False, preact, maps, target, enc_bias, same_weight)
         parts = swap_from_far(latent_parts(False, back, turned_weight, slots), WIDE, wide)
         return outer(latents, back), own_gradient(False, parts, own, width)
 

time: 83.2 us -> 85 us (1.022)
  local copies, waits for them, and re-layouts: 1.47 us -> 4.34 us
    unnamed x8 -> x12, local copies, waits for them, and re-layouts: 0.83 us -> 3.7 us
  transfers between devices with their start and end apart: 2 -> 2, of which waited for: 1 -> 0; matrix products, arithmetic and copies ran while one was open for 0% -> 0% of each run, Pallas kernels for 6% -> 6%
where the time goes in v13:
time: 85 us; the launch traced here: 84.5 us
  blocking collectives  37.1 us (44%)
  starting transfers between devices  27.7 us (33%)
  Pallas kernels  13.7 us (16%)
  local copies, waits for them, and re-layouts  4.34 us (5%)
  between operations  1.48 us (2%)
    all_to_all x2, starting transfers between devices, swap_from_far(): return lax.all_to_all(pieces, axes, 0, 0, axis_index_groups=order)  27.7 us
    all_to_all x2, blocking collectives, swap_from_far(): return lax.all_to_all(pieces, axes, 0, 0, axis_index_groups=order)  26.3 us
    pallas_call x7, Pallas kernels, call(): pl.pallas_call(kernel, out_shape=shapes, compiler_params=pltpu.CompilerPa...  13.7 us
    all_gather x1, blocking collectives, summed_over_wide(): both = lax.all_gather(partial, core)  8.37 us
    unnamed x12, local copies, waits for them, and re-layouts  3.7 us
    all_gather x1, blocking collectives, summed_over_wide(): return lax.all_gather(jnp.sum(pieces.astype(F32), axis=0), core, tiled=True)  2.39 us
  transfers between devices with their start and end apart: 2, of which 0 were waited for; matrix products, arithmetic and copies ran while one was open for 0% of the time, Pallas kernels for 6%

profile of v13, /device:TPU:1, one launch (start us, length us, event | category | flops | bytes accessed | tf_op | source)
XLA Modules:
  0.0 84.5 jit_solution(15737147107825573908)
XLA Ops:
  0.6 0.0 copy-start.5
  0.7 0.0 copy-start.4
  0.7 0.8 copy-done.5
  1.5 0.0 copy-done.4
  1.5 3.6 %shard_map.81 = (f32[32,128]{1,0:T(8,128)S(1)}, s32[16,512]{1,0:T(8,128)S(1)}, s32[512,128]{1,0:T(8,128)S(1)}, s32[8,512]{1,0:T(8,128)S(1)}, f32[32,512]{1,0:T(8,128)S(1)}) custom-call(s32[1]{0:T(128)} %bitcast.9.group, s32[1]{0:T(128)} %bitcast.10.place_of, s32[64,512]{1,0:T(8,128)S(1)} %bitcast.29, bf16[512,512]{1,0:T(8,128)(2,1)} %act.1, ...), custom_call_target="tpu_custom_call" | custom-call | flops 536870912 | bytes 2099208 | tf_op jit(solution)/shard_map/pallas_call | solution.py:277
  5.2 8.4 %all-gather.1 = f32[64,128]{1,0:T(8,128)S(1)} all-gather(f32[32,128]{1,0:T(8,128)S(1)} %get-tuple-element.55), channel_id=3, replica_groups=mesh['wide_0'=16,'wide_1'=2,'narrow_0'=4,'narrow_1'=4] {'wide_1'}, dimensions={0}, use_global_device_ids=true | all-gather | bytes 49152 | tf_op jit(solution)/shard_map/all_gather | solution.py:310
  13.6 0.6 broadcast_in_dim.48
  14.2 12.9 %all-to-all-start.4 = ((bf16[16,16,128]{2,1,0:T(8,128)(2,1)}), bf16[16,16,128]{2,1,0:T(8,128)(2,1)S(1)}, u32[]{:S(2)}, u32[]{:S(2)}) async-start(bf16[16,16,128]{2,1,0:T(8,128)(2,1)} %broadcast_in_dim.48), calls=%async_computation.4 | async-start | bytes 131072 | tf_op jit(solution)/shard_map/all_to_all | solution.py:304
  27.1 3.8 %shard_map.82 = (s32[2,512,128]{2,1,0:T(8,128)S(1)}, s32[2,16,128]{2,1,0:T(8,128)S(1)}, bf16[512,1024]{1,0:T(8,128)(2,1)S(1)}, bf16[1024,512]{1,0:T(8,128)(2,1)S(1)}, s32[1]{0:T(128)}) custom-call(s32[1]{0:T(128)} %bitcast.8.owner, s32[16,512]{1,0:T(8,128)S(1)} %get-tuple-element.51.named, s32[8,512]{1,0:T(8,128)S(1)} %get-tuple-element.52.base, ...), custom_call_target="tpu_custom_call" | custom-call | flops 67108864 | bytes 3866632 | tf_op jit(solution)/shard_map/pallas_call | solution.py:277
  30.9 0.0 copy-start
  31.0 1.0 %copy-done = bf16[1024,512]{1,0:T(8,128)(2,1)} copy-done((bf16[1024,512]{1,0:T(8,128)(2,1)}, bf16[1024,512]{1,0:T(8,128)(2,1)S(1)}, u32[]{:S(2)}) %copy-start) | copy-done | bytes 1048600
  31.9 0.0 all-to-all-done.4
  31.9 2.4 %all_gather.20.packed = f32[32,128]{1,0:T(8,128)S(1)} all-gather(f32[16,128]{1,0:T(8,128)S(1)} %convert_reduce_fusion.1), channel_id=1, replica_groups=mesh['wide_0'=16,'wide_1'=2,'narrow_0'=4,'narrow_1'=4] {'wide_1'}, dimensions={0}, use_global_device_ids=true | all-gather | bytes 24576 | tf_op jit(solution)/shard_map/all_gather | solution.py:315
  34.3 0.0 copy-start.7
  34.3 0.7 copy-done.7
  35.0 0.0 copy-start.1
  35.0 1.2 %copy-done.1 = bf16[1024,512]{1,0:T(8,128)(2,1)S(1)} copy-done((bf16[1024,512]{1,0:T(8,128)(2,1)S(1)}, bf16[1024,512]{1,0:T(8,128)(2,1)}, u32[]{:S(2)}) %copy-start.1) | copy-done | bytes 1048600
  36.2 1.8 %shard_map.83 = (bf16[512,1024]{1,0:T(8,128)(2,1)S(1)}, bf16[512,512]{1,0:T(8,128)(2,1)S(1)}) custom-call(f32[32,128]{1,0:T(8,128)S(1)} %all_gather.20.packed, s32[2,512,128]{2,1,0:T(8,128)S(1)} %get-tuple-element.56.maps, f32[1,1024]{1,0:T(1,128)S(1)} %bitcast.33, bf16[1024,512]{1,0:T(8,128)(2,1)S(1)} %copy-done.1), custom_call_target="tpu_custom_call" | custom-call | flops 536870912 | bytes 3166208 | tf_op jit(solution)/shard_map/pallas_call | solution.py:277
  38.0 14.1 %all_to_all.38.recs = bf16[16,32,512]{2,1,0:T(8,128)(2,1)S(1)} all-to-all(bf16[16,32,512]{2,1,0:T(8,128)(2,1)S(1)} %bitcast.25), channel_id=1, replica_groups={{10,11,8,9,14,15,12,13,2,3,0,1,6,7,4,5},{26,27,24,25,30,31,28,29,18,19,..., dimensions={0} | all-to-all | bytes 1048576 | tf_op jit(solution)/shard_map/all_to_all | solution.py:304
  52.1 0.2 shard_map.84
  52.3 12.2 %all_to_all.39 = bf16[16,32,512]{2,1,0:T(8,128)(2,1)S(1)} all-to-all(bf16[16,32,512]{2,1,0:T(8,128)(2,1)S(1)} %shard_map.84), channel_id=1, replica_groups={{10,11,8,9,14,15,12,13,2,3,0,1,6,7,4,5},{26,27,24,25,30,31,28,29,18,19,..., dimensions={0} | all-to-all | bytes 1048576 | tf_op jit(solution)/shard_map/all_to_all | solution.py:304
  64.5 2.0 %shard_map.85 = f32[32,1,128]{2,1,0:T(1,128)} custom-call(bf16[512,512]{1,0:T(8,128)(2,1)S(1)} %bitcast.21, bf16[512,1024]{1,0:T(8,128)(2,1)S(1)} %get-tuple-element.59.turned_weight, s32[512,128]{1,0:T(8,128)S(1)} %get-tuple-element.60.slots), custom_call_target="tpu_custom_call" | custom-call | flops 536870912 | bytes 1851392 | tf_op jit(solution)/shard_map/pallas_call | solution.py:277
  66.5 14.8 %all-to-all-start.7 = ((f32[32,1,128]{2,1,0:T(1,128)}), f32[32,1,128]{2,1,0:T(1,128)S(1)}, u32[]{:S(2)}, u32[]{:S(2)}) async-start(f32[32,1,128]{2,1,0:T(1,128)} %shard_map.85), calls=%async_computation.7 | async-start | bytes 32768 | tf_op jit(solution)/shard_map/all_to_all | solution.py:304
  82.0 0.0 copy-start.6
  82.0 1.5 %shard_map.86 = bf16[1024,512]{1,0:T(8,128)(2,1)} custom-call(bf16[512,1024]{1,0:T(8,128)(2,1)S(1)} %get-tuple-element.62.latents, bf16[512,512]{1,0:T(8,128)(2,1)S(1)} %bitcast.22), custom_call_target="tpu_custom_call" | custom-call | flops 536870912 | bytes 2621440 | tf_op jit(solution)/shard_map/pallas_call | solution.py:277
  83.5 0.0 all-to-all-done.7
  83.5 0.0 copy-done.6
  83.5 1.0 %conditional.1 = (bf16[1024,512]{1,0:T(8,128)(2,1)}, f32[16,1024]{1,0:T(8,128)}) conditional(s32[]{:T(128)} %bitcast.13, (s32[64,512]{1,0:T(8,128)S(1)}, bf16[512,512]{1,0:T(8,128)(2,1)}, bf16[512,1024]{1,0:T(8,128)(2,1)S(1)}, bf16[1024,512]{1,0:T(8,128)(2,1)}, f32[1024]{0:T(1024)S(1)}, /*index=5*/f32[32,512]{1,0:T(8,128)S(1)}) %tuple.25, ...), branch_computations={%region_1.3_spmd, %region_3.4_spmd} | conditional | flops 2218278912 | bytes 29696944 | solution.py:447
  83.8 0.8 branch_1_fun.1
  (2 shorter events, 0.0 us)
Async XLA Ops:
  0.6 0.9 %copy-start.5 = (s32[512,64]{0,1:T(8,128)S(1)}, s32[512,64]{0,1:T(8,128)}, u32[]{:S(2)}) copy-start(s32[512,64]{0,1:T(8,128)} %param.13) | copy-start | bytes 393220
  0.7 0.8 copy-start.4
  14.2 17.7 %all-to-all-start.4 = ((bf16[16,16,128]{2,1,0:T(8,128)(2,1)}), bf16[16,16,128]{2,1,0:T(8,128)(2,1)S(1)}, u32[]{:S(2)}, u32[]{:S(2)}) async-start(bf16[16,16,128]{2,1,0:T(8,128)(2,1)} %broadcast_in_dim.48), calls=%async_computation.4 | async-start | bytes 131072 | tf_op jit(solution)/shard_map/all_to_all | solution.py:304
  30.9 1.0 %copy-start = (bf16[1024,512]{1,0:T(8,128)(2,1)}, bf16[1024,512]{1,0:T(8,128)(2,1)S(1)}, u32[]{:S(2)}) copy-start(bf16[1024,512]{1,0:T(8,128)(2,1)S(1)} %get-tuple-element.57.weight) | copy-start | bytes 3145732
  34.3 0.7 copy-start.7
  35.0 1.2 %copy-start.1 = (bf16[1024,512]{1,0:T(8,128)(2,1)S(1)}, bf16[1024,512]{1,0:T(8,128)(2,1)}, u32[]{:S(2)}) copy-start(bf16[1024,512]{1,0:T(8,128)(2,1)} %copy-done) | copy-start | bytes 3145732
  66.5 17.0 %all-to-all-start.7 = ((f32[32,1,128]{2,1,0:T(1,128)}), f32[32,1,128]{2,1,0:T(1,128)S(1)}, u32[]{:S(2)}, u32[]{:S(2)}) async-start(f32[32,1,128]{2,1,0:T(1,128)} %shard_map.85), calls=%async_computation.7 | async-start | bytes 32768 | tf_op jit(solution)/shard_map/all_to_all | solution.py:304
  82.0 1.5 %copy-start.6 = (bf16[512,1024]{1,0:T(8,128)(2,1)S(1)}, bf16[512,1024]{1,0:T(8,128)(2,1)}, u32[]{:S(2)}) copy-start(bf16[512,1024]{1,0:T(8,128)(2,1)} %weight.2) | copy-start | bytes 3145732
